TPU v7x, 32 devices: a whole 2x2x4 slice. The times are simulated.
32 devices in a mesh: rows: 4 (over z), crops: 8 (over y, x, core).
Axes of the slice: x: 2, y: 2, z: 4, core: 2. Of those that a mesh axis runs over, the one named last changes fastest.
Arguments:
- images: bfloat16 [32, 56, 56, 256], P('crops', 'rows'), may hold values from -6 to 6
- reduce_one: bfloat16 [256, 128], replicated, may hold values from -0.375 to 0.375
- spatial_one: bfloat16 [3, 3, 128, 128], replicated, may hold values from -0.1875 to 0.1875
- expand_one: bfloat16 [128, 512], replicated, may hold values from -0.5 to 0.5
- shortcut: bfloat16 [256, 512], replicated, may hold values from -0.375 to 0.375
- reduce_two: bfloat16 [512, 128], replicated, may hold values from -0.25 to 0.25
- spatial_two: bfloat16 [3, 3, 128, 128], replicated, may hold values from -0.1875 to 0.1875
- expand_two: bfloat16 [128, 512], replicated, may hold values from -0.5 to 0.5
- mid_gain: float32 [4, 128], replicated, may hold values from 0.1 to 1.9
- mid_bias: float32 [4, 128], replicated, may hold values from -3 to 3
- wide_gain: float32 [3, 512], replicated, may hold values from 0.1 to 1.9
- wide_bias: float32 [3, 512], replicated, may hold values from -3 to 3
- widths: int32 [32, 2], P('crops'), may hold values from 32 to 128, as said below
- depth_gate: int32 [32], P('crops'), may hold values 0 or 1
- cotangent: bfloat16 [32, 28, 28, 512], P(('crops', 'rows')), may hold values from -6 to 6
Outputs:
- output: bfloat16 [32, 28, 28, 512], P(('crops', 'rows'))
- images_grad: bfloat16 [32, 56, 56, 256], P('crops', 'rows')
- reduce_one_grad: float32 [256, 128], replicated
- spatial_one_grad: float32 [3, 3, 128, 128], replicated
- expand_one_grad: float32 [128, 512], replicated
- shortcut_grad: float32 [256, 512], replicated
- reduce_two_grad: float32 [512, 128], replicated
- spatial_two_grad: float32 [3, 3, 128, 128], replicated
- expand_two_grad: float32 [128, 512], replicated
- mid_gain_grad: float32 [4, 128], replicated
- mid_bias_grad: float32 [4, 128], replicated
- wide_gain_grad: float32 [3, 512], replicated
- wide_bias_grad: float32 [3, 512], replicated
Inputs may be any that keep to these rules, and one draw needn't show every extreme that they name: `widths`: every entry is a multiple of 32.
All inputs are finite; a program needn't handle non-finite values. No bound on the sum of `depth_gate` on one device may be relied on, other than what follows from the above.
Results may differ from a plain program's by a relative error of at most 0.015.
Values may be sent and summed in bfloat16 or wider, within the bound.
A program may use at most 128 MiB of HBM per device.

v0:
```python
import jax
import jax.numpy as jnp
from jax import lax
from jax.sharding import PartitionSpec as P

epsilon = 1e-05
layout_spec = ("NHWC", "HWIO", "NHWC")


def passed_along(block, axis, distance):
    devices = range(lax.axis_size(axis))
    route = [(i - distance, i) for i in devices if i - distance in devices]
    return lax.ppermute(block, axis, route)


def padded_2(block, sides, width):
    for axis, dim in sides:
        count = lax.axis_size(axis)
        forward = [(i, i + 1) for i in range(count - 1)]
        backward = [(target, source) for source, target in forward]
        low = lax.ppermute(
            lax.slice_in_dim(block, block.shape[dim] - width, None, axis=dim), axis, forward
        )
        high = lax.ppermute(lax.slice_in_dim(block, 0, width, axis=dim), axis, backward)
        block = jnp.concatenate([low, block, high], axis=dim)
    return block


def shortened(shard):
    return jax.tree.map(lambda a: a.astype(jnp.bfloat16) if a.dtype == jnp.float32 else a, shard)


def smooth_slope(values):
    sigma = jax.nn.sigmoid(values)
    return sigma * (1.0 + values * (1.0 - sigma))


def dense_map(activation, weight):
    return jnp.einsum("nhwc,cd->nhwd", activation, weight, preferred_element_type=jnp.float32)


def dense_back(upstream, weight):
    return jnp.einsum("nhwd,cd->nhwc", upstream, weight, preferred_element_type=jnp.float32)


def weight_of(activation, upstream):
    return jnp.einsum("nhwc,nhwd->cd", activation, upstream, preferred_element_type=jnp.float32)


def spatial_map(padded, kernel, stride):
    return lax.conv_general_dilated(
        padded,
        kernel,
        (stride, stride),
        "VALID",
        dimension_numbers=layout_spec,
        preferred_element_type=jnp.float32,
    )


def spatial_weight(padded, upstream, stride):
    rows_out = upstream.shape[1]
    cols_out = upstream.shape[2]
    tap_rows = []
    for row_tap in range(3):
        tap_line = []
        for col_tap in range(3):
            window = padded[
                :,
                row_tap : row_tap + stride * (rows_out - 1) + 1 : stride,
                col_tap : col_tap + stride * (cols_out - 1) + 1 : stride,
            ]
            tap_line.append(weight_of(window, upstream))
        tap_rows.append(jnp.stack(tap_line))
    return jnp.stack(tap_rows)


def flipped(kernel):
    return jnp.transpose(kernel[::-1, ::-1], (0, 1, 3, 2))


def local_stats(values, selector):
    masked = selector * values
    count_local = jnp.sum(selector, axis=(0, 1, 2)) * (values.shape[1] * values.shape[2])
    return (jnp.sum(masked, axis=(0, 1, 2)), jnp.sum(masked * values, axis=(0, 1, 2)), count_local)


def norm_finish(values, selector, gain_row, bias_row, total_sum, square_sum, number):
    number = jnp.maximum(number, 1.0)
    center = total_sum / number
    spread = square_sum / number - center * center
    inv_scale = lax.rsqrt(spread + epsilon)
    normed = (values - center) * inv_scale
    return (selector * (gain_row * normed + bias_row), (normed, inv_scale, number))


def norm_forward(values, selector, gain_row, bias_row):
    total_sum, square_sum, number = lax.psum(local_stats(values, selector), ("rows", "crops"))
    return norm_finish(values, selector, gain_row, bias_row, total_sum, square_sum, number)


def local_grads(upstream, selector, stored):
    masked = selector * upstream
    return (jnp.sum(masked, axis=(0, 1, 2)), jnp.sum(masked * stored[0], axis=(0, 1, 2)))


def norm_back_finish(upstream, selector, gain_row, stored, bias_grad, gain_grad):
    normed, inv_scale, number = stored
    values_grad = (
        selector
        * (gain_row * inv_scale)
        * (upstream - bias_grad / number - normed * gain_grad / number)
    )
    return (values_grad, gain_grad, bias_grad)


def norm_backward(upstream, selector, gain_row, stored):
    bias_grad, gain_grad = lax.psum(local_grads(upstream, selector, stored), ("rows", "crops"))
    return norm_back_finish(upstream, selector, gain_row, stored, bias_grad, gain_grad)


def masks_of(width_rows, gate_rows, mid_width):
    channel = jnp.arange(mid_width, dtype=jnp.int32)
    gate_scale = (gate_rows > 0).astype(jnp.float32)[:, None, None, None]
    mask_first = (channel[None, :] < width_rows[:, 0:1]).astype(jnp.float32)[:, None, None, :]
    mask_second = (channel[None, :] < width_rows[:, 1:2]).astype(jnp.float32)[
        :, None, None, :
    ] * gate_scale
    return (mask_first, mask_second, gate_scale)


def on_device(
    images,
    reduce_one,
    spatial_one,
    expand_one,
    shortcut,
    reduce_two,
    spatial_two,
    expand_two,
    mid_gain,
    mid_bias,
    wide_gain,
    wide_bias,
    widths,
    depth_gate,
    cotangent,
):
    float_type = jnp.float32
    low_type = jnp.bfloat16
    mid_width = reduce_one.shape[1]
    wide_width = expand_one.shape[1]
    crops_here = images.shape[0]
    mask_one, mask_two_rows, gate_rows = masks_of(widths, depth_gate, mid_width)
    wide_ones = jnp.ones((crops_here, 1, 1, wide_width), float_type)
    col_pad = ((0, 0), (0, 0), (1, 1), (0, 0))
    reduced_one = dense_map(images, reduce_one)
    normed_one, stored_one = norm_forward(reduced_one, mask_one, mid_gain[0], mid_bias[0])
    act_one = jax.nn.silu(normed_one).astype(low_type)
    upper_row = passed_along(act_one[:, -1:], "rows", 1)
    padded_one = jnp.pad(jnp.concatenate([upper_row, act_one], 1), col_pad)
    spatial_out = spatial_map(padded_one, spatial_one, 2)
    normed_two, stored_two = norm_forward(spatial_out, mask_one, mid_gain[1], mid_bias[1])
    act_two = jax.nn.silu(normed_two).astype(low_type)
    expanded = dense_map(act_two, expand_one)
    skip_input = images[:, ::2, ::2, :]
    skipped = dense_map(skip_input, shortcut)
    normed_three, stored_three = norm_forward(expanded, wide_ones, wide_gain[0], wide_bias[0])
    normed_skip, stored_skip = norm_forward(skipped, wide_ones, wide_gain[1], wide_bias[1])
    pre_one = normed_three + normed_skip
    hidden_rows = jax.nn.silu(pre_one).astype(low_type)
    upstream = lax.all_to_all(cotangent, "rows", split_axis=1, concat_axis=0, tiled=True).astype(
        float_type
    )
    reduced_two = dense_map(hidden_rows, reduce_two)
    normed_four, stored_four = norm_forward(reduced_two, mask_two_rows, mid_gain[2], mid_bias[2])
    act_four = jax.nn.silu(normed_four).astype(low_type)
    framed = padded_2(act_four, (("rows", 1),), 1)
    padded_four = jnp.pad(framed, col_pad)
    spatial_mid = spatial_map(padded_four, spatial_two, 1)
    normed_five, stored_five = norm_forward(spatial_mid, mask_two_rows, mid_gain[3], mid_bias[3])
    act_five = jax.nn.silu(normed_five).astype(low_type)
    expanded_two = dense_map(act_five, expand_two)
    gate_wide = jnp.broadcast_to(gate_rows, (gate_rows.shape[0], 1, 1, wide_width))
    normed_six, stored_six = norm_forward(expanded_two, gate_wide, wide_gain[2], wide_bias[2])
    hidden_float = hidden_rows.astype(float_type)
    pre_two = hidden_float + normed_six
    result = (gate_rows * jax.nn.silu(pre_two) + (1.0 - gate_rows) * hidden_float).astype(low_type)
    result = lax.all_to_all(result, "rows", split_axis=0, concat_axis=1, tiled=True)
    live = gate_rows * upstream * smooth_slope(pre_two)
    grad_six, gain_six, bias_six = norm_backward(live, gate_wide, wide_gain[2], stored_six)
    grad_six = grad_six.astype(low_type)
    expand_two_grad = weight_of(act_five, grad_six)
    back_five = dense_back(grad_six, expand_two) * smooth_slope(normed_five)
    grad_five, gain_five, bias_five = norm_backward(
        back_five, mask_two_rows, mid_gain[3], stored_five
    )
    grad_five = grad_five.astype(low_type)
    spatial_two_grad = spatial_weight(padded_four, grad_five, 1)
    framed_grad = padded_2(grad_five, (("rows", 1),), 1)
    back_four = spatial_map(jnp.pad(framed_grad, col_pad), flipped(spatial_two), 1) * smooth_slope(
        normed_four
    )
    grad_four, gain_four, bias_four = norm_backward(
        back_four, mask_two_rows, mid_gain[2], stored_four
    )
    grad_four = grad_four.astype(low_type)
    reduce_two_grad = weight_of(hidden_rows, grad_four)
    hidden_grad = (dense_back(grad_four, reduce_two) + (1.0 - gate_rows) * upstream + live).astype(
        low_type
    )
    pre_grad = hidden_grad.astype(float_type) * smooth_slope(pre_one)
    grad_three, gain_three, bias_three = norm_backward(
        pre_grad, wide_ones, wide_gain[0], stored_three
    )
    grad_skip, gain_skip, bias_skip = norm_backward(pre_grad, wide_ones, wide_gain[1], stored_skip)
    grad_three = grad_three.astype(low_type)
    grad_skip = grad_skip.astype(low_type)
    expand_one_grad = weight_of(act_two, grad_three)
    shortcut_grad = weight_of(skip_input, grad_skip)
    back_two = dense_back(grad_three, expand_one) * smooth_slope(normed_two)
    grad_two, gain_two, bias_two = norm_backward(back_two, mask_one, mid_gain[1], stored_two)
    grad_two = grad_two.astype(low_type)
    spatial_one_grad = spatial_weight(padded_one, grad_two, 2)
    spread_grad = lax.conv_general_dilated(
        grad_two,
        flipped(spatial_one),
        (1, 1),
        ((2, 2), (2, 3)),
        lhs_dilation=(2, 2),
        dimension_numbers=layout_spec,
        preferred_element_type=float_type,
    )
    from_below = passed_along(shortened(spread_grad[:, 0:1, 1:-1]), "rows", -1)
    inner_grad = spread_grad[:, 1:, 1:-1]
    back_one = jnp.concatenate(
        [inner_grad[:, :-1], inner_grad[:, -1:] + from_below], 1
    ) * smooth_slope(normed_one)
    grad_one, gain_one, bias_one = norm_backward(back_one, mask_one, mid_gain[0], stored_one)
    grad_one = grad_one.astype(low_type)
    reduce_one_grad = weight_of(images, grad_one)
    skip_back = dense_back(grad_skip, shortcut)
    crops_n, rows_half, cols_half, chan_in = skip_back.shape
    placed = jnp.stack([skip_back, jnp.zeros_like(skip_back)], 2).reshape(
        crops_n, 2 * rows_half, cols_half, chan_in
    )
    placed = jnp.stack([placed, jnp.zeros_like(placed)], 3).reshape(
        crops_n, 2 * rows_half, 2 * cols_half, chan_in
    )
    images_grad = (dense_back(grad_one, reduce_one) + placed).astype(low_type)
    summed = lax.psum(
        (
            reduce_one_grad,
            spatial_one_grad,
            expand_one_grad,
            shortcut_grad,
            reduce_two_grad,
            spatial_two_grad,
            expand_two_grad,
        ),
        ("rows", "crops"),
    )
    mid_gain_grad = jnp.stack([gain_one, gain_two, gain_four, gain_five])
    mid_bias_grad = jnp.stack([bias_one, bias_two, bias_four, bias_five])
    wide_gain_grad = jnp.stack([gain_three, gain_skip, gain_six])
    wide_bias_grad = jnp.stack([bias_three, bias_skip, bias_six])
    return (
        result,
        images_grad,
        summed[0],
        summed[1],
        summed[2],
        summed[3],
        summed[4],
        summed[5],
        summed[6],
        mid_gain_grad,
        mid_bias_grad,
        wide_gain_grad,
        wide_bias_grad,
    )


def solution(mesh):
    return jax.shard_map(
        on_device,
        mesh=mesh,
        in_specs=(
            P("crops", "rows", None, None),
            P(),
            P(),
            P(),
            P(),
            P(),
            P(),
            P(),
            P(),
            P(),
            P(),
            P(),
            P("crops", None),
            P("crops"),
            P(("crops", "rows"), None, None, None),
        ),
        out_specs=(
            P(("crops", "rows"), None, None, None),
            P("crops", "rows", None, None),
            P(),
            P(),
            P(),
            P(),
            P(),
            P(),
            P(),
            P(),
            P(),
            P(),
            P(),
        ),
        check_vma=False,
    )
```

profile of v0, /device:TPU:0, one launch (start us, length us, event | category | flops | bytes accessed | tf_op | source)
XLA Modules:
  0.0 868.2 jit_solution(10294848652343104325)
XLA Ops:
  13.5 42.0 %all-reduce.15 = (f32[128]{0:T(128)S(1)}, f32[128]{0:T(128)S(1)}, f32[128]{0:T(128)S(1)}) all-reduce(f32[128]{0:T(128)S(1)} %get-tuple-element.79, f32[128]{0:T(128)S(1)} %get-tuple-element.203, f32[128]{0:T(128)S(1)} %get-tuple-element.78), channel_id=1, replica_groups=mesh['rows'=4,'crops'=8] {'rows','crops'}, use_global_device_ids=true, to_apply=%region_5.0 | all-reduce | flops 384 | bytes 3072 | tf_op jit(solution)/shard_map/psum | solution.py:98
  65.3 12.0 %slice.152 = bf16[4,7,28,256]{3,2,1,0:T(8,128)(2,1)S(1)} slice(bf16[4,14,56,256]{3,2,1,0:T(8,128)(2,1)} %param.15), slice={[0:4:1], [0:14:2], [0:56:2], [0:256:1]} | slice | bytes 802816 | tf_op jit(solution)/shard_map/slice | solution.py:166
  88.7 40.5 %all-reduce.14 = (f32[128]{0:T(128)S(1)}, f32[128]{0:T(128)S(1)}, f32[128]{0:T(128)S(1)}) all-reduce(f32[128]{0:T(128)S(1)} %get-tuple-element.83, f32[128]{0:T(128)S(1)} %copy-done.138, f32[128]{0:T(128)S(1)} %get-tuple-element.82), channel_id=1, replica_groups=mesh['rows'=4,'crops'=8] {'rows','crops'}, use_global_device_ids=true, to_apply=%region_7.8 | all-reduce | flops 384 | bytes 3072 | tf_op jit(solution)/shard_map/psum | solution.py:98
  133.9 41.1 %all-reduce.13 = (f32[512]{0:T(512)S(1)}, f32[512]{0:T(512)S(1)}, f32[512]{0:T(512)S(1)}, f32[512]{0:T(512)S(1)}) all-reduce(f32[512]{0:T(512)S(1)} %copy-done.83, f32[512]{0:T(512)S(1)} %copy-done.82, f32[512]{0:T(512)S(1)} %get-tuple-element.73, f32[512]{0:T(512)S(1)} %get-tuple-element.72), channel_id=1, replica_groups=mesh['rows'=4,'crops'=8] {'rows','crops'}, use_global_device_ids=true, to_apply=%region_18.19 | all-reduce | flops 2048 | bytes 16384 | tf_op jit(solution)/shard_map/psum | solution.py:98
  180.6 39.1 %all-reduce.12 = (f32[128]{0:T(128)S(1)}, f32[128]{0:T(128)S(1)}, f32[128]{0:T(128)S(1)}) all-reduce(f32[128]{0:T(128)S(1)} %get-tuple-element.91, f32[128]{0:T(128)S(1)} %broadcast_multiply_fusion.5, f32[128]{0:T(128)S(1)} %get-tuple-element.90), channel_id=1, replica_groups=mesh['rows'=4,'crops'=8] {'rows','crops'}, use_global_device_ids=true, to_apply=%region_24.25 | all-reduce | flops 384 | bytes 3072 | tf_op jit(solution)/shard_map/psum | solution.py:98
  228.1 8.6 slice.170
  236.7 8.6 slice.169
  245.3 8.6 slice.168
  253.9 8.6 slice.173
  262.5 8.6 slice.172
  271.0 8.6 slice.171
  279.6 8.7 %slice.176 = bf16[4,7,28,128]{3,2,1,0:T(8,128)(2,1)} slice(bf16[4,15,58,128]{3,2,1,0:T(8,128)(2,1)S(1)} %pad.11), slice={[0:4:1], [2:15:2], [2:57:2], [0:128:1]} | slice | bytes 401408 | tf_op jit(solution)/shard_map/slice | solution.py:68
  288.3 8.7 %slice.175 = bf16[4,7,28,128]{3,2,1,0:T(8,128)(2,1)} slice(bf16[4,15,58,128]{3,2,1,0:T(8,128)(2,1)S(1)} %pad.11), slice={[0:4:1], [2:15:2], [1:56:2], [0:128:1]} | slice | bytes 401408 | tf_op jit(solution)/shard_map/slice | solution.py:68
  297.0 8.6 slice.174
  310.9 42.1 %all-reduce.11 = (f32[128]{0:T(128)S(1)}, f32[128]{0:T(128)S(1)}) all-reduce(f32[128]{0:T(128)S(1)} %get-tuple-element.81, f32[128]{0:T(128)S(1)} %get-tuple-element.80), channel_id=1, replica_groups=mesh['rows'=4,'crops'=8] {'rows','crops'}, use_global_device_ids=true, to_apply=%region_26.27 | all-reduce | flops 256 | bytes 2048 | tf_op jit(solution)/shard_map/psum | solution.py:98
  358.1 39.0 %all-reduce.10 = (f32[512]{0:T(512)S(1)}, f32[512]{0:T(512)S(1)}, f32[512]{0:T(512)S(1)}) all-reduce(f32[512]{0:T(512)S(1)} %get-tuple-element.68, f32[512]{0:T(512)S(1)} %copy-done.84, f32[512]{0:T(512)S(1)} %get-tuple-element.67), channel_id=1, replica_groups=mesh['rows'=4,'crops'=8] {'rows','crops'}, use_global_device_ids=true, to_apply=%region_30.31 | all-reduce | flops 1536 | bytes 12288 | tf_op jit(solution)/shard_map/psum | solution.py:98
  407.8 41.0 %all-reduce.9 = (f32[512]{0:T(512)S(1)}, f32[512]{0:T(512)S(1)}) all-reduce(f32[512]{0:T(512)S(1)} %get-tuple-element.66, f32[512]{0:T(512)S(1)} %get-tuple-element.65), channel_id=1, replica_groups=mesh['rows'=4,'crops'=8] {'rows','crops'}, use_global_device_ids=true, to_apply=%region_38.39 | all-reduce | flops 1024 | bytes 8192 | tf_op jit(solution)/shard_map/psum | solution.py:118
  453.6 39.0 %all-reduce.8 = (f32[128]{0:T(128)S(1)}, f32[128]{0:T(128)S(1)}) all-reduce(f32[128]{0:T(128)S(1)} %get-tuple-element.89, f32[128]{0:T(128)S(1)} %get-tuple-element.88), channel_id=1, replica_groups=mesh['rows'=4,'crops'=8] {'rows','crops'}, use_global_device_ids=true, to_apply=%region_42.43 | all-reduce | flops 256 | bytes 2048 | tf_op jit(solution)/shard_map/psum | solution.py:118
  509.0 41.1 %all-reduce.7 = (f32[128]{0:T(128)S(1)}, f32[128]{0:T(128)S(1)}) all-reduce(f32[128]{0:T(128)S(1)} %get-tuple-element.87, f32[128]{0:T(128)S(1)} %get-tuple-element.86), channel_id=1, replica_groups=mesh['rows'=4,'crops'=8] {'rows','crops'}, use_global_device_ids=true, to_apply=%region_46.47 | all-reduce | flops 256 | bytes 2048 | tf_op jit(solution)/shard_map/psum | solution.py:118
  559.2 38.9 %all-reduce.6 = (f32[512]{0:T(512)S(1)}, f32[512]{0:T(512)S(1)}) all-reduce(f32[512]{0:T(512)S(1)} %get-tuple-element.71, f32[512]{0:T(512)S(1)} %get-tuple-element.69), channel_id=1, replica_groups=mesh['rows'=4,'crops'=8] {'rows','crops'}, use_global_device_ids=true, to_apply=%region_48.49 | all-reduce | flops 1024 | bytes 8192 | tf_op jit(solution)/shard_map/psum | solution.py:118
  602.3 41.3 %all-reduce.5 = (f32[128]{0:T(128)S(1)}, f32[128]{0:T(128)S(1)}) all-reduce(f32[128]{0:T(128)S(1)} %get-tuple-element.85, f32[128]{0:T(128)S(1)} %get-tuple-element.84), channel_id=1, replica_groups=mesh['rows'=4,'crops'=8] {'rows','crops'}, use_global_device_ids=true, to_apply=%region_54.55 | all-reduce | flops 256 | bytes 2048 | tf_op jit(solution)/shard_map/psum | solution.py:118
  655.4 40.7 %all-reduce.4 = (f32[512]{0:T(512)S(1)}, f32[128]{0:T(128)S(1)}, f32[128]{0:T(128)}) all-reduce(f32[512]{0:T(512)} %get-tuple-element.70, f32[128]{0:T(128)} %get-tuple-element.77, f32[128]{0:T(128)S(1)} %get-tuple-element.76), channel_id=1, replica_groups=mesh['rows'=4,'crops'=8] {'rows','crops'}, use_global_device_ids=true, to_apply=%region_60.61 | all-reduce | flops 768 | bytes 6144 | tf_op jit(solution)/shard_map/psum | solution.py:118
  725.0 12.4 %all-to-all-done = bf16[4,7,28,512]{3,2,1,0:T(8,128)(2,1)S(1)} async-done(((bf16[4,7,28,512]{3,2,1,0:T(8,128)(2,1)}), bf16[4,7,28,512]{3,2,1,0:T(8,128)(2,1)S(1)}, u32[]{:S(2)}, u32[]{:S(2)}) %all-to-all-start) | async-done | bytes 802848 | tf_op jit(solution)/shard_map/all_to_all | solution.py:189
  737.4 115.3 %all-reduce.19.cloned.1.call-done = (f32[256,128]{0,1:T(8,128)}, f32[3,3,128,128]{3,2,1,0:T(8,128)}, f32[128,512]{1,0:T(8,128)}, f32[256,512]{0,1:T(8,128)}, f32...) async-done(((f32[256,128]{0,1:T(8,128)}, f32[3,3,128,128]{3,2,1,0:T(8,128)}, f32[128,512]{1,0:T(8,128)}, f32[256,512]{0,1:T(8,128)}, ...) | async-done | bytes 2621456 | tf_op jit(solution)/shard_map/psum | solution.py:251
  (451 shorter events, 149.1 us)
Async XLA Ops:
  7.2 79.8 %copy-start = (bf16[3,3,128,128]{3,2,1,0:T(8,128)(2,1)S(1)}, bf16[3,3,128,128]{3,2,1,0:T(8,128)(2,1)}, u32[]{:S(2)}) copy-start(bf16[3,3,128,128]{3,2,1,0:T(8,128)(2,1)} %param.17) | copy-start | bytes 884740
  8.7 68.6 %copy-start.86 = (s32[4]{0:T(128)}, s32[4]{0:T(128)S(1)}, u32[]{:S(2)}) copy-start(s32[4]{0:T(128)S(1)} %get-tuple-element.192) | copy-start | bytes 52
  11.2 46.2 %copy-start.96 = (f32[128]{0:T(128)}, f32[128]{0:T(128)S(1)}, u32[]{:S(2)}) copy-start(f32[128]{0:T(128)S(1)} %get-tuple-element.188) | copy-start | bytes 1540
  11.2 46.2 %copy-start.98 = (f32[128]{0:T(128)}, f32[128]{0:T(128)S(1)}, u32[]{:S(2)}) copy-start(f32[128]{0:T(128)S(1)} %get-tuple-element.220) | copy-start | bytes 1540
  57.4 27.4 %collective-permute-start = (bf16[4,1,56,128]{3,2,1,0:T(8,128)(2,1)S(1)}, bf16[4,1,56,128]{3,2,1,0:T(8,128)(2,1)S(1)}, u32[]{:S(2)}, u32[]{:S(2)}) collective-permute-start(bf16[4,1,56,128]{3,2,1,0:T(8,128)(2,1)S(1)} %slice.200), channel_id=1, source_target_pairs={{0,8},{8,16},{16,24},{1,9},{9,17},{17,25},{2,10},{10,18},{18,26},{... | collective-permute-start | bytes 172040 | tf_op jit(solution)/shard_map/ppermute | solution.py:13
  61.0 341.8 %all-to-all-start.1 = ((bf16[1,28,28,512]{3,2,0,1:T(8,128)(2,1)}), bf16[1,28,28,512]{3,2,0,1:T(8,128)(2,1)}, u32[]{:S(2)}, u32[]{:S(2)}) async-start(bf16[1,28,28,512]{3,2,0,1:T(8,128)(2,1)} %bitcast.394), calls=%async_computation.1 | async-start | bytes 1835008 | tf_op jit(solution)/shard_map/all_to_all | solution.py:172
  65.2 787.4 %all-reduce.19.cloned.1.call-start = ((), (), s32[]{:S(2)}) async-start(), calls=%async_computation.2 | async-start | bytes 5242880 | tf_op jit(solution)/shard_map/psum | solution.py:251
  80.0 95.0 %copy-start.63 = (f32[1,512]{1,0:T(1,128)}, f32[1,512]{1,0:T(1,128)S(1)}, u32[]{:S(2)}) copy-start(f32[1,512]{1,0:T(1,128)S(1)} %get-tuple-element.169) | copy-start | bytes 6148
  131.3 44.9 %copy-start.75 = (f32[1,512]{1,0:T(1,128)S(1)}, f32[1,512]{1,0:T(1,128)}, u32[]{:S(2)}) copy-start(f32[1,512]{1,0:T(1,128)} %get-tuple-element.172) | copy-start | bytes 6148
  180.2 45.8 %copy-start.89 = (s32[4]{0:T(128)S(1)}, s32[4]{0:T(128)}, u32[]{:S(2)}) copy-start(s32[4]{0:T(128)} %copy-done.88) | copy-start | bytes 52
  180.2 45.8 %copy-start.125 = (f32[128]{0:T(128)S(1)}, f32[128]{0:T(128)}, u32[]{:S(2)}) copy-start(f32[128]{0:T(128)} %get-tuple-element.130) | copy-start | bytes 1540
  180.6 47.1 %copy-start.7 = (f32[4,7,28,128]{3,2,1,0:T(8,128)}, f32[4,7,28,128]{3,2,1,0:T(8,128)S(1)}, u32[]{:S(2)}) copy-start(f32[4,7,28,128]{3,2,1,0:T(8,128)S(1)} %get-tuple-element.208) | copy-start | bytes 1204228
  221.0 86.7 %collective-permute-start.1 = (bf16[4,1,28,128]{3,2,1,0:T(8,128)(2,1)S(1)}, bf16[4,1,28,128]{3,2,1,0:T(8,128)(2,1)S(1)}, u32[]{:S(2)}, u32[]{:S(2)}) collective-permute-start(bf16[4,1,28,128]{3,2,1,0:T(8,128)(2,1)S(1)} %get-tuple-element.166), channel_id=1, source_target_pairs={{0,8},{8,16},{16,24},{1,9},{9,17},{17,25},{2,10},{10,18},{18,26},{... | collective-permute-start | bytes 86024 | tf_op jit(solution)/shard_map/ppermute | solution.py:21
  224.4 83.3 %collective-permute-start.2 = (bf16[4,1,28,128]{3,2,1,0:T(8,128)(2,1)S(1)}, bf16[4,1,28,128]{3,2,1,0:T(8,128)(2,1)S(1)}, u32[]{:S(2)}, u32[]{:S(2)}) collective-permute-start(bf16[4,1,28,128]{3,2,1,0:T(8,128)(2,1)S(1)} %get-tuple-element.167), channel_id=1, source_target_pairs={{8,0},{16,8},{24,16},{9,1},{17,9},{25,17},{10,2},{18,10},{26,18},{... | collective-permute-start | bytes 86024 | tf_op jit(solution)/shard_map/ppermute | solution.py:24
  357.0 45.0 %copy-start.87 = (s32[4]{0:T(128)S(1)}, s32[4]{0:T(128)}, u32[]{:S(2)}) copy-start(s32[4]{0:T(128)} %copy-done.86) | copy-start | bytes 52
  357.0 45.0 %copy-start.121 = (f32[128]{0:T(128)S(1)}, f32[128]{0:T(128)}, u32[]{:S(2)}) copy-start(f32[128]{0:T(128)} %get-tuple-element.139) | copy-start | bytes 1540
  357.0 45.7 %copy-start.67 = (f32[1,512]{1,0:T(1,128)S(1)}, f32[1,512]{1,0:T(1,128)}, u32[]{:S(2)}) copy-start(f32[1,512]{1,0:T(1,128)} %get-tuple-element.168) | copy-start | bytes 6148
  357.0 45.8 %copy-start.3 = (bf16[4,7,28,512]{3,2,1,0:T(8,128)(2,1)S(1)}, bf16[4,7,28,512]{3,2,1,0:T(8,128)(2,1)}, u32[]{:S(2)}) copy-start(bf16[4,7,28,512]{3,2,1,0:T(8,128)(2,1)} %copy-done.2) | copy-start | bytes 2408452
  357.0 45.8 %copy-start.81 = (f32[1,512]{1,0:T(1,128)S(1)}, f32[1,512]{1,0:T(1,128)}, u32[]{:S(2)}) copy-start(f32[1,512]{1,0:T(1,128)} %get-tuple-element.171) | copy-start | bytes 6148
  357.0 45.8 %copy-start.132 = (f32[4]{0:T(128)S(1)}, f32[4]{0:T(128)}, u32[]{:S(2)}) copy-start(f32[4]{0:T(128)} %broadcast_subtract_fusion) | copy-start | bytes 52
  496.6 8.5 collective-permute-start.3
  500.2 5.8 collective-permute-start.4
  647.6 6.2 collective-permute-start.5
  702.5 34.8 %all-to-all-start = ((bf16[4,7,28,512]{3,2,1,0:T(8,128)(2,1)}), bf16[4,7,28,512]{3,2,1,0:T(8,128)(2,1)S(1)}, u32[]{:S(2)}, u32[]{:S(2)}) async-start(bf16[4,7,28,512]{3,2,1,0:T(8,128)(2,1)} %get-tuple-element.151), calls=%async_computation | async-start | bytes 1835008 | tf_op jit(solution)/shard_map/all_to_all | solution.py:189
  (126 other events, 1545.3 us)
Sparse Core Ops, SparseCore 0:
  702.6 149.9 all-reduce.18
where the time goes:
time: 878 us; the launch traced here: 868 us
  blocking collectives  486 us (55%)
  local copies, waits for them, and re-layouts  133 us (15%)
  waiting for transfers between devices  130 us (15%)
  other arithmetic  43.4 us (5%)
  matrix products  36.7 us (4%)
  starting transfers between devices  23.4 us (3%)
  between operations  16.3 us (2%)
    psum x6, blocking collectives, norm_forward(): lax.psum(local_stats(values, selector), ('rows', 'crops'))  244 us
    psum x6, blocking collectives, norm_backward(): lax.psum(local_grads(upstream, selector, stored), ('rows', 'crops'))  242 us
    psum x1, waiting for transfers between devices, on_device(): lax.psum((reduce_one_grad, spatial_one_grad, expand_one_grad, shortcut_gr...  115 us
    slice x10, local copies, waits for them, and re-layouts, spatial_weight(): padded[:, row_tap:row_tap + stride * (rows_out - 1) + 1:stride, col_tap:c...  80.5 us
  transfers between devices with their start and end apart: 9, of which 4 were waited for; matrix products, arithmetic and copies ran while one was open for 18% of the time, Pallas kernels for 0%

commit v1 on v0

--- a/solution.py
+++ b/solution.py
@@ -1,10 +1,82 @@
 import jax
 import jax.numpy as jnp
+import functools
 from jax import lax
+from jax.experimental import pallas as pl
+from jax.experimental.pallas import tpu as pltpu
 from jax.sharding import PartitionSpec as P
 
 epsilon = 1e-05
 layout_spec = ("NHWC", "HWIO", "NHWC")
+
+
+MESH = pl.DeviceIdType.MESH
+
+
+def sum_kernel(nr, nc, x_ref, o_ref, buf, send_sem, recv_sem):
+    row = lax.axis_index("rows")
+    col = lax.axis_index("crops")
+    total = nr * nc
+    me = row * nc + col
+
+    def place(i):
+        return (lax.div(i, nc), lax.rem(i, nc))
+
+    barrier = pltpu.get_barrier_semaphore()
+
+    def greet(k, c):
+        pl.semaphore_signal(
+            barrier, inc=1, device_id=place(lax.rem(me + k, total)), device_id_type=MESH
+        )
+        return c
+
+    lax.fori_loop(1, total, greet, 0)
+    buf[me] = x_ref[...]
+    pl.semaphore_wait(barrier, total - 1)
+
+    def send(k, c):
+        pltpu.make_async_remote_copy(
+            src_ref=buf.at[me],
+            dst_ref=buf.at[me],
+            send_sem=send_sem,
+            recv_sem=recv_sem,
+            device_id=place(lax.rem(me + k, total)),
+            device_id_type=MESH,
+        ).start()
+        return c
+
+    lax.fori_loop(1, total, send, 0)
+    others = buf.at[pl.ds(0, total - 1)]
+    pltpu.make_async_copy(others, others, recv_sem).wait()
+    o_ref[...] = lax.fori_loop(1, total, lambda k, v: v + buf[k], buf[0])
+    pltpu.make_async_copy(others, others, send_sem).wait()
+
+
+def summed_small(parts):
+    sizes = [p.size for p in parts]
+    flat = jnp.concatenate([p.reshape(-1) for p in parts])
+    rows = -(-flat.size // 1024) * 8
+    flat = jnp.pad(flat, (0, rows * 128 - flat.size)).reshape(rows, 128)
+    nr, nc = lax.axis_size("rows"), lax.axis_size("crops")
+    out = pl.pallas_call(
+        functools.partial(sum_kernel, nr, nc),
+        out_shape=jax.ShapeDtypeStruct((rows, 128), jnp.float32),
+        in_specs=[pl.BlockSpec(memory_space=pltpu.VMEM)],
+        out_specs=pl.BlockSpec(memory_space=pltpu.VMEM),
+        scratch_shapes=[
+            pltpu.VMEM((nr * nc, rows, 128), jnp.float32),
+            pltpu.SemaphoreType.DMA,
+            pltpu.SemaphoreType.DMA,
+        ],
+        compiler_params=pltpu.CompilerParams(
+            collective_id=rows // 8, has_side_effects=True, vmem_limit_bytes=16 << 20
+        ),
+    )(flat).reshape(-1)
+    result, at = [], 0
+    for p, n in zip(parts, sizes):
+        result.append(out[at : at + n].reshape(p.shape))
+        at += n
+    return tuple(result)
 
 
 def passed_along(block, axis, distance):
@@ -59,20 +131,17 @@
 
 
 def spatial_weight(padded, upstream, stride):
-    rows_out = upstream.shape[1]
-    cols_out = upstream.shape[2]
-    tap_rows = []
-    for row_tap in range(3):
-        tap_line = []
-        for col_tap in range(3):
-            window = padded[
-                :,
-                row_tap : row_tap + stride * (rows_out - 1) + 1 : stride,
-                col_tap : col_tap + stride * (cols_out - 1) + 1 : stride,
-            ]
-            tap_line.append(weight_of(window, upstream))
-        tap_rows.append(jnp.stack(tap_line))
-    return jnp.stack(tap_rows)
+    rows_out, cols_out = upstream.shape[1:3]
+    used = padded[:, : stride * (rows_out - 1) + 3, : stride * (cols_out - 1) + 3]
+    return lax.conv_general_dilated(
+        used,
+        upstream,
+        (1, 1),
+        "VALID",
+        rhs_dilation=(stride, stride),
+        dimension_numbers=("CHWN", "IHWO", "HWNC"),
+        preferred_element_type=jnp.float32,
+    )
 
 
 def flipped(kernel):
@@ -95,7 +164,7 @@
 
 
 def norm_forward(values, selector, gain_row, bias_row):
-    total_sum, square_sum, number = lax.psum(local_stats(values, selector), ("rows", "crops"))
+    total_sum, square_sum, number = summed_small(local_stats(values, selector))
     return norm_finish(values, selector, gain_row, bias_row, total_sum, square_sum, number)
 
 
@@ -115,7 +184,7 @@
 
 
 def norm_backward(upstream, selector, gain_row, stored):
-    bias_grad, gain_grad = lax.psum(local_grads(upstream, selector, stored), ("rows", "crops"))
+    bias_grad, gain_grad = summed_small(local_grads(upstream, selector, stored))
     return norm_back_finish(upstream, selector, gain_row, stored, bias_grad, gain_grad)
 
 

time: 878 us -> 399 us (0.45)
  blocking collectives: 486 us -> 0 us
  Pallas kernels: 0 us -> 133 us
  local copies, waits for them, and re-layouts: 133 us -> 37.2 us
  other arithmetic: 43.4 us -> 24.2 us
    psum x12 -> x0, blocking collectives: 486 us -> none  [the longest x6 244 us: norm_forward(): lax.psum(local_stats(values, selector), ('rows', 'crops'))]
    pallas_call x0 -> x14, Pallas kernels: none -> 133 us  [summed_small(): pl.pallas_call(functools.partial(sum_kernel, nr, nc), out_shape=jax.Shape...]
    slice x10 -> x7, local copies, waits for them, and re-layouts: 80.5 us -> 1.68 us  [summed_small(): result.append(out[at:at + n].reshape(p.shape))]
  transfers between devices with their start and end apart: 9 -> 9, of which waited for: 4 -> 5; matrix products, arithmetic and copies ran while one was open for 18% -> 13% of each run, Pallas kernels for 0% -> 15%
where the time goes in v1:
time: 399 us; the launch traced here: 398 us
  waiting for transfers between devices  135 us (34%)
  Pallas kernels  133 us (33%)
  local copies, waits for them, and re-layouts  37.2 us (9%)
  matrix products  28.7 us (7%)
  other arithmetic  24.2 us (6%)
  starting transfers between devices  23.9 us (6%)
  between operations  15.8 us (4%)
    pallas_call x14, Pallas kernels, summed_small(): pl.pallas_call(functools.partial(sum_kernel, nr, nc), out_shape=jax.Shape...  133 us
    psum x1, waiting for transfers between devices, on_device(): lax.psum((reduce_one_grad, spatial_one_grad, expand_one_grad, shortcut_gr...  116 us
    all_to_all x1, waiting for transfers between devices, on_device(): lax.all_to_all(result, 'rows', split_axis=0, concat_axis=1, tiled=True)  12.8 us
    unnamed x235, local copies, waits for them, and re-layouts  12.8 us
    slice x1, local copies, waits for them, and re-layouts, on_device(): skip_input = images[:, ::2, ::2, :]  12 us
    dot_general x5, matrix products, dense_back(): jnp.einsum('nhwd,cd->nhwc', upstream, weight, preferred_element_type=jnp....  8.99 us
  transfers between devices with their start and end apart: 9, of which 5 were waited for; matrix products, arithmetic and copies ran while one was open for 13% of the time, Pallas kernels for 15%

profile of v1, /device:TPU:0, one launch (start us, length us, event | category | flops | bytes accessed | tf_op | source)
XLA Modules:
  0.0 397.9 jit_solution(7179212345408677776)
XLA Ops:
  11.1 10.3 %shard_map.246 = f32[8,128]{1,0:T(8,128)S(1)} custom-call(f32[8,128]{1,0:T(8,128)S(1)} %fusion.60.x_ref), custom_call_target="tpu_custom_call" | custom-call | tf_op jit(solution)/shard_map/pallas_call | solution.py:61
  23.2 3.5 collective-permute-start
  26.7 4.2 %all-to-all-start.1 = ((bf16[1,28,28,512]{3,2,0,1:T(8,128)(2,1)}), bf16[1,28,28,512]{3,2,0,1:T(8,128)(2,1)}, u32[]{:S(2)}, u32[]{:S(2)}) async-start(bf16[1,28,28,512]{3,2,0,1:T(8,128)(2,1)} %bitcast.327), calls=%async_computation.1 | async-start | bytes 1835008 | tf_op jit(solution)/shard_map/all_to_all | solution.py:241
  31.0 12.0 %slice.293 = bf16[4,7,28,256]{3,2,1,0:T(8,128)(2,1)S(1)} slice(bf16[4,14,56,256]{3,2,1,0:T(8,128)(2,1)} %param.15), slice={[0:4:1], [0:14:2], [0:56:2], [0:256:1]} | slice | bytes 802816 | tf_op jit(solution)/shard_map/slice | solution.py:235
  47.6 11.0 %shard_map.247 = f32[8,128]{1,0:T(8,128)S(1)} custom-call(f32[8,128]{1,0:T(8,128)S(1)} %fusion.59.x_ref), custom_call_target="tpu_custom_call" | custom-call | tf_op jit(solution)/shard_map/pallas_call | solution.py:61
  59.4 8.8 %shard_map.248 = f32[16,128]{1,0:T(8,128)S(1)} custom-call(f32[16,128]{1,0:T(8,128)S(1)} %pad_bitcast_fusion.1.x_ref), custom_call_target="tpu_custom_call" | custom-call | tf_op jit(solution)/shard_map/pallas_call | solution.py:61
  68.2 11.5 %shard_map.249 = f32[16,128]{1,0:T(8,128)S(1)} custom-call(f32[16,128]{1,0:T(8,128)S(1)} %pad_bitcast_fusion.x_ref), custom_call_target="tpu_custom_call" | custom-call | tf_op jit(solution)/shard_map/pallas_call | solution.py:61
  82.7 9.9 %shard_map.250 = f32[8,128]{1,0:T(8,128)S(1)} custom-call(f32[8,128]{1,0:T(8,128)S(1)} %pad_bitcast_fusion.3.x_ref), custom_call_target="tpu_custom_call" | custom-call | tf_op jit(solution)/shard_map/pallas_call | solution.py:61
  94.9 3.6 collective-permute-start.1
  105.1 8.1 %shard_map.251 = f32[8,128]{1,0:T(8,128)S(1)} custom-call(f32[8,128]{1,0:T(8,128)S(1)} %pad_bitcast_fusion.2.x_ref), custom_call_target="tpu_custom_call" | custom-call | tf_op jit(solution)/shard_map/pallas_call | solution.py:61
  115.4 10.4 %shard_map.252 = f32[16,128]{1,0:T(8,128)S(1)} custom-call(f32[16,128]{1,0:T(8,128)S(1)} %fusion.54.x_ref), custom_call_target="tpu_custom_call" | custom-call | tf_op jit(solution)/shard_map/pallas_call | solution.py:61
  128.3 4.5 %multiply_reduce_fusion.7 = (f32[512]{0:T(512)S(1)}, f32[512]{0:T(512)S(1)}, f32[4,7,28,512]{3,2,1,0:T(8,128)S(1)}, bf16[4,7,28,512]{3,2,1,0:T(8,128)(2,1)}) fusion(f32[4]{0:T(128)S(1)} %compare_convert_fusion, f32[512]{0:T(512)} %get-tuple-element.134, f32[4,7,28,512]{3,2,1,0:T(8,128)} %get-tuple-element.196, f32[512]{0:T(512)} %get-tuple-element.135, ...), kind=kLoop, calls=%fused_computation.32 | loop fusion | flops 10435584 | bytes 5632032 | tf_op jit(solution)/shard_map/reduce_sum | solution.py:173
  132.8 9.9 %shard_map.253 = f32[8,128]{1,0:T(8,128)S(1)} custom-call(f32[8,128]{1,0:T(8,128)S(1)} %pad_maximum_fusion.8.x_ref), custom_call_target="tpu_custom_call" | custom-call | tf_op jit(solution)/shard_map/pallas_call | solution.py:61
  145.3 9.1 %shard_map.254 = f32[8,128]{1,0:T(8,128)S(1)} custom-call(f32[8,128]{1,0:T(8,128)S(1)} %fusion.58.x_ref), custom_call_target="tpu_custom_call" | custom-call | tf_op jit(solution)/shard_map/pallas_call | solution.py:61
  165.9 8.6 %shard_map.255 = f32[8,128]{1,0:T(8,128)S(1)} custom-call(f32[8,128]{1,0:T(8,128)S(1)} %fusion.57.x_ref), custom_call_target="tpu_custom_call" | custom-call | tf_op jit(solution)/shard_map/pallas_call | solution.py:61
  178.7 9.1 %shard_map.259 = f32[8,128]{1,0:T(8,128)S(1)} custom-call(f32[8,128]{1,0:T(8,128)S(1)} %get-tuple-element.172.x_ref), custom_call_target="tpu_custom_call" | custom-call | tf_op jit(solution)/shard_map/pallas_call | solution.py:61
  187.8 8.6 %shard_map.256 = f32[8,128]{1,0:T(8,128)S(1)} custom-call(f32[8,128]{1,0:T(8,128)S(1)} %get-tuple-element.171.x_ref), custom_call_target="tpu_custom_call" | custom-call | tf_op jit(solution)/shard_map/pallas_call | solution.py:61
  198.6 8.9 %shard_map.257 = f32[8,128]{1,0:T(8,128)S(1)} custom-call(f32[8,128]{1,0:T(8,128)S(1)} %fusion.56.x_ref), custom_call_target="tpu_custom_call" | custom-call | tf_op jit(solution)/shard_map/pallas_call | solution.py:61
  219.4 8.9 %shard_map.258 = f32[8,128]{1,0:T(8,128)S(1)} custom-call(f32[8,128]{1,0:T(8,128)S(1)} %fusion.55.x_ref), custom_call_target="tpu_custom_call" | custom-call | tf_op jit(solution)/shard_map/pallas_call | solution.py:61
  230.9 4.4 %all-to-all-start = ((bf16[4,7,28,512]{3,2,1,0:T(8,128)(2,1)}), bf16[4,7,28,512]{3,2,1,0:T(8,128)(2,1)S(1)}, u32[]{:S(2)}, u32[]{:S(2)}) async-start(bf16[4,7,28,512]{3,2,1,0:T(8,128)(2,1)} %get-tuple-element.137), calls=%async_computation | async-start | bytes 1835008 | tf_op jit(solution)/shard_map/all_to_all | solution.py:258
  242.1 5.4 %reshape.820 = f32[4,14,56,256]{3,2,1,0:T(8,128)} reshape(f32[4,14,28,2,256]{4,3,2,1,0:T(2,128)} %stack.49.clone) | data formatting | bytes 6422528 | tf_op jit(solution)/shard_map/reshape | solution.py:316
  249.9 3.7 add_convert_fusion
  253.6 12.8 %all-to-all-done = bf16[4,7,28,512]{3,2,1,0:T(8,128)(2,1)S(1)} async-done(((bf16[4,7,28,512]{3,2,1,0:T(8,128)(2,1)}), bf16[4,7,28,512]{3,2,1,0:T(8,128)(2,1)S(1)}, u32[]{:S(2)}, u32[]{:S(2)}) %all-to-all-start) | async-done | bytes 802848 | tf_op jit(solution)/shard_map/all_to_all | solution.py:258
  266.4 116.1 %all-reduce.16.cloned.1.call-done = (f32[256,128]{0,1:T(8,128)}, f32[3,3,128,128]{3,2,1,0:T(8,128)}, f32[128,512]{1,0:T(8,128)}, f32[256,512]{0,1:T(8,128)}, f32...) async-done(((f32[256,128]{0,1:T(8,128)}, f32[3,3,128,128]{3,2,1,0:T(8,128)}, f32[128,512]{1,0:T(8,128)}, f32[256,512]{0,1:T(8,128)}, ...) | async-done | bytes 2621456 | tf_op jit(solution)/shard_map/psum | solution.py:320
  (358 shorter events, 79.0 us)
Async XLA Ops:
  7.2 39.2 %copy-start = (bf16[3,3,128,128]{3,2,1,0:T(8,128)(2,1)S(1)}, bf16[3,3,128,128]{3,2,1,0:T(8,128)(2,1)}, u32[]{:S(2)}) copy-start(bf16[3,3,128,128]{3,2,1,0:T(8,128)(2,1)} %param.17) | copy-start | bytes 884740
  8.7 34.3 %copy-start.70 = (s32[4]{0:T(128)}, s32[4]{0:T(128)S(1)}, u32[]{:S(2)}) copy-start(s32[4]{0:T(128)S(1)} %get-tuple-element.185) | copy-start | bytes 52
  22.6 36.1 %copy-start.76 = (f32[128]{0:T(128)}, f32[128]{0:T(128)S(1)}, u32[]{:S(2)}) copy-start(f32[128]{0:T(128)S(1)} %get-tuple-element.178) | copy-start | bytes 1540
  22.6 36.1 %copy-start.78 = (f32[128]{0:T(128)}, f32[128]{0:T(128)S(1)}, u32[]{:S(2)}) copy-start(f32[128]{0:T(128)S(1)} %get-tuple-element.202) | copy-start | bytes 1540
  23.2 23.1 %collective-permute-start = (bf16[4,1,56,128]{3,2,1,0:T(8,128)(2,1)S(1)}, bf16[4,1,56,128]{3,2,1,0:T(8,128)(2,1)S(1)}, u32[]{:S(2)}, u32[]{:S(2)}) collective-permute-start(bf16[4,1,56,128]{3,2,1,0:T(8,128)(2,1)S(1)} %slice.350), channel_id=1, source_target_pairs={{0,8},{8,16},{16,24},{1,9},{9,17},{17,25},{2,10},{10,18},{18,26},{... | collective-permute-start | bytes 172040 | tf_op jit(solution)/shard_map/ppermute | solution.py:85
  26.7 101.5 %all-to-all-start.1 = ((bf16[1,28,28,512]{3,2,0,1:T(8,128)(2,1)}), bf16[1,28,28,512]{3,2,0,1:T(8,128)(2,1)}, u32[]{:S(2)}, u32[]{:S(2)}) async-start(bf16[1,28,28,512]{3,2,0,1:T(8,128)(2,1)} %bitcast.327), calls=%async_computation.1 | async-start | bytes 1835008 | tf_op jit(solution)/shard_map/all_to_all | solution.py:241
  31.0 351.6 %all-reduce.16.cloned.1.call-start = ((), (), s32[]{:S(2)}) async-start(), calls=%async_computation.2 | async-start | bytes 5242880 | tf_op jit(solution)/shard_map/psum | solution.py:320
  44.3 36.6 %copy-start.37 = (f32[1,512]{1,0:T(1,128)}, f32[1,512]{1,0:T(1,128)S(1)}, u32[]{:S(2)}) copy-start(f32[1,512]{1,0:T(1,128)S(1)} %get-tuple-element.145) | copy-start | bytes 6148
  44.3 36.6 %copy-start.39 = (f32[1,512]{1,0:T(1,128)}, f32[1,512]{1,0:T(1,128)S(1)}, u32[]{:S(2)}) copy-start(f32[1,512]{1,0:T(1,128)S(1)} %get-tuple-element.146) | copy-start | bytes 6148
  44.3 83.3 %copy-start.41 = (f32[1,512]{1,0:T(1,128)}, f32[1,512]{1,0:T(1,128)S(1)}, u32[]{:S(2)}) copy-start(f32[1,512]{1,0:T(1,128)S(1)} %get-tuple-element.144) | copy-start | bytes 6148
  44.9 36.0 %copy-start.62 = (f32[1,512]{1,0:T(1,128)}, f32[1,512]{1,0:T(1,128)S(1)}, u32[]{:S(2)}) copy-start(f32[1,512]{1,0:T(1,128)S(1)} %get-tuple-element.148) | copy-start | bytes 6148
  44.9 36.0 %copy-start.64 = (f32[1,512]{1,0:T(1,128)}, f32[1,512]{1,0:T(1,128)S(1)}, u32[]{:S(2)}) copy-start(f32[1,512]{1,0:T(1,128)S(1)} %get-tuple-element.149) | copy-start | bytes 6148
  46.3 34.7 %copy-start.1 = (f32[4,7,28,512]{3,2,1,0:T(8,128)}, f32[4,7,28,512]{3,2,1,0:T(8,128)S(1)}, u32[]{:S(2)}) copy-start(f32[4,7,28,512]{3,2,1,0:T(8,128)S(1)} %get-tuple-element.194) | copy-start | bytes 4816900
  47.3 33.6 %copy-start.8 = (f32[4,7,28,128]{3,0,2,1:T(4,128)}, f32[4,7,28,128]{3,0,2,1:T(4,128)S(1)}, u32[]{:S(2)}) copy-start(f32[4,7,28,128]{3,0,2,1:T(4,128)S(1)} %get-tuple-element.192) | copy-start | bytes 1204228
  58.6 23.2 %copy-start.45 = (f32[128]{0:T(128)}, f32[128]{0:T(128)S(1)}, u32[]{:S(2)}) copy-start(f32[128]{0:T(128)S(1)} %get-tuple-element.118) | copy-start | bytes 1540
  59.4 22.5 %copy-start.3 = (f32[4,7,28,512]{3,2,1,0:T(8,128)}, f32[4,7,28,512]{3,2,1,0:T(8,128)S(1)}, u32[]{:S(2)}) copy-start(f32[4,7,28,512]{3,2,1,0:T(8,128)S(1)} %get-tuple-element.193) | copy-start | bytes 4816900
  82.6 30.7 %copy-start.80 = (f32[128]{0:T(128)S(1)}, f32[128]{0:T(128)}, u32[]{:S(2)}) copy-start(f32[128]{0:T(128)} %get-tuple-element.180) | copy-start | bytes 1540
  82.6 30.7 %copy-start.82 = (f32[128]{0:T(128)S(1)}, f32[128]{0:T(128)}, u32[]{:S(2)}) copy-start(f32[128]{0:T(128)} %get-tuple-element.204) | copy-start | bytes 1540
  94.9 6.3 %collective-permute-start.1 = (bf16[4,1,28,128]{3,0,2,1:T(4,128)(2,1)S(1)}, bf16[4,1,28,128]{3,0,2,1:T(4,128)(2,1)S(1)}, u32[]{:S(2)}, u32[]{:S(2)}) collective-permute-start(bf16[4,1,28,128]{3,0,2,1:T(4,128)(2,1)S(1)} %get-tuple-element.142), channel_id=1, source_target_pairs={{0,8},{8,16},{16,24},{1,9},{9,17},{17,25},{2,10},{10,18},{18,26},{... | collective-permute-start | bytes 86024 | tf_op jit(solution)/shard_map/ppermute | solution.py:93
  98.5 5.8 %collective-permute-start.2 = (bf16[4,1,28,128]{3,0,2,1:T(4,128)(2,1)S(1)}, bf16[4,1,28,128]{3,0,2,1:T(4,128)(2,1)S(1)}, u32[]{:S(2)}, u32[]{:S(2)}) collective-permute-start(bf16[4,1,28,128]{3,0,2,1:T(4,128)(2,1)S(1)} %get-tuple-element.143), channel_id=1, source_target_pairs={{8,0},{16,8},{24,16},{9,1},{17,9},{25,17},{10,2},{18,10},{26,18},{... | collective-permute-start | bytes 86024 | tf_op jit(solution)/shard_map/ppermute | solution.py:96
  155.2 8.2 %collective-permute-start.3 = (bf16[4,1,28,128]{3,0,2,1:T(4,128)(2,1)S(1)}, bf16[4,1,28,128]{3,0,2,1:T(4,128)(2,1)S(1)}, u32[]{:S(2)}, u32[]{:S(2)}) collective-permute-start(bf16[4,1,28,128]{3,0,2,1:T(4,128)(2,1)S(1)} %get-tuple-element.140), channel_id=1, source_target_pairs={{0,8},{8,16},{16,24},{1,9},{9,17},{17,25},{2,10},{10,18},{18,26},{... | collective-permute-start | bytes 86024 | tf_op jit(solution)/shard_map/ppermute | solution.py:93
  158.7 5.9 %collective-permute-start.4 = (bf16[4,1,28,128]{3,0,2,1:T(4,128)(2,1)S(1)}, bf16[4,1,28,128]{3,0,2,1:T(4,128)(2,1)S(1)}, u32[]{:S(2)}, u32[]{:S(2)}) collective-permute-start(bf16[4,1,28,128]{3,0,2,1:T(4,128)(2,1)S(1)} %get-tuple-element.141), channel_id=1, source_target_pairs={{8,0},{16,8},{24,16},{9,1},{17,9},{25,17},{10,2},{18,10},{26,18},{... | collective-permute-start | bytes 86024 | tf_op jit(solution)/shard_map/ppermute | solution.py:96
  212.2 6.1 %collective-permute-start.5 = (bf16[4,1,56,128]{3,0,2,1:T(4,128)(2,1)S(1)}, bf16[4,1,56,128]{3,0,2,1:T(4,128)(2,1)S(1)}, u32[]{:S(2)}, u32[]{:S(2)}) collective-permute-start(bf16[4,1,56,128]{3,0,2,1:T(4,128)(2,1)S(1)} %slice.469), channel_id=1, source_target_pairs={{8,0},{16,8},{24,16},{9,1},{17,9},{25,17},{10,2},{18,10},{26,18},{... | collective-permute-start | bytes 172040 | tf_op jit(solution)/shard_map/ppermute | solution.py:85
  230.9 35.5 %all-to-all-start = ((bf16[4,7,28,512]{3,2,1,0:T(8,128)(2,1)}), bf16[4,7,28,512]{3,2,1,0:T(8,128)(2,1)S(1)}, u32[]{:S(2)}, u32[]{:S(2)}) async-start(bf16[4,7,28,512]{3,2,1,0:T(8,128)(2,1)} %get-tuple-element.137), calls=%async_computation | async-start | bytes 1835008 | tf_op jit(solution)/shard_map/all_to_all | solution.py:258
  (97 other events, 854.8 us)
Sparse Core Ops, SparseCore 0:
  231.0 151.5 all-reduce.15

commit v2 on v0

v2 whole, which is shorter than its diff:
```python
import functools
from types import SimpleNamespace

import jax
import jax.numpy as jnp
from jax import lax
from jax.experimental import pallas as pl
from jax.experimental.pallas import tpu as pltpu
from jax.sharding import PartitionSpec as P

MESH = pl.DeviceIdType.MESH
F32 = jnp.float32
BF16 = jnp.bfloat16
epsilon = 1e-05
PAD = 32
LANES = 128

ROUND_ROWS = (4, 2, 16, 2, 2, 8, 8, 2, 2, 12, 2, 2)

GROUPS = (
    (("expand_two", 512), ("spatial_two", 1152)),
    (("reduce_two", 512), ("expand_one", 512), ("shortcut", 1024)),
    (("spatial_one", 1152), ("reduce_one", 256)),
)


def group_rows(group, devices):
    unit = 16 * devices
    return -(-sum(rows for _, rows in group) // unit) * unit


def dot(a, b):
    return lax.dot_general(a, b, (((1,), (0,)), ((), ())), preferred_element_type=F32)


def dot_nt(a, b):
    return lax.dot_general(a, b, (((1,), (1,)), ((), ())), preferred_element_type=F32)


def dot_tn(a, b):
    return lax.dot_general(a, b, (((0,), (0,)), ((), ())), preferred_element_type=F32)


def half_silu(h, half_mask=0.5):
    t = jnp.tanh(h)
    p = h * t
    return h + p, (half_mask + half_mask * t) * (1.0 + (h - p))


def folded(x):
    return jnp.sum(x.reshape(-1, 8, x.shape[-1]), axis=0)


def row_sum(x):
    return jnp.sum(x, axis=0, keepdims=True)


def flat2(x):
    return x.reshape(-1, x.shape[-1])


def mega(cfg, *refs):
    r = SimpleNamespace(**dict(zip(cfg.names, refs)))
    nr, nc, nk, hh, wv = cfg.nr, cfg.nc, cfg.nk, cfg.hh, cfg.wv
    ndev, nxy, own = nr * nc, nc // 2, nk // nr
    m_half = hh * PAD
    row = lax.axis_index("rows")
    col = lax.axis_index("crops")
    xy, core = lax.div(col, 2), lax.rem(col, 2)
    me = row * nc + col

    image_copies = [
        pltpu.make_async_copy(r.images.at[k], r.x_in.at[k], r.image_sem.at[k]) for k in range(nk)
    ]
    for copy in image_copies:
        copy.start()

    barrier = pltpu.get_barrier_semaphore()

    def place(i):
        return (lax.div(i, nc), lax.rem(i, nc))

    def greet(k, c):
        pl.semaphore_signal(
            barrier, inc=1, device_id=place(lax.rem(me + k, ndev)), device_id_type=MESH
        )
        return c

    lax.fori_loop(1, ndev, greet, 0)

    lane = lax.broadcasted_iota(jnp.int32, (1, LANES), 1)
    for k in range(nk):
        gate = (jnp.full((1, LANES), r.depth_gate[k], jnp.int32) > 0).astype(F32)
        r.mask_one[k] = (lane < r.widths[k, 0]).astype(F32)
        r.mask_two[k] = (lane < r.widths[k, 1]).astype(F32) * gate
        r.gates[k] = jnp.concatenate([gate] * 4, axis=1)
    col_mask = (lax.broadcasted_iota(jnp.int32, (PAD, 1), 0) < wv).astype(F32)
    half_mask = 0.5 * col_mask

    def tap(ref, i, j):
        return ref[i, j * LANES : (j + 1) * LANES, :].T

    for i in range(3):
        for j in range(3):
            r.back_two[i, j * LANES : (j + 1) * LANES, :] = tap(r.spatial_two, 2 - i, 2 - j)
    zeros = jnp.zeros((LANES, LANES), BF16)
    k1 = r.spatial_one
    here = [[tap(k1, 2, 2), tap(k1, 1, 2), tap(k1, 2, 1), tap(k1, 1, 1)],
            [tap(k1, 2, 0), tap(k1, 1, 0), zeros, zeros]]
    below = [[tap(k1, 0, 2), tap(k1, 0, 1)], [tap(k1, 0, 0), zeros]]
    for ref, blocks in ((r.back_here, here), (r.back_below, below)):
        for i, line in enumerate(blocks):
            for j, block in enumerate(line):
                ref[i * LANES : (i + 1) * LANES, j * LANES : (j + 1) * LANES] = block

    def send_sums(idx, vectors):
        buf, rows = r.sums[idx], ROUND_ROWS[idx]
        at = 0
        for v in vectors:
            for q in range(v.shape[1] // LANES):
                buf[me, at : at + 1, :] = v[:, q * LANES : (q + 1) * LANES]
                at += 1
        assert at == rows

        def send(k, c):
            pltpu.make_async_remote_copy(
                src_ref=buf.at[me],
                dst_ref=buf.at[me],
                send_sem=r.sum_send.at[idx],
                recv_sem=r.sum_recv.at[idx],
                device_id=place(lax.rem(me + k, ndev)),
                device_id_type=MESH,
            ).start()
            return c

        lax.fori_loop(1, ndev, send, 0)

    def take_sums(idx, widths):
        buf = r.sums[idx]
        others = buf.at[pl.ds(0, ndev - 1)]
        pltpu.make_async_copy(others, others, r.sum_recv.at[idx]).wait()
        total = jnp.sum(buf[...], axis=0)
        pltpu.make_async_copy(others, others, r.sum_send.at[idx]).wait()
        result, at = [], 0
        for w in widths:
            parts = [total[at + q : at + q + 1, :] for q in range(w // LANES)]
            at += w // LANES
            result.append(jnp.concatenate(parts, axis=1) if len(parts) > 1 else parts[0])
        return result

    up_ok, down_ok = row > 0, row < nr - 1
    from_above = jnp.where(row > 0, 1.0, 0.0)
    from_below = jnp.where(row < nr - 1, 1.0, 0.0)

    def halo(idx, up, src, dst):
        shift = -1 if up else 1
        return pltpu.make_async_remote_copy(
            src_ref=src,
            dst_ref=dst,
            send_sem=r.halo_send.at[idx],
            recv_sem=r.halo_recv.at[idx],
            device_id=(row + shift, col),
            device_id_type=MESH,
        )

    def halo_start(idx, up, src, dst):
        @pl.when(up_ok if up else down_ok)
        def _():
            halo(idx, up, src, dst).start()

    def halo_wait(idx, up, src, dst):
        @pl.when(up_ok if up else down_ok)
        def _():
            halo(idx, up, src, dst).wait_send()

        @pl.when(down_ok if up else up_ok)
        def _():
            halo(idx, up, src, dst).wait_recv()

    axes = (("core", 2), ("xy", nxy), ("rows", nr))
    seat = {"core": core, "xy": xy, "rows": row}

    def device_of(kind, i):
        if kind == "core":
            return (row, xy * 2 + i)
        if kind == "xy":
            return (row, i * 2 + core)
        return (i, col)

    def level_rows(g, level):
        size = cfg.group_size[g]
        for _, n in axes[:level]:
            size //= n
        return size

    def offset(g, level):
        at = 0
        for i, (kind, _) in enumerate(axes[:level]):
            at = at + seat[kind] * level_rows(g, i + 1)
        return pl.multiple_of(at, 16) if level else 0

    def scatter_send(g, level):
        kind, n = axes[level]
        chunk = level_rows(g, level + 1)
        for k in range(1, n):
            p = lax.rem(seat[kind] + k, n)
            pltpu.make_async_remote_copy(
                src_ref=r.part[g][level].at[pl.ds(pl.multiple_of(p * chunk, 16), chunk)],
                dst_ref=r.came[g][level].at[k - 1],
                send_sem=r.grad_send.at[g, level],
                recv_sem=r.grad_recv.at[g, level],
                device_id=device_of(kind, p),
                device_id_type=MESH,
            ).start()

    def scatter_take(g, level):
        kind, n = axes[level]
        chunk = level_rows(g, level + 1)
        came = r.came[g][level]
        pltpu.make_async_copy(came, came, r.grad_recv.at[g, level]).wait()
        mine = pl.ds(pl.multiple_of(seat[kind] * chunk, 16), chunk)
        total = r.part[g][level][mine, :].astype(F32) + jnp.sum(came[...].astype(F32), axis=0)
        pltpu.make_async_copy(came, came, r.grad_send.at[g, level]).wait()
        if level + 1 < len(axes):
            r.part[g][level + 1][...] = total.astype(BF16)
        else:
            r.full[g][pl.ds(offset(g, 3), chunk), :] = total.astype(BF16)

    def gather_send(g, level):
        kind, n = axes[level]
        size = level_rows(g, level + 1)
        region = r.full[g].at[pl.ds(offset(g, level + 1), size)]
        for k in range(1, n):
            p = lax.rem(seat[kind] + k, n)
            pltpu.make_async_remote_copy(
                src_ref=region,
                dst_ref=region,
                send_sem=r.grad_send.at[g, 3 + level],
                recv_sem=r.grad_recv.at[g, 3 + level],
                device_id=device_of(kind, p),
                device_id_type=MESH,
            ).start()

    def gather_take(g, level):
        n = axes[level][1]
        size = level_rows(g, level + 1) * (n - 1)
        bytes_of = r.full[g].at[pl.ds(0, size)]
        pltpu.make_async_copy(bytes_of, bytes_of, r.grad_recv.at[g, 3 + level]).wait()
        pltpu.make_async_copy(bytes_of, bytes_of, r.grad_send.at[g, 3 + level]).wait()

    steps = (
        (scatter_send, 0), (scatter_take, 0), (scatter_send, 1), (scatter_take, 1),
        (scatter_send, 2), (scatter_take, 2), (gather_send, 2), (gather_take, 2),
        (gather_send, 1), (gather_take, 1), (gather_send, 0), (gather_take, 0),
    )

    def advance(g, phase):
        for fn, level in steps[max(0, 2 * phase - 1) : 2 * phase + 1]:
            fn(g, level)

    def stage(g, name, value):
        at = 0
        for other, rows in GROUPS[g]:
            if other == name:
                break
            at += rows
        blocks = value.shape[1] // LANES
        for q in range(blocks):
            n = value.shape[0]
            lo = at + q * n
            r.part[g][0][lo : lo + n, :] = value[:, q * LANES : (q + 1) * LANES].astype(BF16)

    def unstage(g, name, ref):
        at = 0
        for other, rows in GROUPS[g]:
            if other == name:
                break
            at += rows
        n = ref.shape[0]
        for q in range(ref.shape[1] // LANES):
            lo = at + q * n
            ref[:, q * LANES : (q + 1) * LANES] = r.full[g][lo : lo + n, :].astype(F32)

    def coefficients(total, square, count, gain, bias):
        n = jnp.maximum(count, 1.0)
        mu = total / n
        inv = lax.rsqrt(square / n - mu * mu + epsilon)
        scale = gain * inv
        return SimpleNamespace(n=n, mu=mu, inv=inv, scale=scale, shift=bias - mu * scale)

    def backward(norm, dbias, dz_sum):
        dgain = norm.inv * (dz_sum - norm.mu * dbias)
        c2 = -norm.scale * norm.inv * dgain / norm.n
        c3 = -norm.scale * dbias / norm.n - c2 * norm.mu
        return dgain, (norm.scale, c2, c3)

    def loop(body, init=0):
        return lax.fori_loop(0, nk, body, init)

    def zero8(width, count):
        return tuple(jnp.zeros((8, width), F32) for _ in range(count))

    lane_blocks = cfg.c_in // LANES
    for slot in range(2 * hh):
        for q in range(lane_blocks):
            r.spread[q, slot, 2 * wv : 2 * PAD, :] = jnp.zeros((2 * PAD - 2 * wv, LANES), F32)
    w1 = r.reduce_one[...]
    acc = zero8(LANES, 2)
    for copy in image_copies:
        copy.wait()

    def first(k, acc):
        for i in range(2 * hh):
            for q in range(lane_blocks):
                lanes = slice(q * LANES, (q + 1) * LANES)
                r.spread[q, i, 0 : 2 * wv, :] = r.x_in[k, i, :, lanes].astype(F32)
        m = r.mask_one[k]
        s1, s2 = acc
        for pr in range(2):
            for pc in range(2):
                for i in range(hh):
                    for q in range(lane_blocks):
                        lanes = slice(q * LANES, (q + 1) * LANES)
                        r.x[pr, pc, k, i, :, lanes] = r.spread[
                            q, 2 * i + pr, pl.ds(pc, PAD, stride=2), :
                        ].astype(BF16)
                z = dot(flat2(r.x[pr, pc, k]), w1)
                r.z1[pr, pc, k] = z.reshape(hh, PAD, LANES)
                s1 += m * folded(z)
                s2 += m * folded(z * z)
        return s1, s2

    s1, s2 = loop(first, acc)
    count_one = sum(r.mask_one[k] for k in range(nk))
    count_two = sum(r.mask_two[k] for k in range(nk))
    pl.semaphore_wait(barrier, ndev - 1)
    send_sums(0, [row_sum(s1), row_sum(s2), count_one, count_two])
    halo_z1 = (0, False, r.z1.at[1, :, :, hh - 1], r.h1)
    halo_start(*halo_z1)

    def cot_copy(k, p):
        return pltpu.make_async_remote_copy(
            src_ref=r.cot.at[:, pl.ds(p * hh, hh)],
            dst_ref=r.cot_rows.at[pl.ds(row * own, own)],
            send_sem=r.cot_send.at[k],
            recv_sem=r.cot_recv.at[k],
            device_id=(p, col),
            device_id_type=MESH,
        )

    cot_copies = [cot_copy(k, lax.rem(row + k, nr)) for k in range(1, nr)]
    cot_local = pltpu.make_async_copy(
        r.cot.at[:, pl.ds(row * hh, hh)], r.cot_rows.at[pl.ds(row * own, own)], r.local_sem.at[0]
    )
    for copy in cot_copies:
        copy.start()
    cot_local.start()

    sc = r.shortcut[...]

    def skip(k, acc):
        z = dot(flat2(r.x[0, 0, k]), sc)
        r.zs[k] = z.reshape(hh, PAD, cfg.c_out)
        return acc[0] + folded(z), acc[1] + folded(z * z)

    zs1, zs2 = loop(skip, zero8(cfg.c_out, 2))

    t1, t2, active_one, active_two = take_sums(0, [LANES] * 4)
    half_px, full_px = float(hh * wv), float(4 * hh * wv)
    active_gate = active_two[:, 0:1]
    g1, b1 = r.mid_gain[0:1, :], r.mid_bias[0:1, :]
    n1 = coefficients(t1, t2, active_one * full_px, g1, b1)
    halo_wait(*halo_z1)

    def shifted_right(a):
        return pltpu.roll(a, 1, axis=a.ndim - 2)

    def shifted_left(a):
        return pltpu.roll(a, PAD - 1, axis=a.ndim - 2)

    def affine(norm, m):
        return 0.5 * m * norm.scale, (0.5 * m * norm.shift) * col_mask

    k_one = [r.spatial_one[i] for i in range(3)]

    def second(k, acc):
        m = r.mask_one[k]
        ah, bh = affine(n1, m)
        for pr in range(2):
            for pc in range(2):
                a, s = half_silu(r.z1[pr, pc, k] * ah + bh, half_mask)
                r.s1[pr, pc, k] = s
                dst = r.even if pr == 0 else r.odd
                rows = pl.ds(0, hh) if pr == 0 else pl.ds(1, hh)
                if pc == 0:
                    dst[k, rows, :, LANES : 2 * LANES] = a.astype(BF16)
                else:
                    dst[k, rows, :, 2 * LANES : 3 * LANES] = a.astype(BF16)
                    dst[k, rows, :, 0:LANES] = shifted_right(a).astype(BF16)
        for pc in range(2):
            a, _ = half_silu(r.h1[pc, k] * ah + bh)
            a = jnp.where(row > 0, a, 0.0)
            if pc == 0:
                r.odd[k, 0, :, LANES : 2 * LANES] = a.astype(BF16)
            else:
                r.odd[k, 0, :, 2 * LANES : 3 * LANES] = a.astype(BF16)
                r.odd[k, 0, :, 0:LANES] = shifted_right(a).astype(BF16)
        z = dot(flat2(r.even[k]), k_one[1])
        z += dot(flat2(r.odd[k, 1 : hh + 1]), k_one[2])
        z += dot(flat2(r.odd[k, 0:hh]), k_one[0])
        z = z.reshape(hh, PAD, LANES) * col_mask
        r.z2[k] = z
        return acc[0] + m * folded(z), acc[1] + m * folded(z * z)

    s1, s2 = loop(second, zero8(LANES, 2))
    send_sums(1, [row_sum(s1), row_sum(s2)])
    halo_z2 = (1, True, r.z2.at[:, 0], r.h2)
    halo_start(*halo_z2)
    t1, t2 = take_sums(1, [LANES] * 2)
    n2 = coefficients(t1, t2, active_one * half_px, r.mid_gain[1:2, :], r.mid_bias[1:2, :])
    e1 = r.expand_one[...]

    def third(k, acc):
        ah, bh = affine(n2, r.mask_one[k])
        a, s = half_silu(r.z2[k] * ah + bh, half_mask)
        r.s2[k] = s
        a = a.astype(BF16)
        r.a2[k] = a
        z = dot(flat2(a), e1)
        r.z3[k] = z.reshape(hh, PAD, cfg.c_out)
        return acc[0] + folded(z), acc[1] + folded(z * z)

    s1, s2 = loop(third, zero8(cfg.c_out, 2))
    send_sums(2, [row_sum(s1), row_sum(s2), row_sum(zs1), row_sum(zs2)])
    t1, t2, ts1, ts2 = take_sums(2, [cfg.c_out] * 4)
    all_px = float(nk * nc) * float(nr) * half_px
    n3 = coefficients(t1, t2, all_px, r.wide_gain[0:1, :], r.wide_bias[0:1, :])
    ns = coefficients(ts1, ts2, all_px, r.wide_gain[1:2, :], r.wide_bias[1:2, :])
    w2 = r.reduce_two[...]

    def fourth(k, acc):
        a3, as_ = 0.5 * n3.scale, 0.5 * ns.scale
        b3 = (0.5 * (n3.shift + ns.shift)) * col_mask
        for i in range(hh):
            a, s = half_silu(r.z3[k, i] * a3 + r.zs[k, i] * as_ + b3, half_mask)
            r.hidden[k, i] = a.astype(BF16)
            r.s3[k, i] = s
        z = dot(flat2(r.hidden[k]), w2)
        r.z4[k] = z.reshape(hh, PAD, LANES)
        m = r.mask_two[k]
        return acc[0] + m * folded(z), acc[1] + m * folded(z * z)

    s1, s2 = loop(fourth, zero8(LANES, 2))
    send_sums(3, [row_sum(s1), row_sum(s2)])
    halos_z4 = [
        (2, False, r.z4.at[:, hh - 1], r.h4.at[0]),
        (3, True, r.z4.at[:, 0], r.h4.at[1]),
    ]
    for h in halos_z4:
        halo_start(*h)
    t1, t2 = take_sums(3, [LANES] * 2)
    n4 = coefficients(t1, t2, active_two * half_px, r.mid_gain[2:3, :], r.mid_bias[2:3, :])
    for h in halos_z4:
        halo_wait(*h)

    def put3(dst, k, rows, a):
        dst[k, rows, :, LANES : 2 * LANES] = a.astype(BF16)
        dst[k, rows, :, 0:LANES] = shifted_right(a).astype(BF16)
        dst[k, rows, :, 2 * LANES : 3 * LANES] = shifted_left(a).astype(BF16)

    k_two = [r.spatial_two[i] for i in range(3)]

    def fifth(k, acc):
        m = r.mask_two[k]
        ah, bh = affine(n4, m)
        a, s = half_silu(r.z4[k] * ah + bh, half_mask)
        r.s4[k] = s
        put3(r.a4, k, pl.ds(1, hh), a)
        a, _ = half_silu(r.h4[0, k] * ah + bh)
        put3(r.a4, k, 0, jnp.where(row > 0, a, 0.0))
        a, _ = half_silu(r.h4[1, k] * ah + bh)
        put3(r.a4, k, hh + 1, jnp.where(row < nr - 1, a, 0.0))
        z = sum(dot(flat2(r.a4[k, i : i + hh]), k_two[i]) for i in range(3))
        z = z.reshape(hh, PAD, LANES) * col_mask
        r.z5[k] = z
        return acc[0] + m * folded(z), acc[1] + m * folded(z * z)

    s1, s2 = loop(fifth, zero8(LANES, 2))
    send_sums(4, [row_sum(s1), row_sum(s2)])
    halos_z5 = [
        (4, False, r.z5.at[:, hh - 1], r.h5.at[0]),
        (5, True, r.z5.at[:, 0], r.h5.at[1]),
    ]
    for h in halos_z5:
        halo_start(*h)
    t1, t2 = take_sums(4, [LANES] * 2)
    n5 = coefficients(t1, t2, active_two * half_px, r.mid_gain[3:4, :], r.mid_bias[3:4, :])
    e2 = r.expand_two[...]

    def sixth(k, acc):
        ah, bh = affine(n5, r.mask_two[k])
        a, s = half_silu(r.z5[k] * ah + bh, half_mask)
        r.s5[k] = s
        a = a.astype(BF16)
        r.a5[k] = a
        z = dot(flat2(a), e2)
        r.z6[k] = z.reshape(hh, PAD, cfg.c_out)
        g = r.gates[k]
        return acc[0] + g * folded(z), acc[1] + g * folded(z * z)

    s1, s2 = loop(sixth, zero8(cfg.c_out, 2))
    send_sums(5, [row_sum(s1), row_sum(s2)])
    for copy in cot_copies:
        copy.wait()
    cot_local.wait()
    t1, t2 = take_sums(5, [cfg.c_out] * 2)
    gate_count = active_gate * half_px
    n6 = coefficients(t1, t2, gate_count, r.wide_gain[2:3, :], r.wide_bias[2:3, :])
    pad_rows = jnp.zeros((PAD - wv, cfg.c_out), F32)

    def cot_row(k, i):
        return jnp.concatenate([r.cot_rows[k, i].astype(F32), pad_rows], axis=0)

    def seventh(k, acc):
        g = r.gates[k]
        a6, b6 = (0.5 * g) * n6.scale, ((0.5 * g) * n6.shift) * col_mask
        d1, d2 = acc
        for i in range(hh):
            hid = r.hidden[k, i].astype(F32)
            z = r.z6[k, i]
            a, s = half_silu(0.5 * hid + (z * a6 + b6))
            r.out_rows[k, i] = jnp.where(g > 0.0, a, hid).astype(BF16)
            live = g * cot_row(k, i) * s
            r.live[k, i] = live
            d1 += folded(live)
            d2 += folded(live * z)
        return d1, d2

    d1, d2 = loop(seventh, zero8(cfg.c_out, 2))
    send_sums(6, [row_sum(d1), row_sum(d2)])

    def out_copy(k, p):
        return pltpu.make_async_remote_copy(
            src_ref=r.out_rows.at[pl.ds(p * own, own)],
            dst_ref=r.out.at[:, pl.ds(row * hh, hh)],
            send_sem=r.out_send.at[k],
            recv_sem=r.out_recv.at[k],
            device_id=(p, col),
            device_id_type=MESH,
        )

    out_copies = [out_copy(k, lax.rem(row + k, nr)) for k in range(1, nr)]
    out_local = pltpu.make_async_copy(
        r.out_rows.at[pl.ds(row * own, own)], r.out.at[:, pl.ds(row * hh, hh)], r.local_sem.at[1]
    )
    for copy in out_copies:
        copy.start()
    out_local.start()
    db6, q6 = take_sums(6, [cfg.c_out] * 2)
    dg6, (c1, c2, c3) = backward(n6, db6, q6)

    def eighth(k, acc, c1=c1, c2=c2, c3=c3):
        g = r.gates[k]
        f1, f2, f3 = g * c1, g * c2, (g * c3) * col_mask
        for i in range(hh):
            r.dz6[k, i] = (r.live[k, i] * f1 + r.z6[k, i] * f2 + f3).astype(BF16)
        q = dot_nt(flat2(r.dz6[k]), e2).reshape(hh, PAD, LANES) * r.s5[k]
        r.q5[k] = q
        m = r.mask_two[k]
        return acc[0] + m * folded(q), acc[1] + m * folded(q * r.z5[k])

    d1, d2 = loop(eighth, zero8(LANES, 2))
    send_sums(7, [row_sum(d1), row_sum(d2)])
    halos_q5 = [
        (6, False, r.q5.at[:, hh - 1], r.hq5.at[0]),
        (7, True, r.q5.at[:, 0], r.hq5.at[1]),
    ]
    for h in halos_q5:
        halo_start(*h)
    stage(0, "expand_two", dot_tn(flat2(r.a5[...]), flat2(r.dz6[...])))
    for h in halos_z5:
        halo_wait(*h)
    db5, q5 = take_sums(7, [LANES] * 2)
    dg5, (c1, c2, c3) = backward(n5, db5, q5)
    for h in halos_q5:
        halo_wait(*h)

    def ninth(k, acc, c1=c1, c2=c2, c3=c3):
        m = r.mask_two[k]
        f1, f2, f3 = m * c1, m * c2, (m * c3) * col_mask
        put3(r.dz5, k, pl.ds(1, hh), r.q5[k] * f1 + r.z5[k] * f2 + f3)
        d = r.hq5[0, k] * f1 + r.h5[0, k] * f2 + f3
        put3(r.dz5, k, 0, jnp.where(row > 0, d, 0.0))
        d = r.hq5[1, k] * f1 + r.h5[1, k] * f2 + f3
        put3(r.dz5, k, hh + 1, jnp.where(row < nr - 1, d, 0.0))
        q = sum(dot(flat2(r.dz5[k, i : i + hh]), r.back_two[i]) for i in range(3))
        q = q.reshape(hh, PAD, LANES) * r.s4[k]
        r.q4[k] = q
        return acc[0] + m * folded(q), acc[1] + m * folded(q * r.z4[k])

    d1, d2 = loop(ninth, zero8(LANES, 2))
    send_sums(8, [row_sum(d1), row_sum(d2)])
    d5 = flat2(r.dz5[:, 1 : hh + 1, :, LANES : 2 * LANES])
    stage(
        0,
        "spatial_two",
        jnp.concatenate([dot_tn(flat2(r.a4[:, i : i + hh]), d5) for i in range(3)], axis=0),
    )
    advance(0, 0)
    db4, q4 = take_sums(8, [LANES] * 2)
    dg4, (c1, c2, c3) = backward(n4, db4, q4)

    def tenth(k, acc, c1=c1, c2=c2, c3=c3):
        m, g = r.mask_two[k], r.gates[k]
        f1, f2, f3 = m * c1, m * c2, (m * c3) * col_mask
        r.dz4[k] = (r.q4[k] * f1 + r.z4[k] * f2 + f3).astype(BF16)
        back = dot_nt(flat2(r.dz4[k]), w2).reshape(hh, PAD, cfg.c_out)
        e1_, e2_, e3_ = acc
        for i in range(hh):
            d = back[i] + (1.0 - g) * cot_row(k, i) + r.live[k, i]
            q = d.astype(BF16).astype(F32) * r.s3[k, i]
            r.q3[k, i] = q
            e1_ += folded(q)
            e2_ += folded(q * r.z3[k, i])
            e3_ += folded(q * r.zs[k, i])
        return e1_, e2_, e3_

    d1, d2, d3 = loop(tenth, zero8(cfg.c_out, 3))
    send_sums(9, [row_sum(d1), row_sum(d2), row_sum(d3)])
    stage(1, "reduce_two", dot_tn(flat2(r.hidden[...]), flat2(r.dz4[...])))
    advance(0, 1)
    db3, q3, qs = take_sums(9, [cfg.c_out] * 3)
    dg3, (c1, c2, c3) = backward(n3, db3, q3)
    dgs, (p1, p2, p3) = backward(ns, db3, qs)

    def eleventh(k, acc, c1=c1, c2=c2, c3=c3):
        f3, h3 = c3 * col_mask, p3 * col_mask
        for i in range(hh):
            q = r.q3[k, i]
            r.dz3[k, i] = (q * c1 + r.z3[k, i] * c2 + f3).astype(BF16)
            r.dzs[k, i] = (q * p1 + r.zs[k, i] * p2 + h3).astype(BF16)
        q = dot_nt(flat2(r.dz3[k]), e1).reshape(hh, PAD, LANES) * r.s2[k]
        r.q2[k] = q
        m = r.mask_one[k]
        return acc[0] + m * folded(q), acc[1] + m * folded(q * r.z2[k])

    d1, d2 = loop(eleventh, zero8(LANES, 2))
    send_sums(10, [row_sum(d1), row_sum(d2)])
    halo_q2 = (8, True, r.q2.at[:, 0], r.hq2)
    halo_start(*halo_q2)
    stage(1, "expand_one", dot_tn(flat2(r.a2[...]), flat2(r.dz3[...])))
    stage(1, "shortcut", dot_tn(flat2(r.x[0, 0]), flat2(r.dzs[...])))
    advance(1, 0)
    advance(0, 2)
    halo_wait(*halo_z2)
    db2, q2 = take_sums(10, [LANES] * 2)
    dg2, (c1, c2, c3) = backward(n2, db2, q2)
    halo_wait(*halo_q2)

    def twelfth(k, acc, c1=c1, c2=c2, c3=c3):
        m = r.mask_one[k]
        f1, f2, f3 = m * c1, m * c2, (m * c3) * col_mask
        d = r.q2[k] * f1 + r.z2[k] * f2 + f3
        r.dz2[k, 0:hh, :, 0:LANES] = d.astype(BF16)
        r.dz2[k, 0:hh, :, LANES : 2 * LANES] = shifted_left(d).astype(BF16)
        d = jnp.where(row < nr - 1, r.hq2[k] * f1 + r.h2[k] * f2 + f3, 0.0)
        r.dz2[k, hh, :, 0:LANES] = d.astype(BF16)
        r.dz2[k, hh, :, LANES : 2 * LANES] = shifted_left(d).astype(BF16)
        u = dot(flat2(r.dz2[k, 0:hh]), r.back_here[...])
        v = dot(flat2(r.dz2[k, 1 : hh + 1]), r.back_below[...])
        s1, s2 = acc
        planes = (
            (1, 1, u[:, 0:LANES] + v[:, 0:LANES]),
            (0, 1, u[:, LANES : 2 * LANES]),
            (1, 0, u[:, 2 * LANES : 3 * LANES] + v[:, LANES : 2 * LANES]),
            (0, 0, u[:, 3 * LANES : 4 * LANES]),
        )
        for pr, pc, q in planes:
            q = q.reshape(hh, PAD, LANES) * r.s1[pr, pc, k]
            r.q1[pr, pc, k] = q
            s1 += m * folded(q)
            s2 += m * folded(q * r.z1[pr, pc, k])
        return s1, s2

    d1, d2 = loop(twelfth, zero8(LANES, 2))
    send_sums(11, [row_sum(d1), row_sum(d2)])
    d2_ = flat2(r.dz2[:, 0:hh, :, 0:LANES])
    lines = [r.odd[:, 0:hh], r.even[...], r.odd[:, 1 : hh + 1]]
    stage(
        2, "spatial_one", jnp.concatenate([dot_tn(flat2(a), d2_) for a in lines], axis=0)
    )
    advance(1, 1)
    advance(0, 3)

    def skip_back(k, c):
        r.skip_back[k] = dot_nt(flat2(r.dzs[k]), sc).reshape(hh, PAD, cfg.c_in)
        return c

    loop(skip_back)
    db1, q1 = take_sums(11, [LANES] * 2)
    dg1, (c1, c2, c3) = backward(n1, db1, q1)

    def last(k, acc, c1=c1, c2=c2, c3=c3):
        m = r.mask_one[k]
        f1, f2, f3 = m * c1, m * c2, (m * c3) * col_mask
        for pr in range(2):
            for pc in range(2):
                d = (r.q1[pr, pc, k] * f1 + r.z1[pr, pc, k] * f2 + f3).astype(BF16)
                r.dz1[pr, pc, k] = d
        return acc

    loop(last)
    total = sum(
        dot_tn(flat2(r.x[pr, pc]), flat2(r.dz1[pr, pc])) for pr in range(2) for pc in range(2)
    )
    stage(2, "reduce_one", total)
    advance(2, 0)
    advance(1, 2)
    advance(0, 4)

    def images_back(k, c):
        for pr in range(2):
            for pc in range(2):
                g = dot_nt(flat2(r.dz1[pr, pc, k]), w1).reshape(hh, PAD, cfg.c_in)
                if pr == 0 and pc == 0:
                    g += r.skip_back[k]
                for i in range(hh):
                    for q in range(lane_blocks):
                        r.spread[q, 2 * i + pr, pl.ds(pc, PAD, stride=2), :] = g[
                            i, :, q * LANES : (q + 1) * LANES
                        ]
        for i in range(2 * hh):
            for q in range(lane_blocks):
                lanes = slice(q * LANES, (q + 1) * LANES)
                r.x_in[k, i, :, lanes] = r.spread[q, i, 0 : 2 * wv, :].astype(BF16)
        return c

    loop(images_back)
    back_copy = pltpu.make_async_copy(r.x_in, r.images_grad, r.local_sem.at[2])
    back_copy.start()

    for k in range(4):
        r.mid_gain_grad[k : k + 1, :] = (dg1, dg2, dg4, dg5)[k]
        r.mid_bias_grad[k : k + 1, :] = (db1, db2, db4, db5)[k]
    for k in range(3):
        r.wide_gain_grad[k : k + 1, :] = (dg3, dgs, dg6)[k]
        r.wide_bias_grad[k : k + 1, :] = (db3, db3, db6)[k]

    for phase in range(1, 7):
        advance(2, phase)
        if phase + 2 <= 6:
            advance(1, phase + 2)
        if phase + 4 <= 6:
            advance(0, phase + 4)
    for g, group in enumerate(GROUPS):
        for name, _ in group:
            unstage(g, name, getattr(r, name + "_grad"))
    for copy in out_copies:
        copy.wait()
    out_local.wait()
    back_copy.wait()


def on_device(nr, nc, *args):
    (images, reduce_one, spatial_one, expand_one, shortcut, reduce_two, spatial_two, expand_two,
     mid_gain, mid_bias, wide_gain, wide_bias, widths, depth_gate, cot) = args
    nk, full_rows, full_cols, c_in = images.shape
    hh, wv, c_out = full_rows // 2, full_cols // 2, expand_one.shape[1]
    own = cot.shape[0]
    ndev, nxy = nr * nc, nc // 2
    sizes = [group_rows(g, ndev) for g in GROUPS]

    vmem, smem, hbm = pltpu.VMEM, pltpu.SMEM, pl.ANY
    ins = [
        ("images", images, hbm), ("cot", cot, hbm),
        ("reduce_one", reduce_one, vmem), ("spatial_one", spatial_one.reshape(3, 3 * LANES, LANES), vmem),
        ("expand_one", expand_one, vmem), ("shortcut", shortcut, vmem), ("reduce_two", reduce_two, vmem),
        ("spatial_two", spatial_two.reshape(3, 3 * LANES, LANES), vmem), ("expand_two", expand_two, vmem),
        ("mid_gain", mid_gain, vmem), ("mid_bias", mid_bias, vmem),
        ("wide_gain", wide_gain, vmem), ("wide_bias", wide_bias, vmem),
        ("widths", widths, smem), ("depth_gate", depth_gate, smem),
    ]
    outs = [
        ("out", (own, nr * hh, PAD, c_out), BF16, hbm),
        ("images_grad", images.shape, BF16, hbm),
        ("reduce_one_grad", (c_in, LANES), F32, vmem),
        ("spatial_one_grad", (9 * LANES, LANES), F32, vmem),
        ("expand_one_grad", (LANES, c_out), F32, vmem),
        ("shortcut_grad", (c_in, c_out), F32, vmem),
        ("reduce_two_grad", (c_out, LANES), F32, vmem),
        ("spatial_two_grad", (9 * LANES, LANES), F32, vmem),
        ("expand_two_grad", (LANES, c_out), F32, vmem),
        ("mid_gain_grad", mid_gain.shape, F32, vmem), ("mid_bias_grad", mid_bias.shape, F32, vmem),
        ("wide_gain_grad", wide_gain.shape, F32, vmem), ("wide_bias_grad", wide_bias.shape, F32, vmem),
    ]
    half, quad = (nk, hh, PAD), (2, 2, nk, hh, PAD)
    dma = pltpu.SemaphoreType.DMA
    scratch = [
        ("x_in", vmem(images.shape, BF16)),
        ("spread", vmem((c_in // LANES, 2 * hh, 2 * PAD, LANES), F32)),
        ("x", vmem(quad + (c_in,), BF16)),
        ("z1", vmem(quad + (LANES,), F32)),
        ("s1", vmem(quad + (LANES,), F32)),
        ("q1", vmem(quad + (LANES,), F32)),
        ("dz1", vmem(quad + (LANES,), BF16)),
        ("h1", vmem((2, nk, PAD, LANES), F32)),
        ("even", vmem(half + (3 * LANES,), BF16)),
        ("odd", vmem((nk, hh + 1, PAD, 3 * LANES), BF16)),
        ("dz2", vmem((nk, hh + 1, PAD, 2 * LANES), BF16)),
        ("a4", vmem((nk, hh + 2, PAD, 3 * LANES), BF16)),
        ("dz5", vmem((nk, hh + 2, PAD, 3 * LANES), BF16)),
        ("h2", vmem((nk, PAD, LANES), F32)),
        ("hq2", vmem((nk, PAD, LANES), F32)),
        ("h4", vmem((2, nk, PAD, LANES), F32)),
        ("h5", vmem((2, nk, PAD, LANES), F32)),
        ("hq5", vmem((2, nk, PAD, LANES), F32)),
        ("cot_rows", vmem((nk, hh, wv, c_out), BF16)),
        ("out_rows", vmem(half + (c_out,), BF16)),
        ("skip_back", vmem(half + (c_in,), F32)),
        ("back_two", vmem((3, 3 * LANES, LANES), BF16)),
        ("back_here", vmem((2 * LANES, 4 * LANES), BF16)),
        ("back_below", vmem((2 * LANES, 2 * LANES), BF16)),
        ("mask_one", vmem((nk, 1, LANES), F32)),
        ("mask_two", vmem((nk, 1, LANES), F32)),
        ("gates", vmem((nk, 1, c_out), F32)),
    ]
    scratch += [(n, vmem(half + (LANES,), F32)) for n in ("z2", "s2", "q2", "z4", "s4", "q4", "z5", "s5", "q5")]
    scratch += [(n, vmem(half + (c_out,), F32)) for n in ("z3", "zs", "s3", "q3", "z6", "live")]
    scratch += [(n, vmem(half + (LANES,), BF16)) for n in ("a2", "a5", "dz4")]
    scratch += [(n, vmem(half + (c_out,), BF16)) for n in ("hidden", "dz6", "dz3", "dzs")]
    scratch += [
        ("image_sem", dma((nk,))), ("local_sem", dma((3,))),
        ("sum_send", dma((len(ROUND_ROWS),))), ("sum_recv", dma((len(ROUND_ROWS),))),
        ("halo_send", dma((9,))), ("halo_recv", dma((9,))),
        ("cot_send", dma((nr,))), ("cot_recv", dma((nr,))),
        ("out_send", dma((nr,))), ("out_recv", dma((nr,))),
        ("grad_send", dma((len(GROUPS), 6))), ("grad_recv", dma((len(GROUPS), 6))),
    ]
    scratch += [(f"sums{i}", vmem((ndev, n, LANES), F32)) for i, n in enumerate(ROUND_ROWS)]
    for g, size in enumerate(sizes):
        levels = (size, size // 2, size // nc, size // ndev)
        for level, n in enumerate((2, nxy, nr)):
            scratch.append((f"part{g}_{level}", vmem((levels[level], LANES), BF16)))
            scratch.append((f"came{g}_{level}", vmem((n - 1, levels[level + 1], LANES), BF16)))
        scratch.append((f"full{g}", vmem((size, LANES), BF16)))
    cfg = SimpleNamespace(
        nr=nr, nc=nc, nk=nk, hh=hh, wv=wv, c_in=c_in, c_out=c_out, group_size=sizes,
        names=[n for n, *_ in ins] + [n for n, *_ in outs] + [n for n, _ in scratch],
    )

    def body(*refs):
        named = dict(zip(cfg.names, refs))
        named["sums"] = [named[f"sums{i}"] for i in range(len(ROUND_ROWS))]
        named["part"] = [[named[f"part{g}_{j}"] for j in range(3)] for g in range(len(GROUPS))]
        named["came"] = [[named[f"came{g}_{j}"] for j in range(3)] for g in range(len(GROUPS))]
        named["full"] = [named[f"full{g}"] for g in range(len(GROUPS))]
        inner = SimpleNamespace(**vars(cfg))
        inner.names = list(named)
        mega(inner, *named.values())

    result = pl.pallas_call(
        body,
        out_shape=[jax.ShapeDtypeStruct(s, t) for _, s, t, _ in outs],
        in_specs=[pl.BlockSpec(memory_space=m) for _, _, m in ins],
        out_specs=[pl.BlockSpec(memory_space=m) for _, _, _, m in outs],
        scratch_shapes=[s for _, s in scratch],
        compiler_params=pltpu.CompilerParams(
            collective_id=0, has_side_effects=True, vmem_limit_bytes=60 << 20
        ),
    )(*[a for _, a, _ in ins])
    result = list(result)
    result[0] = result[0][:, :, :wv, :]
    result[3] = result[3].reshape(3, 3, LANES, LANES)
    result[7] = result[7].reshape(3, 3, LANES, LANES)
    return tuple(result)


def solution(mesh):
    nr, nc = mesh.shape["rows"], mesh.shape["crops"]
    whole = P()
    return jax.shard_map(
        functools.partial(on_device, nr, nc),
        mesh=mesh,
        in_specs=(P("crops", "rows", None, None),)
        + (whole,) * 11
        + (P("crops", None), P("crops"), P(("crops", "rows"), None, None, None)),
        out_specs=(P(("crops", "rows"), None, None, None), P("crops", "rows", None, None))
        + (whole,) * 11,
        check_vma=False,
    )
```

time: 878 us -> 153 us (0.17); the launches traced: 868 us -> 152 us
  blocking collectives: 486 us -> 0 us
  Pallas kernels: 0 us -> 139 us
  waiting for transfers between devices: 130 us -> 0 us
  local copies, waits for them, and re-layouts: 133 us -> 12.4 us
  other arithmetic: 43.4 us -> 0 us
  matrix products: 36.7 us -> 0 us
  starting transfers between devices: 23.4 us -> 0 us
  between operations: 16.3 us -> 0.69 us
    psum x12 -> x0, blocking collectives: 486 us -> none  [the longest x6 244 us: norm_forward(): lax.psum(local_stats(values, selector), ('rows', 'crops'))]
    pallas_call x0 -> x1, Pallas kernels: none -> 139 us  [on_device(): pl.pallas_call(body, out_shape=[jax.ShapeDtypeStruct(s, t) for _, s, t, _...]
    psum x1 -> x0, waiting for transfers between devices: 115 us -> none  [on_device(): lax.psum((reduce_one_grad, spatial_one_grad, expand_one_grad, shortcut_gr...]
    slice x18 -> x0, local copies, waits for them, and re-layouts: 95.5 us -> none  [the longest x10 80.5 us: spatial_weight(): padded[:, row_tap:row_tap + stride * (rows_out - 1) + 1:stride, col_tap:c...]
    dot_general x33 -> x0, matrix products: 32.8 us -> none  [the longest x5 13.5 us: dense_back(): jnp.einsum('nhwd,cd->nhwc', upstream, weight, preferred_element_type=jnp....]
    ppermute x6 -> x0, starting transfers between devices: 15.3 us -> none  [the longest x2 7.03 us: padded_2(): lax.ppermute(lax.slice_in_dim(block, block.shape[dim] - width, None, axis...]
    convert_element_type x14 -> x0, other arithmetic: 12.6 us -> none  [the longest x1 2.98 us: on_device(): hidden_rows = jax.nn.silu(pre_one).astype(low_type)]
    all_to_all x2 -> x0, waiting for transfers between devices: 12.4 us -> none  [the longest x1 12.4 us: on_device(): lax.all_to_all(result, 'rows', split_axis=0, concat_axis=1, tiled=True)]
  transfers between devices with their start and end apart: 9 -> 0, of which waited for: 4 -> 0; matrix products, arithmetic and copies ran while one was open for 18% -> 0% of each run, Pallas kernels for 0% -> 0%
where the time goes in v2:
time: 153 us; the launch traced here: 152 us
  Pallas kernels  139 us (91%)
  local copies, waits for them, and re-layouts  12.4 us (8%)
    pallas_call x1, Pallas kernels, on_device(): pl.pallas_call(body, out_shape=[jax.ShapeDtypeStruct(s, t) for _, s, t, _...  139 us
    unnamed x38, local copies, waits for them, and re-layouts  12.4 us

profile of v2, /device:TPU:0, one launch (start us, length us, event | category | flops | bytes accessed | tf_op | source)
XLA Modules:
  0.0 152.3 jit_solution(2177667128322793623)
XLA Ops:
  0.6 1.3 copy.28.refs_13_
  2.0 139.3 %shard_map.246 = (bf16[1,28,32,512]{3,2,1,0:T(8,128)(2,1)}, bf16[4,14,56,256]{3,2,1,0:T(8,128)(2,1)}, f32[256,128]{1,0:T(8,128)}, f32[1152,128]{1,0:T(8,128)}, f...) custom-call(bf16[4,14,56,256]{3,2,1,0:T(8,128)(2,1)} %refs_0_.1, ...), custom_call_target="tpu_custom_call" | custom-call | tf_op jit(solution)/shard_map/pallas_call | solution.py:861
  141.2 0.0 copy-start
  141.2 2.3 %copy.42 = bf16[1,28,28,512]{3,2,1,0:T(8,128)(2,1)} copy(bf16[1,28,28,512]{3,2,1,0:T(8,128)(2,1)} %bitcast.5) | data formatting | bytes 1605632
  143.6 0.0 copy-done
  143.6 1.2 copy.43
  144.7 0.0 copy-done.7
  144.7 0.7 copy.44
  145.4 0.0 copy-done.2
  145.4 0.8 copy.45
  146.2 0.0 copy-done.6
  146.2 0.7 copy.46
  146.9 0.0 copy-done.3
  146.9 0.0 copy-start.8
  146.9 0.8 copy.47
  147.7 0.0 copy-done.5
  147.7 0.7 copy.48
  148.5 0.8 copy.49
  149.3 0.0 copy-done.4
  149.3 0.7 copy.50
  150.0 0.6 copy.51
  150.6 0.6 copy.52
  151.1 0.6 copy.53
  151.7 0.6 copy.54
  (15 shorter events, 0.0 us)
Async XLA Ops:
  141.2 2.3 %copy-start = (bf16[4,14,56,256]{3,2,1,0:T(8,128)(2,1)S(1)}, bf16[4,14,56,256]{3,2,1,0:T(8,128)(2,1)}, u32[]{:S(2)}) copy-start(bf16[4,14,56,256]{3,2,1,0:T(8,128)(2,1)} %get-tuple-element.53) | copy-start | bytes 4816900
  143.6 1.2 copy-start.7
  143.6 1.8 %copy-start.2 = (f32[1152,128]{1,0:T(8,128)S(1)}, f32[1152,128]{1,0:T(8,128)}, u32[]{:S(2)}) copy-start(f32[1152,128]{1,0:T(8,128)} %get-tuple-element.29) | copy-start | bytes 1769476
  143.6 2.6 %copy-start.6 = (f32[128,512]{1,0:T(8,128)S(1)}, f32[128,512]{1,0:T(8,128)}, u32[]{:S(2)}) copy-start(f32[128,512]{1,0:T(8,128)} %get-tuple-element.56) | copy-start | bytes 786436
  144.7 2.2 %copy-start.3 = (f32[256,512]{1,0:T(8,128)S(1)}, f32[256,512]{1,0:T(8,128)}, u32[]{:S(2)}) copy-start(f32[256,512]{1,0:T(8,128)} %get-tuple-element.57) | copy-start | bytes 1572868
  144.7 3.0 %copy-start.5 = (f32[512,128]{1,0:T(8,128)S(1)}, f32[512,128]{1,0:T(8,128)}, u32[]{:S(2)}) copy-start(f32[512,128]{1,0:T(8,128)} %get-tuple-element.58) | copy-start | bytes 786436
  145.4 3.1 %copy-start.1 = (f32[1152,128]{1,0:T(8,128)S(1)}, f32[1152,128]{1,0:T(8,128)}, u32[]{:S(2)}) copy-start(f32[1152,128]{1,0:T(8,128)} %get-tuple-element.33) | copy-start | bytes 1769476
  146.2 3.0 %copy-start.4 = (f32[128,512]{1,0:T(8,128)S(1)}, f32[128,512]{1,0:T(8,128)}, u32[]{:S(2)}) copy-start(f32[128,512]{1,0:T(8,128)} %get-tuple-element.60) | copy-start | bytes 786436
  146.9 3.0 %copy-start.11 = (f32[4,128]{1,0:T(4,128)S(1)}, f32[4,128]{1,0:T(4,128)}, u32[]{:S(2)}) copy-start(f32[4,128]{1,0:T(4,128)} %get-tuple-element.61) | copy-start | bytes 6148
  146.9 3.6 %copy-start.10 = (f32[4,128]{1,0:T(4,128)S(1)}, f32[4,128]{1,0:T(4,128)}, u32[]{:S(2)}) copy-start(f32[4,128]{1,0:T(4,128)} %get-tuple-element.62) | copy-start | bytes 6148
  146.9 4.2 %copy-start.9 = (f32[3,512]{1,0:T(4,128)S(1)}, f32[3,512]{1,0:T(4,128)}, u32[]{:S(2)}) copy-start(f32[3,512]{1,0:T(4,128)} %get-tuple-element.63) | copy-start | bytes 18436
  146.9 4.8 %copy-start.8 = (f32[3,512]{1,0:T(4,128)S(1)}, f32[3,512]{1,0:T(4,128)}, u32[]{:S(2)}) copy-start(f32[3,512]{1,0:T(4,128)} %get-tuple-element.64) | copy-start | bytes 18436

commit v3 on v2

--- a/solution.py
+++ b/solution.py
@@ -91,8 +91,8 @@
     lane = lax.broadcasted_iota(jnp.int32, (1, LANES), 1)
     for k in range(nk):
         gate = (jnp.full((1, LANES), r.depth_gate[k], jnp.int32) > 0).astype(F32)
-        r.mask_one[k] = (lane < r.widths[k, 0]).astype(F32)
-        r.mask_two[k] = (lane < r.widths[k, 1]).astype(F32) * gate
+        r.mask_one[k] = (lane < r.widths[0, k]).astype(F32)
+        r.mask_two[k] = (lane < r.widths[1, k]).astype(F32) * gate
         r.gates[k] = jnp.concatenate([gate] * 4, axis=1)
     col_mask = (lax.broadcasted_iota(jnp.int32, (PAD, 1), 0) < wv).astype(F32)
     half_mask = 0.5 * col_mask
@@ -270,17 +270,6 @@
             lo = at + q * n
             r.part[g][0][lo : lo + n, :] = value[:, q * LANES : (q + 1) * LANES].astype(BF16)
 
-    def unstage(g, name, ref):
-        at = 0
-        for other, rows in GROUPS[g]:
-            if other == name:
-                break
-            at += rows
-        n = ref.shape[0]
-        for q in range(ref.shape[1] // LANES):
-            lo = at + q * n
-            ref[:, q * LANES : (q + 1) * LANES] = r.full[g][lo : lo + n, :].astype(F32)
-
     def coefficients(total, square, count, gain, bias):
         n = jnp.maximum(count, 1.0)
         mu = total / n
@@ -299,6 +288,40 @@
 
     def zero8(width, count):
         return tuple(jnp.zeros((8, width), F32) for _ in range(count))
+
+    def row_pieces(src_of, dst_of, send, recv, local):
+        pieces = []
+        for w, (lo, hi) in enumerate(cfg.pieces):
+            for k in range(1, nr):
+                p = lax.rem(row + k, nr)
+                pieces.append(
+                    pltpu.make_async_remote_copy(
+                        src_ref=src_of(p, lo, hi - lo),
+                        dst_ref=dst_of(lo, hi - lo),
+                        send_sem=send.at[w, k],
+                        recv_sem=recv.at[w, k],
+                        device_id=(p, col),
+                        device_id_type=MESH,
+                    )
+                )
+        here = pltpu.make_async_copy(src_of(row, 0, hh), dst_of(0, hh), local)
+        return pieces, here
+
+    def start_pieces(pieces, w):
+        for copy in pieces[w * (nr - 1) : (w + 1) * (nr - 1)]:
+            copy.start()
+
+    cot_copies, cot_local = row_pieces(
+        lambda p, lo, n: r.cot.at[:, pl.ds(p * hh + lo, n)],
+        lambda lo, n: r.cot_rows.at[pl.ds(row * own, own), pl.ds(lo, n)],
+        r.cot_send, r.cot_recv, r.local_sem.at[0],
+    )
+    out_copies, out_local = row_pieces(
+        lambda p, lo, n: r.out_rows.at[pl.ds(p * own, own), pl.ds(lo, n)],
+        lambda lo, n: r.out.at[:, pl.ds(row * hh + lo, n)],
+        r.out_send, r.out_recv, r.local_sem.at[1],
+    )
+    cot_local.start()
 
     lane_blocks = cfg.c_in // LANES
     for slot in range(2 * hh):
@@ -330,31 +353,16 @@
                 s2 += m * folded(z * z)
         return s1, s2
 
-    s1, s2 = loop(first, acc)
+    acc = lax.fori_loop(0, nk // 2, first, acc)
+    pl.semaphore_wait(barrier, ndev - 1)
+    start_pieces(cot_copies, 0)
+    s1, s2 = lax.fori_loop(nk // 2, nk, first, acc)
     count_one = sum(r.mask_one[k] for k in range(nk))
     count_two = sum(r.mask_two[k] for k in range(nk))
-    pl.semaphore_wait(barrier, ndev - 1)
     send_sums(0, [row_sum(s1), row_sum(s2), count_one, count_two])
     halo_z1 = (0, False, r.z1.at[1, :, :, hh - 1], r.h1)
     halo_start(*halo_z1)
-
-    def cot_copy(k, p):
-        return pltpu.make_async_remote_copy(
-            src_ref=r.cot.at[:, pl.ds(p * hh, hh)],
-            dst_ref=r.cot_rows.at[pl.ds(row * own, own)],
-            send_sem=r.cot_send.at[k],
-            recv_sem=r.cot_recv.at[k],
-            device_id=(p, col),
-            device_id_type=MESH,
-        )
-
-    cot_copies = [cot_copy(k, lax.rem(row + k, nr)) for k in range(1, nr)]
-    cot_local = pltpu.make_async_copy(
-        r.cot.at[:, pl.ds(row * hh, hh)], r.cot_rows.at[pl.ds(row * own, own)], r.local_sem.at[0]
-    )
-    for copy in cot_copies:
-        copy.start()
-    cot_local.start()
+    start_pieces(cot_copies, 1)
 
     sc = r.shortcut[...]
 
@@ -416,6 +424,7 @@
     send_sums(1, [row_sum(s1), row_sum(s2)])
     halo_z2 = (1, True, r.z2.at[:, 0], r.h2)
     halo_start(*halo_z2)
+    start_pieces(cot_copies, 2)
     t1, t2 = take_sums(1, [LANES] * 2)
     n2 = coefficients(t1, t2, active_one * half_px, r.mid_gain[1:2, :], r.mid_bias[1:2, :])
     e1 = r.expand_one[...]
@@ -432,6 +441,7 @@
 
     s1, s2 = loop(third, zero8(cfg.c_out, 2))
     send_sums(2, [row_sum(s1), row_sum(s2), row_sum(zs1), row_sum(zs2)])
+    start_pieces(cot_copies, 3)
     t1, t2, ts1, ts2 = take_sums(2, [cfg.c_out] * 4)
     all_px = float(nk * nc) * float(nr) * half_px
     n3 = coefficients(t1, t2, all_px, r.wide_gain[0:1, :], r.wide_bias[0:1, :])
@@ -458,6 +468,7 @@
     ]
     for h in halos_z4:
         halo_start(*h)
+    start_pieces(cot_copies, 4)
     t1, t2 = take_sums(3, [LANES] * 2)
     n4 = coefficients(t1, t2, active_two * half_px, r.mid_gain[2:3, :], r.mid_bias[2:3, :])
     for h in halos_z4:
@@ -493,6 +504,7 @@
     ]
     for h in halos_z5:
         halo_start(*h)
+    start_pieces(cot_copies, 5)
     t1, t2 = take_sums(4, [LANES] * 2)
     n5 = coefficients(t1, t2, active_two * half_px, r.mid_gain[3:4, :], r.mid_bias[3:4, :])
     e2 = r.expand_two[...]
@@ -529,7 +541,7 @@
             hid = r.hidden[k, i].astype(F32)
             z = r.z6[k, i]
             a, s = half_silu(0.5 * hid + (z * a6 + b6))
-            r.out_rows[k, i] = jnp.where(g > 0.0, a, hid).astype(BF16)
+            r.out_rows[k, i] = jnp.where(g > 0.0, a, hid)[:wv].astype(BF16)
             live = g * cot_row(k, i) * s
             r.live[k, i] = live
             d1 += folded(live)
@@ -539,22 +551,7 @@
     d1, d2 = loop(seventh, zero8(cfg.c_out, 2))
     send_sums(6, [row_sum(d1), row_sum(d2)])
 
-    def out_copy(k, p):
-        return pltpu.make_async_remote_copy(
-            src_ref=r.out_rows.at[pl.ds(p * own, own)],
-            dst_ref=r.out.at[:, pl.ds(row * hh, hh)],
-            send_sem=r.out_send.at[k],
-            recv_sem=r.out_recv.at[k],
-            device_id=(p, col),
-            device_id_type=MESH,
-        )
-
-    out_copies = [out_copy(k, lax.rem(row + k, nr)) for k in range(1, nr)]
-    out_local = pltpu.make_async_copy(
-        r.out_rows.at[pl.ds(row * own, own)], r.out.at[:, pl.ds(row * hh, hh)], r.local_sem.at[1]
-    )
-    for copy in out_copies:
-        copy.start()
+    start_pieces(out_copies, 0)
     out_local.start()
     db6, q6 = take_sums(6, [cfg.c_out] * 2)
     dg6, (c1, c2, c3) = backward(n6, db6, q6)
@@ -577,6 +574,7 @@
     ]
     for h in halos_q5:
         halo_start(*h)
+    start_pieces(out_copies, 1)
     stage(0, "expand_two", dot_tn(flat2(r.a5[...]), flat2(r.dz6[...])))
     for h in halos_z5:
         halo_wait(*h)
@@ -600,6 +598,7 @@
 
     d1, d2 = loop(ninth, zero8(LANES, 2))
     send_sums(8, [row_sum(d1), row_sum(d2)])
+    start_pieces(out_copies, 2)
     d5 = flat2(r.dz5[:, 1 : hh + 1, :, LANES : 2 * LANES])
     stage(
         0,
@@ -627,6 +626,7 @@
 
     d1, d2, d3 = loop(tenth, zero8(cfg.c_out, 3))
     send_sums(9, [row_sum(d1), row_sum(d2), row_sum(d3)])
+    start_pieces(out_copies, 3)
     stage(1, "reduce_two", dot_tn(flat2(r.hidden[...]), flat2(r.dz4[...])))
     advance(0, 1)
     db3, q3, qs = take_sums(9, [cfg.c_out] * 3)
@@ -648,6 +648,7 @@
     send_sums(10, [row_sum(d1), row_sum(d2)])
     halo_q2 = (8, True, r.q2.at[:, 0], r.hq2)
     halo_start(*halo_q2)
+    start_pieces(out_copies, 4)
     stage(1, "expand_one", dot_tn(flat2(r.a2[...]), flat2(r.dz3[...])))
     stage(1, "shortcut", dot_tn(flat2(r.x[0, 0]), flat2(r.dzs[...])))
     advance(1, 0)
@@ -684,6 +685,7 @@
 
     d1, d2 = loop(twelfth, zero8(LANES, 2))
     send_sums(11, [row_sum(d1), row_sum(d2)])
+    start_pieces(out_copies, 5)
     d2_ = flat2(r.dz2[:, 0:hh, :, 0:LANES])
     lines = [r.odd[:, 0:hh], r.even[...], r.odd[:, 1 : hh + 1]]
     stage(
@@ -739,12 +741,10 @@
     back_copy = pltpu.make_async_copy(r.x_in, r.images_grad, r.local_sem.at[2])
     back_copy.start()
 
-    for k in range(4):
-        r.mid_gain_grad[k : k + 1, :] = (dg1, dg2, dg4, dg5)[k]
-        r.mid_bias_grad[k : k + 1, :] = (db1, db2, db4, db5)[k]
-    for k in range(3):
-        r.wide_gain_grad[k : k + 1, :] = (dg3, dgs, dg6)[k]
-        r.wide_bias_grad[k : k + 1, :] = (db3, db3, db6)[k]
+    for k, v in enumerate((dg1, dg2, dg4, dg5, db1, db2, db4, db5)):
+        r.mid_grads[k : k + 1, :] = v
+    for k, v in enumerate((dg3, dgs, dg6, db3, db3, db6)):
+        r.wide_grads[k : k + 1, :] = v
 
     for phase in range(1, 7):
         advance(2, phase)
@@ -752,9 +752,14 @@
             advance(1, phase + 2)
         if phase + 4 <= 6:
             advance(0, phase + 4)
-    for g, group in enumerate(GROUPS):
-        for name, _ in group:
-            unstage(g, name, getattr(r, name + "_grad"))
+    result_copies = [
+        pltpu.make_async_copy(r.full[g], result, r.full_sem.at[g])
+        for g, result in enumerate((r.summed0, r.summed1, r.summed2))
+    ]
+    for copy in result_copies:
+        copy.start()
+    for copy in result_copies:
+        copy.wait()
     for copy in out_copies:
         copy.wait()
     out_local.wait()
@@ -778,20 +783,15 @@
         ("spatial_two", spatial_two.reshape(3, 3 * LANES, LANES), vmem), ("expand_two", expand_two, vmem),
         ("mid_gain", mid_gain, vmem), ("mid_bias", mid_bias, vmem),
         ("wide_gain", wide_gain, vmem), ("wide_bias", wide_bias, vmem),
-        ("widths", widths, smem), ("depth_gate", depth_gate, smem),
+        ("widths", widths.T, smem), ("depth_gate", depth_gate, smem),
     ]
     outs = [
-        ("out", (own, nr * hh, PAD, c_out), BF16, hbm),
+        ("out", cot.shape, BF16, hbm),
         ("images_grad", images.shape, BF16, hbm),
-        ("reduce_one_grad", (c_in, LANES), F32, vmem),
-        ("spatial_one_grad", (9 * LANES, LANES), F32, vmem),
-        ("expand_one_grad", (LANES, c_out), F32, vmem),
-        ("shortcut_grad", (c_in, c_out), F32, vmem),
-        ("reduce_two_grad", (c_out, LANES), F32, vmem),
-        ("spatial_two_grad", (9 * LANES, LANES), F32, vmem),
-        ("expand_two_grad", (LANES, c_out), F32, vmem),
-        ("mid_gain_grad", mid_gain.shape, F32, vmem), ("mid_bias_grad", mid_bias.shape, F32, vmem),
-        ("wide_gain_grad", wide_gain.shape, F32, vmem), ("wide_bias_grad", wide_bias.shape, F32, vmem),
+        ("summed0", (sizes[0], LANES), BF16, hbm),
+        ("summed1", (sizes[1], LANES), BF16, hbm),
+        ("summed2", (sizes[2], LANES), BF16, hbm),
+        ("mid_grads", (8, LANES), F32, vmem), ("wide_grads", (6, c_out), F32, vmem),
     ]
     half, quad = (nk, hh, PAD), (2, 2, nk, hh, PAD)
     dma = pltpu.SemaphoreType.DMA
@@ -815,7 +815,7 @@
         ("h5", vmem((2, nk, PAD, LANES), F32)),
         ("hq5", vmem((2, nk, PAD, LANES), F32)),
         ("cot_rows", vmem((nk, hh, wv, c_out), BF16)),
-        ("out_rows", vmem(half + (c_out,), BF16)),
+        ("out_rows", vmem((nk, hh, wv, c_out), BF16)),
         ("skip_back", vmem(half + (c_in,), F32)),
         ("back_two", vmem((3, 3 * LANES, LANES), BF16)),
         ("back_here", vmem((2 * LANES, 4 * LANES), BF16)),
@@ -832,8 +832,9 @@
         ("image_sem", dma((nk,))), ("local_sem", dma((3,))),
         ("sum_send", dma((len(ROUND_ROWS),))), ("sum_recv", dma((len(ROUND_ROWS),))),
         ("halo_send", dma((9,))), ("halo_recv", dma((9,))),
-        ("cot_send", dma((nr,))), ("cot_recv", dma((nr,))),
-        ("out_send", dma((nr,))), ("out_recv", dma((nr,))),
+        ("cot_send", dma((6, nr))), ("cot_recv", dma((6, nr))),
+        ("out_send", dma((6, nr))), ("out_recv", dma((6, nr))),
+        ("full_sem", dma((len(GROUPS),))),
         ("grad_send", dma((len(GROUPS), 6))), ("grad_recv", dma((len(GROUPS), 6))),
     ]
     scratch += [(f"sums{i}", vmem((ndev, n, LANES), F32)) for i, n in enumerate(ROUND_ROWS)]
@@ -845,6 +846,7 @@
         scratch.append((f"full{g}", vmem((size, LANES), BF16)))
     cfg = SimpleNamespace(
         nr=nr, nc=nc, nk=nk, hh=hh, wv=wv, c_in=c_in, c_out=c_out, group_size=sizes,
+        pieces=[(i * hh // 6, (i + 1) * hh // 6) for i in range(6)],
         names=[n for n, *_ in ins] + [n for n, *_ in outs] + [n for n, _ in scratch],
     )
 
@@ -868,11 +870,94 @@
             collective_id=0, has_side_effects=True, vmem_limit_bytes=60 << 20
         ),
     )(*[a for _, a, _ in ins])
-    result = list(result)
-    result[0] = result[0][:, :, :wv, :]
-    result[3] = result[3].reshape(3, 3, LANES, LANES)
-    result[7] = result[7].reshape(3, 3, LANES, LANES)
-    return tuple(result)
+    return finished(result, mid_gain.shape, wide_gain.shape)
+
+
+WEIGHTS = (
+    ("reduce_one", (256, 128)),
+    ("spatial_one", (3, 3, 128, 128)),
+    ("expand_one", (128, 512)),
+    ("shortcut", (256, 512)),
+    ("reduce_two", (512, 128)),
+    ("spatial_two", (3, 3, 128, 128)),
+    ("expand_two", (128, 512)),
+)
+
+
+def finish(*refs):
+    ins, outs, held = refs[:7], refs[7:20], refs[20:27]
+    wide_to, (in_sem, out_sem) = refs[27:38], refs[38:]
+    chunks = [(0, i) for i in range(4)] + [(1, i) for i in range(4)]
+
+    def part(ref, which, i):
+        n = ref.shape[1 - which] // 4
+        return ref.at[:, pl.ds(i * n, n)] if which == 0 else ref.at[pl.ds(i * n, n)]
+
+    small = [pltpu.make_async_copy(ins[i], held[i], in_sem.at[i]) for i in (5, 6, 2, 3, 4)]
+    large = [
+        pltpu.make_async_copy(part(ins[w], w, i), part(held[w], w, i), in_sem.at[7 + 4 * w + i])
+        for w, i in chunks
+    ]
+    for copy in small + large:
+        copy.start()
+    leaving = []
+
+    def leave(src, dst):
+        copy = pltpu.make_async_copy(src, dst, out_sem.at[len(leaving)])
+        copy.start()
+        leaving.append(copy)
+
+    for i in range(2):
+        small[i].wait()
+    mid, wide = held[5], held[6]
+    grads = (mid[0:4, :], mid[4:8, :], wide[0:3, :], wide[3:6, :])
+    for ref, value, to in zip(wide_to[7:], grads, outs[9:]):
+        ref[...] = value
+        leave(ref, to)
+    names = [name for name, _ in WEIGHTS]
+    for g, group in enumerate(GROUPS):
+        small[2 + g].wait()
+        summed = held[2 + g]
+        at = 0
+        for name, rows in group:
+            which = names.index(name)
+            ref = wide_to[which]
+            if len(ref.shape) == 4:
+                for i in range(9):
+                    lo = at + i * LANES
+                    ref[i // 3, i % 3] = summed[lo : lo + LANES, :].astype(F32)
+            else:
+                n = ref.shape[0]
+                for q in range(ref.shape[1] // LANES):
+                    lo = at + q * n
+                    ref[:, q * LANES : (q + 1) * LANES] = summed[lo : lo + n, :].astype(F32)
+            leave(ref, outs[2 + which])
+            at += rows
+    for copy, (w, i) in zip(large, chunks):
+        copy.wait()
+        leave(part(held[w], w, i), part(outs[w], w, i))
+    for copy in leaving:
+        copy.wait()
+
+
+def finished(parts, mid_shape, wide_shape):
+    hbm = pl.BlockSpec(memory_space=pl.ANY)
+    outs = [jax.ShapeDtypeStruct(p.shape, p.dtype) for p in parts[:2]]
+    outs += [jax.ShapeDtypeStruct(s, F32) for _, s in WEIGHTS]
+    outs += [jax.ShapeDtypeStruct(s, F32) for s in (mid_shape, mid_shape, wide_shape, wide_shape)]
+    dma = pltpu.SemaphoreType.DMA
+    return tuple(
+        pl.pallas_call(
+            finish,
+            out_shape=outs,
+            in_specs=[hbm] * 7,
+            out_specs=[hbm] * 13,
+            scratch_shapes=[pltpu.VMEM(p.shape, p.dtype) for p in parts]
+            + [pltpu.VMEM(o.shape, o.dtype) for o in outs[2:]]
+            + [dma((15,)), dma((19,))],
+            compiler_params=pltpu.CompilerParams(vmem_limit_bytes=60 << 20),
+        )(*parts)
+    )
 
 
 def solution(mesh):

time: 153 us -> 130 us (0.85)
  local copies, waits for them, and re-layouts: 12.4 us -> 0 us
  Pallas kernels: 139 us -> 129 us
    pallas_call x1, Pallas kernels: 139 us -> 125 us  [on_device(): pl.pallas_call(body, out_shape=[jax.ShapeDtypeStruct(s, t) for _, s, t, _...]
    unnamed x38 -> x0, local copies, waits for them, and re-layouts: 12.4 us -> none
    pallas_call x0 -> x1, Pallas kernels: none -> 3.7 us  [finished(): pl.pallas_call(finish, out_shape=outs, in_specs=[hbm] * 7, out_specs=[hbm...]
where the time goes in v3:
time: 130 us; the launch traced here: 129 us
  Pallas kernels  129 us (99%)
    pallas_call x1, Pallas kernels, on_device(): pl.pallas_call(body, out_shape=[jax.ShapeDtypeStruct(s, t) for _, s, t, _...  125 us
    pallas_call x1, Pallas kernels, finished(): pl.pallas_call(finish, out_shape=outs, in_specs=[hbm] * 7, out_specs=[hbm...  3.7 us

profile of v3, /device:TPU:0, one launch (start us, length us, event | category | flops | bytes accessed | tf_op | source)
XLA Modules:
  0.0 129.4 jit_solution(170615355475871726)
XLA Ops:
  0.7 125.0 %shard_map.246 = (bf16[1,28,28,512]{3,2,1,0:T(8,128)(2,1)}, bf16[4,14,56,256]{3,2,1,0:T(8,128)(2,1)}, bf16[2048,128]{1,0:T(8,128)(2,1)}, bf16[2048,128]{1,0:T(8,...) custom-call(bf16[4,14,56,256]{3,2,1,0:T(8,128)(2,1)} %refs_0_.1, ...), custom_call_target="tpu_custom_call" | custom-call | tf_op jit(solution)/shard_map/pallas_call | solution.py:863
  125.7 3.7 %shard_map.247 = (bf16[1,28,28,512]{3,2,1,0:T(8,128)(2,1)}, bf16[4,14,56,256]{3,2,1,0:T(8,128)(2,1)}, f32[256,128]{1,0:T(8,128)}, f32[3,3,128,128]{3,2,1,0:T(8,1...) custom-call(bf16[1,28,28,512]{3,2,1,0:T(8,128)(2,1)} %get-tuple-elem, ...), custom_call_target="tpu_custom_call" | custom-call | tf_op jit(solution)/shard_map/pallas_call | solution.py:950

commit v4 on v3

--- a/solution.py
+++ b/solution.py
@@ -15,18 +15,25 @@
 PAD = 32
 LANES = 128
 
-ROUND_ROWS = (4, 2, 16, 2, 2, 8, 8, 2, 2, 12, 2, 2)
+ROUND_ROWS = (4, 2, 8, 2, 2, 8, 8, 2, 2, 12, 2, 2)
+WIDE = (2, 5, 6, 9)
 
 GROUPS = (
-    (("expand_two", 512), ("spatial_two", 1152)),
-    (("reduce_two", 512), ("expand_one", 512), ("shortcut", 1024)),
-    (("spatial_one", 1152), ("reduce_one", 256)),
+    (("expand_two", 512),),
+    (("spatial_two", 1152),),
+    (("reduce_two", 512),),
+    (("expand_one", 512), ("shortcut", 1024)),
+    (("spatial_one", 1152),),
 )
 
 
 def group_rows(group, devices):
     unit = 16 * devices
     return -(-sum(rows for _, rows in group) // unit) * unit
+
+
+def split(rows, parts):
+    return [(i * rows // parts, (i + 1) * rows // parts) for i in range(parts)]
 
 
 def dot(a, b):
@@ -59,8 +66,7 @@
     return x.reshape(-1, x.shape[-1])
 
 
-def mega(cfg, *refs):
-    r = SimpleNamespace(**dict(zip(cfg.names, refs)))
+def mega(cfg, r):
     nr, nc, nk, hh, wv = cfg.nr, cfg.nc, cfg.nk, cfg.hh, cfg.wv
     ndev, nxy, own = nr * nc, nc // 2, nk // nr
     m_half = hh * PAD
@@ -69,12 +75,6 @@
     xy, core = lax.div(col, 2), lax.rem(col, 2)
     me = row * nc + col
 
-    image_copies = [
-        pltpu.make_async_copy(r.images.at[k], r.x_in.at[k], r.image_sem.at[k]) for k in range(nk)
-    ]
-    for copy in image_copies:
-        copy.start()
-
     barrier = pltpu.get_barrier_semaphore()
 
     def place(i):
@@ -87,6 +87,23 @@
         return c
 
     lax.fori_loop(1, ndev, greet, 0)
+
+    image_copies = [
+        pltpu.make_async_copy(r.images.at[k], r.x_in.at[k], r.image_sem.at[k]) for k in range(nk)
+    ]
+    weight_copies = {
+        name: pltpu.make_async_copy(r.weights[name], r.held[name], r.weight_sem.at[i])
+        for i, name in enumerate(cfg.order)
+    }
+    for i, copy in enumerate(weight_copies.values()):
+        copy.start()
+        if i == 0:
+            for other in image_copies:
+                other.start()
+
+    def arrived(*names):
+        for name in names:
+            weight_copies[name].wait()
 
     lane = lax.broadcasted_iota(jnp.int32, (1, LANES), 1)
     for k in range(nk):
@@ -97,85 +114,158 @@
     col_mask = (lax.broadcasted_iota(jnp.int32, (PAD, 1), 0) < wv).astype(F32)
     half_mask = 0.5 * col_mask
 
-    def tap(ref, i, j):
-        return ref[i, j * LANES : (j + 1) * LANES, :].T
-
-    for i in range(3):
-        for j in range(3):
-            r.back_two[i, j * LANES : (j + 1) * LANES, :] = tap(r.spatial_two, 2 - i, 2 - j)
-    zeros = jnp.zeros((LANES, LANES), BF16)
-    k1 = r.spatial_one
-    here = [[tap(k1, 2, 2), tap(k1, 1, 2), tap(k1, 2, 1), tap(k1, 1, 1)],
-            [tap(k1, 2, 0), tap(k1, 1, 0), zeros, zeros]]
-    below = [[tap(k1, 0, 2), tap(k1, 0, 1)], [tap(k1, 0, 0), zeros]]
-    for ref, blocks in ((r.back_here, here), (r.back_below, below)):
-        for i, line in enumerate(blocks):
-            for j, block in enumerate(line):
-                ref[i * LANES : (i + 1) * LANES, j * LANES : (j + 1) * LANES] = block
+    def to_all(copy_to):
+        def send(k, c):
+            copy_to(lax.rem(me + k, ndev)).start()
+            return c
+
+        lax.fori_loop(1, ndev, send, 0)
+
+    def sum_copy(idx, p):
+        mine = r.sums[idx].at[me]
+        return pltpu.make_async_remote_copy(
+            src_ref=mine,
+            dst_ref=mine,
+            send_sem=r.sum_send.at[idx],
+            recv_sem=r.sum_recv.at[idx],
+            device_id=place(p),
+            device_id_type=MESH,
+        )
+
+    def pair_copy(step, src, dst):
+        return pltpu.make_async_remote_copy(
+            src_ref=src,
+            dst_ref=dst,
+            send_sem=r.pair_send.at[step],
+            recv_sem=r.pair_recv.at[step],
+            device_id=(row, xy * 2 + 1 - core),
+            device_id_type=MESH,
+        )
+
+    def lines(vectors):
+        return [v[:, q * LANES : (q + 1) * LANES] for v in vectors for q in range(v.shape[1] // LANES)]
 
     def send_sums(idx, vectors):
-        buf, rows = r.sums[idx], ROUND_ROWS[idx]
-        at = 0
-        for v in vectors:
-            for q in range(v.shape[1] // LANES):
-                buf[me, at : at + 1, :] = v[:, q * LANES : (q + 1) * LANES]
-                at += 1
-        assert at == rows
-
-        def send(k, c):
-            pltpu.make_async_remote_copy(
-                src_ref=buf.at[me],
-                dst_ref=buf.at[me],
-                send_sem=r.sum_send.at[idx],
-                recv_sem=r.sum_recv.at[idx],
-                device_id=place(lax.rem(me + k, ndev)),
-                device_id_type=MESH,
-            ).start()
-            return c
-
-        lax.fori_loop(1, ndev, send, 0)
+        rows = lines(vectors)
+        assert len(rows) == ROUND_ROWS[idx]
+        if idx in WIDE:
+            half = len(rows) // 2
+            both, came = r.both[idx], r.from_pair[idx]
+            for at, v in enumerate(rows):
+                both[at // half, at % half : at % half + 1, :] = v
+            copy = pair_copy(idx, both.at[1 - core], came)
+            copy.start()
+            copy.wait()
+            r.sums[idx][me] = both[core] + came[...]
+        else:
+            for at, v in enumerate(rows):
+                r.sums[idx][me, at : at + 1, :] = v
+        to_all(lambda p: sum_copy(idx, p))
 
     def take_sums(idx, widths):
         buf = r.sums[idx]
         others = buf.at[pl.ds(0, ndev - 1)]
         pltpu.make_async_copy(others, others, r.sum_recv.at[idx]).wait()
-        total = jnp.sum(buf[...], axis=0)
+        if idx in WIDE:
+            half = ROUND_ROWS[idx] // 2
+            total = jnp.sum(buf[...].reshape(ndev // 2, 2, half, LANES), axis=0)
+            rows = [total[at // half, at % half : at % half + 1, :] for at in range(2 * half)]
+        else:
+            total = jnp.sum(buf[...], axis=0)
+            rows = [total[at : at + 1, :] for at in range(ROUND_ROWS[idx])]
         pltpu.make_async_copy(others, others, r.sum_send.at[idx]).wait()
         result, at = [], 0
         for w in widths:
-            parts = [total[at + q : at + q + 1, :] for q in range(w // LANES)]
+            parts = rows[at : at + w // LANES]
             at += w // LANES
             result.append(jnp.concatenate(parts, axis=1) if len(parts) > 1 else parts[0])
         return result
 
     up_ok, down_ok = row > 0, row < nr - 1
-    from_above = jnp.where(row > 0, 1.0, 0.0)
-    from_below = jnp.where(row < nr - 1, 1.0, 0.0)
-
-    def halo(idx, up, src, dst):
-        shift = -1 if up else 1
+    halo_up = (False, False, True, False, True, False, True, True, True)
+
+    def halo(idx):
+        return pltpu.make_async_remote_copy(
+            src_ref=r.edge[idx],
+            dst_ref=r.halo[idx],
+            send_sem=r.halo_send.at[idx],
+            recv_sem=r.halo_recv.at[idx],
+            device_id=(row - 1 if halo_up[idx] else row + 1, col),
+            device_id_type=MESH,
+        )
+
+    def halo_put(idx, at, rows):
+        r.edge[idx][at] = rows.astype(BF16)
+
+    def halo_start(idx):
+        @pl.when(up_ok if halo_up[idx] else down_ok)
+        def _():
+            halo(idx).start()
+
+    def halo_wait(idx):
+        @pl.when(up_ok if halo_up[idx] else down_ok)
+        def _():
+            halo(idx).wait_send()
+
+        @pl.when(down_ok if halo_up[idx] else up_ok)
+        def _():
+            halo(idx).wait_recv()
+
+    def halo_row(idx, at, k):
+        return r.halo[idx][at, k].astype(F32)
+
+    def both_edges(idx, ref):
+        halo_put(idx, 0, ref[:, hh - 1])
+        halo_put(idx + 1, 0, ref[:, 0])
+
+    chips = nr * nxy
+    chip = row * nxy + xy
+
+    def chip_copy(src, dst, to, send_sem, recv_sem):
         return pltpu.make_async_remote_copy(
             src_ref=src,
             dst_ref=dst,
-            send_sem=r.halo_send.at[idx],
-            recv_sem=r.halo_recv.at[idx],
-            device_id=(row + shift, col),
+            send_sem=send_sem,
+            recv_sem=recv_sem,
+            device_id=(lax.div(to, nxy), lax.rem(to, nxy) * 2 + core),
             device_id_type=MESH,
         )
 
-    def halo_start(idx, up, src, dst):
-        @pl.when(up_ok if up else down_ok)
-        def _():
-            halo(idx, up, src, dst).start()
-
-    def halo_wait(idx, up, src, dst):
-        @pl.when(up_ok if up else down_ok)
-        def _():
-            halo(idx, up, src, dst).wait_send()
-
-        @pl.when(down_ok if up else up_ok)
-        def _():
-            halo(idx, up, src, dst).wait_recv()
+    def to_chips(copy_to):
+        def send(k, c):
+            copy_to(lax.rem(chip + k, chips)).start()
+            return c
+
+        lax.fori_loop(1, chips, send, 0)
+
+    def all_of(ref, n, sem):
+        pltpu.make_async_copy(ref.at[pl.ds(0, n)], ref.at[pl.ds(0, n)], sem).wait()
+
+    def skip_send(vectors):
+        for at, v in enumerate(lines(vectors)):
+            r.pair_rows[at // 4, at % 4 : at % 4 + 1, :] = v
+        pair_copy(12, r.pair_rows.at[1 - core], r.pair_came).start()
+
+    def skip_spread():
+        pair_copy(12, r.pair_rows.at[1 - core], r.pair_came).wait()
+        r.pair_chips[chip] = r.pair_rows[core] + r.pair_came[...]
+        mine = r.pair_chips.at[chip]
+        to_chips(lambda to: chip_copy(mine, mine, to, r.chip_send.at[0], r.chip_recv.at[0]))
+
+    def skip_return():
+        all_of(r.pair_chips, chips - 1, r.chip_recv.at[0])
+        all_of(r.pair_chips, chips - 1, r.chip_send.at[0])
+        r.pair_total[core] = jnp.sum(r.pair_chips[...], axis=0)
+        mine = r.pair_total.at[core]
+        pair_copy(13, mine, mine).start()
+
+    def skip_take():
+        mine = r.pair_total.at[core]
+        pair_copy(13, mine, mine).wait()
+        return [
+            jnp.concatenate([r.pair_total[i, q : q + 1, :] for q in range(4)], axis=1)
+            for i in range(2)
+        ]
 
     axes = (("core", 2), ("xy", nxy), ("rows", nr))
     seat = {"core": core, "xy": xy, "rows": row}
@@ -270,6 +360,35 @@
             lo = at + q * n
             r.part[g][0][lo : lo + n, :] = value[:, q * LANES : (q + 1) * LANES].astype(BF16)
 
+    def one_send(value):
+        r.one_both[...] = value.reshape(2, chips, -1, LANES)
+        pair_copy(14, r.one_both.at[1 - core], r.one_came).start()
+
+    def one_spread():
+        pair_copy(14, r.one_both.at[1 - core], r.one_came).wait()
+        r.one_half[...] = r.one_both[core] + r.one_came[...]
+        to_chips(
+            lambda to: chip_copy(
+                r.one_half.at[to], r.one_slots.at[chip], to, r.chip_send.at[1], r.chip_recv.at[1]
+            )
+        )
+
+    def one_gather():
+        all_of(r.one_slots, chips - 1, r.chip_recv.at[1])
+        r.one_slots[chip] = r.one_half[chip]
+        r.one_whole[core, chip] = jnp.sum(r.one_slots[...], axis=0)
+        mine = r.one_whole.at[core, chip]
+        to_chips(lambda to: chip_copy(mine, mine, to, r.chip_send.at[2], r.chip_recv.at[2]))
+
+    def one_return():
+        all_of(r.one_slots, chips - 1, r.chip_send.at[1])
+        all_of(r.one_slots, chips - 1, r.chip_recv.at[2])
+        all_of(r.one_slots, chips - 1, r.chip_send.at[2])
+        pair_copy(15, r.one_whole.at[core], r.one_whole.at[core]).start()
+
+    def one_take():
+        pair_copy(15, r.one_whole.at[core], r.one_whole.at[core]).wait()
+
     def coefficients(total, square, count, gain, bias):
         n = jnp.maximum(count, 1.0)
         mu = total / n
@@ -298,8 +417,8 @@
                     pltpu.make_async_remote_copy(
                         src_ref=src_of(p, lo, hi - lo),
                         dst_ref=dst_of(lo, hi - lo),
-                        send_sem=send.at[w, k],
-                        recv_sem=recv.at[w, k],
+                        send_sem=send,
+                        recv_sem=recv,
                         device_id=(p, col),
                         device_id_type=MESH,
                     )
@@ -307,19 +426,25 @@
         here = pltpu.make_async_copy(src_of(row, 0, hh), dst_of(0, hh), local)
         return pieces, here
 
-    def start_pieces(pieces, w):
-        for copy in pieces[w * (nr - 1) : (w + 1) * (nr - 1)]:
-            copy.start()
+    def wait_pieces(which):
+        bytes_of = r.out_rows.at[pl.ds(0, nk - own)]
+        pltpu.make_async_copy(bytes_of, bytes_of, r.row_recv.at[which]).wait()
+        pltpu.make_async_copy(bytes_of, bytes_of, r.row_send.at[which]).wait()
+
+    def start_pieces(pieces, *which):
+        for w in which:
+            for copy in pieces[w * (nr - 1) : (w + 1) * (nr - 1)]:
+                copy.start()
 
     cot_copies, cot_local = row_pieces(
         lambda p, lo, n: r.cot.at[:, pl.ds(p * hh + lo, n)],
         lambda lo, n: r.cot_rows.at[pl.ds(row * own, own), pl.ds(lo, n)],
-        r.cot_send, r.cot_recv, r.local_sem.at[0],
+        r.row_send.at[0], r.row_recv.at[0], r.local_sem.at[0],
     )
     out_copies, out_local = row_pieces(
         lambda p, lo, n: r.out_rows.at[pl.ds(p * own, own), pl.ds(lo, n)],
         lambda lo, n: r.out.at[:, pl.ds(row * hh + lo, n)],
-        r.out_send, r.out_recv, r.local_sem.at[1],
+        r.row_send.at[1], r.row_recv.at[1], r.local_sem.at[1],
     )
     cot_local.start()
 
@@ -327,6 +452,7 @@
     for slot in range(2 * hh):
         for q in range(lane_blocks):
             r.spread[q, slot, 2 * wv : 2 * PAD, :] = jnp.zeros((2 * PAD - 2 * wv, LANES), F32)
+    arrived("reduce_one")
     w1 = r.reduce_one[...]
     acc = zero8(LANES, 2)
     for copy in image_copies:
@@ -353,17 +479,10 @@
                 s2 += m * folded(z * z)
         return s1, s2
 
-    acc = lax.fori_loop(0, nk // 2, first, acc)
-    pl.semaphore_wait(barrier, ndev - 1)
-    start_pieces(cot_copies, 0)
-    s1, s2 = lax.fori_loop(nk // 2, nk, first, acc)
+    s1, s2 = loop(first, acc)
     count_one = sum(r.mask_one[k] for k in range(nk))
     count_two = sum(r.mask_two[k] for k in range(nk))
-    send_sums(0, [row_sum(s1), row_sum(s2), count_one, count_two])
-    halo_z1 = (0, False, r.z1.at[1, :, :, hh - 1], r.h1)
-    halo_start(*halo_z1)
-    start_pieces(cot_copies, 1)
-
+    arrived("shortcut")
     sc = r.shortcut[...]
 
     def skip(k, acc):
@@ -372,13 +491,20 @@
         return acc[0] + folded(z), acc[1] + folded(z * z)
 
     zs1, zs2 = loop(skip, zero8(cfg.c_out, 2))
-
+    for pc in range(2):
+        halo_put(0, pc, r.z1[1, pc, :, hh - 1])
+    pl.semaphore_wait(barrier, ndev - 1)
+    send_sums(0, [row_sum(s1), row_sum(s2), count_one, count_two])
+    halo_start(0)
+    skip_send([row_sum(zs1), row_sum(zs2)])
+    start_pieces(cot_copies, 0)
+    arrived("mid_gain", "mid_bias", "spatial_one")
     t1, t2, active_one, active_two = take_sums(0, [LANES] * 4)
     half_px, full_px = float(hh * wv), float(4 * hh * wv)
     active_gate = active_two[:, 0:1]
     g1, b1 = r.mid_gain[0:1, :], r.mid_bias[0:1, :]
     n1 = coefficients(t1, t2, active_one * full_px, g1, b1)
-    halo_wait(*halo_z1)
+    halo_wait(0)
 
     def shifted_right(a):
         return pltpu.roll(a, 1, axis=a.ndim - 2)
@@ -406,7 +532,7 @@
                     dst[k, rows, :, 2 * LANES : 3 * LANES] = a.astype(BF16)
                     dst[k, rows, :, 0:LANES] = shifted_right(a).astype(BF16)
         for pc in range(2):
-            a, _ = half_silu(r.h1[pc, k] * ah + bh)
+            a, _ = half_silu(halo_row(0, pc, k) * ah + bh)
             a = jnp.where(row > 0, a, 0.0)
             if pc == 0:
                 r.odd[k, 0, :, LANES : 2 * LANES] = a.astype(BF16)
@@ -422,9 +548,24 @@
 
     s1, s2 = loop(second, zero8(LANES, 2))
     send_sums(1, [row_sum(s1), row_sum(s2)])
-    halo_z2 = (1, True, r.z2.at[:, 0], r.h2)
-    halo_start(*halo_z2)
-    start_pieces(cot_copies, 2)
+    skip_spread()
+    start_pieces(cot_copies, 1)
+
+    def early(k, c):
+        m = r.mask_one[k]
+        for pr in range(2):
+            for pc in range(2):
+                zhat = (r.z1[pr, pc, k] - n1.mu) * (m * n1.inv)
+                r.dz1[pr, pc, k] = zhat.astype(BF16)
+        r.dz4[k] = jnp.broadcast_to(m, (hh, PAD, LANES)).astype(BF16)
+        return c
+
+    loop(early)
+    for name in ("expand_one", "wide_gain", "wide_bias", "reduce_two"):
+        arrived(name)
+    planes = [(pr, pc) for pr in range(2) for pc in range(2)]
+    r.part_z[...] = sum(dot_tn(flat2(r.x[q]), flat2(r.dz1[q])) for q in planes)
+    r.part_m[...] = sum(dot_tn(flat2(r.x[q]), flat2(r.dz4[...])) for q in planes)
     t1, t2 = take_sums(1, [LANES] * 2)
     n2 = coefficients(t1, t2, active_one * half_px, r.mid_gain[1:2, :], r.mid_bias[1:2, :])
     e1 = r.expand_one[...]
@@ -440,9 +581,27 @@
         return acc[0] + folded(z), acc[1] + folded(z * z)
 
     s1, s2 = loop(third, zero8(cfg.c_out, 2))
-    send_sums(2, [row_sum(s1), row_sum(s2), row_sum(zs1), row_sum(zs2)])
-    start_pieces(cot_copies, 3)
-    t1, t2, ts1, ts2 = take_sums(2, [cfg.c_out] * 4)
+    send_sums(2, [row_sum(s1), row_sum(s2)])
+    start_pieces(cot_copies, 2, 3)
+    arrived("spatial_two", "expand_two")
+    def tap(ref, i, j):
+        return ref[i, j * LANES : (j + 1) * LANES, :].T
+
+    for i in range(3):
+        for j in range(3):
+            r.back_two[i, j * LANES : (j + 1) * LANES, :] = tap(r.spatial_two, 2 - i, 2 - j)
+    zeros = jnp.zeros((LANES, LANES), BF16)
+    k1 = r.spatial_one
+    here = [[tap(k1, 2, 2), tap(k1, 1, 2), tap(k1, 2, 1), tap(k1, 1, 1)],
+            [tap(k1, 2, 0), tap(k1, 1, 0), zeros, zeros]]
+    below = [[tap(k1, 0, 2), tap(k1, 0, 1)], [tap(k1, 0, 0), zeros]]
+    for ref, blocks in ((r.back_here, here), (r.back_below, below)):
+        for i, line in enumerate(blocks):
+            for j, block in enumerate(line):
+                ref[i * LANES : (i + 1) * LANES, j * LANES : (j + 1) * LANES] = block
+    skip_return()
+    t1, t2 = take_sums(2, [cfg.c_out] * 2)
+    ts1, ts2 = skip_take()
     all_px = float(nk * nc) * float(nr) * half_px
     n3 = coefficients(t1, t2, all_px, r.wide_gain[0:1, :], r.wide_bias[0:1, :])
     ns = coefficients(ts1, ts2, all_px, r.wide_gain[1:2, :], r.wide_bias[1:2, :])
@@ -462,17 +621,14 @@
 
     s1, s2 = loop(fourth, zero8(LANES, 2))
     send_sums(3, [row_sum(s1), row_sum(s2)])
-    halos_z4 = [
-        (2, False, r.z4.at[:, hh - 1], r.h4.at[0]),
-        (3, True, r.z4.at[:, 0], r.h4.at[1]),
-    ]
-    for h in halos_z4:
-        halo_start(*h)
+    both_edges(1, r.z4)
+    halo_start(1)
+    halo_start(2)
     start_pieces(cot_copies, 4)
     t1, t2 = take_sums(3, [LANES] * 2)
     n4 = coefficients(t1, t2, active_two * half_px, r.mid_gain[2:3, :], r.mid_bias[2:3, :])
-    for h in halos_z4:
-        halo_wait(*h)
+    halo_wait(1)
+    halo_wait(2)
 
     def put3(dst, k, rows, a):
         dst[k, rows, :, LANES : 2 * LANES] = a.astype(BF16)
@@ -487,9 +643,9 @@
         a, s = half_silu(r.z4[k] * ah + bh, half_mask)
         r.s4[k] = s
         put3(r.a4, k, pl.ds(1, hh), a)
-        a, _ = half_silu(r.h4[0, k] * ah + bh)
+        a, _ = half_silu(halo_row(1, 0, k) * ah + bh)
         put3(r.a4, k, 0, jnp.where(row > 0, a, 0.0))
-        a, _ = half_silu(r.h4[1, k] * ah + bh)
+        a, _ = half_silu(halo_row(2, 0, k) * ah + bh)
         put3(r.a4, k, hh + 1, jnp.where(row < nr - 1, a, 0.0))
         z = sum(dot(flat2(r.a4[k, i : i + hh]), k_two[i]) for i in range(3))
         z = z.reshape(hh, PAD, LANES) * col_mask
@@ -498,13 +654,7 @@
 
     s1, s2 = loop(fifth, zero8(LANES, 2))
     send_sums(4, [row_sum(s1), row_sum(s2)])
-    halos_z5 = [
-        (4, False, r.z5.at[:, hh - 1], r.h5.at[0]),
-        (5, True, r.z5.at[:, 0], r.h5.at[1]),
-    ]
-    for h in halos_z5:
-        halo_start(*h)
-    start_pieces(cot_copies, 5)
+    start_pieces(cot_copies, 5, 6)
     t1, t2 = take_sums(4, [LANES] * 2)
     n5 = coefficients(t1, t2, active_two * half_px, r.mid_gain[3:4, :], r.mid_bias[3:4, :])
     e2 = r.expand_two[...]
@@ -522,8 +672,10 @@
 
     s1, s2 = loop(sixth, zero8(cfg.c_out, 2))
     send_sums(5, [row_sum(s1), row_sum(s2)])
-    for copy in cot_copies:
-        copy.wait()
+    both_edges(3, r.z5)
+    halo_start(3)
+    halo_start(4)
+    wait_pieces(0)
     cot_local.wait()
     t1, t2 = take_sums(5, [cfg.c_out] * 2)
     gate_count = active_gate * half_px
@@ -551,7 +703,7 @@
     d1, d2 = loop(seventh, zero8(cfg.c_out, 2))
     send_sums(6, [row_sum(d1), row_sum(d2)])
 
-    start_pieces(out_copies, 0)
+    start_pieces(out_copies, 0, 1)
     out_local.start()
     db6, q6 = take_sums(6, [cfg.c_out] * 2)
     dg6, (c1, c2, c3) = backward(n6, db6, q6)
@@ -568,28 +720,26 @@
 
     d1, d2 = loop(eighth, zero8(LANES, 2))
     send_sums(7, [row_sum(d1), row_sum(d2)])
-    halos_q5 = [
-        (6, False, r.q5.at[:, hh - 1], r.hq5.at[0]),
-        (7, True, r.q5.at[:, 0], r.hq5.at[1]),
-    ]
-    for h in halos_q5:
-        halo_start(*h)
-    start_pieces(out_copies, 1)
+    both_edges(5, r.q5)
+    halo_start(5)
+    halo_start(6)
+    start_pieces(out_copies, 2)
     stage(0, "expand_two", dot_tn(flat2(r.a5[...]), flat2(r.dz6[...])))
-    for h in halos_z5:
-        halo_wait(*h)
+    advance(0, 0)
+    halo_wait(3)
+    halo_wait(4)
     db5, q5 = take_sums(7, [LANES] * 2)
     dg5, (c1, c2, c3) = backward(n5, db5, q5)
-    for h in halos_q5:
-        halo_wait(*h)
+    halo_wait(5)
+    halo_wait(6)
 
     def ninth(k, acc, c1=c1, c2=c2, c3=c3):
         m = r.mask_two[k]
         f1, f2, f3 = m * c1, m * c2, (m * c3) * col_mask
         put3(r.dz5, k, pl.ds(1, hh), r.q5[k] * f1 + r.z5[k] * f2 + f3)
-        d = r.hq5[0, k] * f1 + r.h5[0, k] * f2 + f3
+        d = halo_row(5, 0, k) * f1 + halo_row(3, 0, k) * f2 + f3
         put3(r.dz5, k, 0, jnp.where(row > 0, d, 0.0))
-        d = r.hq5[1, k] * f1 + r.h5[1, k] * f2 + f3
+        d = halo_row(6, 0, k) * f1 + halo_row(4, 0, k) * f2 + f3
         put3(r.dz5, k, hh + 1, jnp.where(row < nr - 1, d, 0.0))
         q = sum(dot(flat2(r.dz5[k, i : i + hh]), r.back_two[i]) for i in range(3))
         q = q.reshape(hh, PAD, LANES) * r.s4[k]
@@ -598,14 +748,17 @@
 
     d1, d2 = loop(ninth, zero8(LANES, 2))
     send_sums(8, [row_sum(d1), row_sum(d2)])
-    start_pieces(out_copies, 2)
+    start_pieces(out_copies, 3)
     d5 = flat2(r.dz5[:, 1 : hh + 1, :, LANES : 2 * LANES])
     stage(
-        0,
+        1,
         "spatial_two",
         jnp.concatenate([dot_tn(flat2(r.a4[:, i : i + hh]), d5) for i in range(3)], axis=0),
     )
-    advance(0, 0)
+    halo_put(8, 0, r.z2[:, 0])
+    halo_start(8)
+    advance(0, 1)
+    advance(1, 0)
     db4, q4 = take_sums(8, [LANES] * 2)
     dg4, (c1, c2, c3) = backward(n4, db4, q4)
 
@@ -626,9 +779,11 @@
 
     d1, d2, d3 = loop(tenth, zero8(cfg.c_out, 3))
     send_sums(9, [row_sum(d1), row_sum(d2), row_sum(d3)])
-    start_pieces(out_copies, 3)
-    stage(1, "reduce_two", dot_tn(flat2(r.hidden[...]), flat2(r.dz4[...])))
-    advance(0, 1)
+    start_pieces(out_copies, 4)
+    stage(2, "reduce_two", dot_tn(flat2(r.hidden[...]), flat2(r.dz4[...])))
+    advance(1, 1)
+    advance(0, 2)
+    advance(2, 0)
     db3, q3, qs = take_sums(9, [cfg.c_out] * 3)
     dg3, (c1, c2, c3) = backward(n3, db3, q3)
     dgs, (p1, p2, p3) = backward(ns, db3, qs)
@@ -646,61 +801,83 @@
 
     d1, d2 = loop(eleventh, zero8(LANES, 2))
     send_sums(10, [row_sum(d1), row_sum(d2)])
-    halo_q2 = (8, True, r.q2.at[:, 0], r.hq2)
-    halo_start(*halo_q2)
-    start_pieces(out_copies, 4)
-    stage(1, "expand_one", dot_tn(flat2(r.a2[...]), flat2(r.dz3[...])))
-    stage(1, "shortcut", dot_tn(flat2(r.x[0, 0]), flat2(r.dzs[...])))
-    advance(1, 0)
-    advance(0, 2)
-    halo_wait(*halo_z2)
+    halo_put(7, 0, r.q2[:, 0])
+    halo_start(7)
+    stage(3, "expand_one", dot_tn(flat2(r.a2[...]), flat2(r.dz3[...])))
+    stage(3, "shortcut", dot_tn(flat2(r.x[0, 0]), flat2(r.dzs[...])))
+    advance(3, 0)
+    advance(1, 2)
+    advance(2, 1)
+    start_pieces(out_copies, 5)
+    halo_wait(8)
     db2, q2 = take_sums(10, [LANES] * 2)
     dg2, (c1, c2, c3) = backward(n2, db2, q2)
-    halo_wait(*halo_q2)
-
-    def twelfth(k, acc, c1=c1, c2=c2, c3=c3):
+    halo_wait(7)
+    advance(3, 1)
+
+    def twelfth(k, c, c1=c1, c2=c2, c3=c3):
         m = r.mask_one[k]
         f1, f2, f3 = m * c1, m * c2, (m * c3) * col_mask
         d = r.q2[k] * f1 + r.z2[k] * f2 + f3
         r.dz2[k, 0:hh, :, 0:LANES] = d.astype(BF16)
         r.dz2[k, 0:hh, :, LANES : 2 * LANES] = shifted_left(d).astype(BF16)
-        d = jnp.where(row < nr - 1, r.hq2[k] * f1 + r.h2[k] * f2 + f3, 0.0)
+        d = jnp.where(row < nr - 1, halo_row(7, 0, k) * f1 + halo_row(8, 0, k) * f2 + f3, 0.0)
         r.dz2[k, hh, :, 0:LANES] = d.astype(BF16)
         r.dz2[k, hh, :, LANES : 2 * LANES] = shifted_left(d).astype(BF16)
+        return c
+
+    loop(twelfth)
+    d2_ = flat2(r.dz2[:, 0:hh, :, 0:LANES])
+    inputs = [r.odd[:, 0:hh], r.even[...], r.odd[:, 1 : hh + 1]]
+    stage(4, "spatial_one", jnp.concatenate([dot_tn(flat2(a), d2_) for a in inputs], axis=0))
+    advance(4, 0)
+
+    def thirteenth(k, acc):
+        m = r.mask_one[k]
         u = dot(flat2(r.dz2[k, 0:hh]), r.back_here[...])
         v = dot(flat2(r.dz2[k, 1 : hh + 1]), r.back_below[...])
         s1, s2 = acc
-        planes = (
+        parts = (
             (1, 1, u[:, 0:LANES] + v[:, 0:LANES]),
             (0, 1, u[:, LANES : 2 * LANES]),
             (1, 0, u[:, 2 * LANES : 3 * LANES] + v[:, LANES : 2 * LANES]),
             (0, 0, u[:, 3 * LANES : 4 * LANES]),
         )
-        for pr, pc, q in planes:
+        for pr, pc, q in parts:
             q = q.reshape(hh, PAD, LANES) * r.s1[pr, pc, k]
             r.q1[pr, pc, k] = q
+            r.dz1[pr, pc, k] = (m * q).astype(BF16)
             s1 += m * folded(q)
             s2 += m * folded(q * r.z1[pr, pc, k])
         return s1, s2
 
-    d1, d2 = loop(twelfth, zero8(LANES, 2))
+    d1, d2 = loop(thirteenth, zero8(LANES, 2))
     send_sums(11, [row_sum(d1), row_sum(d2)])
-    start_pieces(out_copies, 5)
-    d2_ = flat2(r.dz2[:, 0:hh, :, 0:LANES])
-    lines = [r.odd[:, 0:hh], r.even[...], r.odd[:, 1 : hh + 1]]
-    stage(
-        2, "spatial_one", jnp.concatenate([dot_tn(flat2(a), d2_) for a in lines], axis=0)
-    )
-    advance(1, 1)
+    advance(4, 1)
     advance(0, 3)
+    start_pieces(out_copies, 6)
+    part_q = sum(dot_tn(flat2(r.x[q]), flat2(r.dz1[q])) for q in planes)
+    advance(1, 3)
+    advance(2, 2)
 
     def skip_back(k, c):
         r.skip_back[k] = dot_nt(flat2(r.dzs[k]), sc).reshape(hh, PAD, cfg.c_in)
         return c
 
     loop(skip_back)
+    advance(3, 2)
     db1, q1 = take_sums(11, [LANES] * 2)
     dg1, (c1, c2, c3) = backward(n1, db1, q1)
+
+    total = n1.scale * part_q
+    total += (c2 / n1.inv) * r.part_z[...] + (c3 + c2 * n1.mu) * r.part_m[...]
+    one_send(total)
+    advance(4, 2)
+    one_spread()
+    advance(3, 3)
+    advance(1, 4)
+    advance(2, 3)
+    advance(0, 4)
 
     def last(k, acc, c1=c1, c2=c2, c3=c3):
         m = r.mask_one[k]
@@ -712,13 +889,6 @@
         return acc
 
     loop(last)
-    total = sum(
-        dot_tn(flat2(r.x[pr, pc]), flat2(r.dz1[pr, pc])) for pr in range(2) for pc in range(2)
-    )
-    stage(2, "reduce_one", total)
-    advance(2, 0)
-    advance(1, 2)
-    advance(0, 4)
 
     def images_back(k, c):
         for pr in range(2):
@@ -742,28 +912,50 @@
     back_copy.start()
 
     for k, v in enumerate((dg1, dg2, dg4, dg5, db1, db2, db4, db5)):
-        r.mid_grads[k : k + 1, :] = v
+        r.mid_held[k : k + 1, :] = v
     for k, v in enumerate((dg3, dgs, dg6, db3, db3, db6)):
-        r.wide_grads[k : k + 1, :] = v
-
-    for phase in range(1, 7):
-        advance(2, phase)
-        if phase + 2 <= 6:
-            advance(1, phase + 2)
-        if phase + 4 <= 6:
-            advance(0, phase + 4)
-    result_copies = [
-        pltpu.make_async_copy(r.full[g], result, r.full_sem.at[g])
-        for g, result in enumerate((r.summed0, r.summed1, r.summed2))
-    ]
-    for copy in result_copies:
+        r.wide_held[k : k + 1, :] = v
+    results = []
+
+    def give(src, dst):
+        copy = pltpu.make_async_copy(src, dst, r.full_sem.at[len(results)])
         copy.start()
-    for copy in result_copies:
-        copy.wait()
-    for copy in out_copies:
-        copy.wait()
+        results.append(copy)
+
+    give(r.mid_held, r.mid_grads)
+    give(r.wide_held, r.wide_grads)
+
+    def result(g):
+        give(r.full[g], r.summed[g])
+
+    advance(4, 3)
+    one_gather()
+    advance(3, 4)
+    advance(1, 5)
+    advance(2, 4)
+    advance(0, 5)
+    advance(4, 4)
+    one_return()
+    advance(3, 5)
+    advance(1, 6)
+    result(1)
+    advance(2, 5)
+    advance(0, 6)
+    result(0)
+    advance(4, 5)
+    advance(3, 6)
+    result(3)
+    advance(2, 6)
+    result(2)
+    one_take()
+    give(r.one_whole, r.summed_one)
+    advance(4, 6)
+    result(4)
+    wait_pieces(1)
     out_local.wait()
     back_copy.wait()
+    for copy in results:
+        copy.wait()
 
 
 def on_device(nr, nc, *args):
@@ -772,105 +964,110 @@
     nk, full_rows, full_cols, c_in = images.shape
     hh, wv, c_out = full_rows // 2, full_cols // 2, expand_one.shape[1]
     own = cot.shape[0]
-    ndev, nxy = nr * nc, nc // 2
+    ndev, nxy, groups = nr * nc, nc // 2, len(GROUPS)
     sizes = [group_rows(g, ndev) for g in GROUPS]
-
-    vmem, smem, hbm = pltpu.VMEM, pltpu.SMEM, pl.ANY
-    ins = [
-        ("images", images, hbm), ("cot", cot, hbm),
-        ("reduce_one", reduce_one, vmem), ("spatial_one", spatial_one.reshape(3, 3 * LANES, LANES), vmem),
-        ("expand_one", expand_one, vmem), ("shortcut", shortcut, vmem), ("reduce_two", reduce_two, vmem),
-        ("spatial_two", spatial_two.reshape(3, 3 * LANES, LANES), vmem), ("expand_two", expand_two, vmem),
-        ("mid_gain", mid_gain, vmem), ("mid_bias", mid_bias, vmem),
-        ("wide_gain", wide_gain, vmem), ("wide_bias", wide_bias, vmem),
-        ("widths", widths.T, smem), ("depth_gate", depth_gate, smem),
-    ]
-    outs = [
-        ("out", cot.shape, BF16, hbm),
-        ("images_grad", images.shape, BF16, hbm),
-        ("summed0", (sizes[0], LANES), BF16, hbm),
-        ("summed1", (sizes[1], LANES), BF16, hbm),
-        ("summed2", (sizes[2], LANES), BF16, hbm),
-        ("mid_grads", (8, LANES), F32, vmem), ("wide_grads", (6, c_out), F32, vmem),
-    ]
+    chunk = (ndev // 2, c_in // ndev, LANES)
     half, quad = (nk, hh, PAD), (2, 2, nk, hh, PAD)
-    dma = pltpu.SemaphoreType.DMA
-    scratch = [
-        ("x_in", vmem(images.shape, BF16)),
-        ("spread", vmem((c_in // LANES, 2 * hh, 2 * PAD, LANES), F32)),
-        ("x", vmem(quad + (c_in,), BF16)),
-        ("z1", vmem(quad + (LANES,), F32)),
-        ("s1", vmem(quad + (LANES,), F32)),
-        ("q1", vmem(quad + (LANES,), F32)),
-        ("dz1", vmem(quad + (LANES,), BF16)),
-        ("h1", vmem((2, nk, PAD, LANES), F32)),
-        ("even", vmem(half + (3 * LANES,), BF16)),
-        ("odd", vmem((nk, hh + 1, PAD, 3 * LANES), BF16)),
-        ("dz2", vmem((nk, hh + 1, PAD, 2 * LANES), BF16)),
-        ("a4", vmem((nk, hh + 2, PAD, 3 * LANES), BF16)),
-        ("dz5", vmem((nk, hh + 2, PAD, 3 * LANES), BF16)),
-        ("h2", vmem((nk, PAD, LANES), F32)),
-        ("hq2", vmem((nk, PAD, LANES), F32)),
-        ("h4", vmem((2, nk, PAD, LANES), F32)),
-        ("h5", vmem((2, nk, PAD, LANES), F32)),
-        ("hq5", vmem((2, nk, PAD, LANES), F32)),
-        ("cot_rows", vmem((nk, hh, wv, c_out), BF16)),
-        ("out_rows", vmem((nk, hh, wv, c_out), BF16)),
-        ("skip_back", vmem(half + (c_in,), F32)),
-        ("back_two", vmem((3, 3 * LANES, LANES), BF16)),
-        ("back_here", vmem((2 * LANES, 4 * LANES), BF16)),
-        ("back_below", vmem((2 * LANES, 2 * LANES), BF16)),
-        ("mask_one", vmem((nk, 1, LANES), F32)),
-        ("mask_two", vmem((nk, 1, LANES), F32)),
-        ("gates", vmem((nk, 1, c_out), F32)),
-    ]
-    scratch += [(n, vmem(half + (LANES,), F32)) for n in ("z2", "s2", "q2", "z4", "s4", "q4", "z5", "s5", "q5")]
-    scratch += [(n, vmem(half + (c_out,), F32)) for n in ("z3", "zs", "s3", "q3", "z6", "live")]
-    scratch += [(n, vmem(half + (LANES,), BF16)) for n in ("a2", "a5", "dz4")]
-    scratch += [(n, vmem(half + (c_out,), BF16)) for n in ("hidden", "dz6", "dz3", "dzs")]
-    scratch += [
-        ("image_sem", dma((nk,))), ("local_sem", dma((3,))),
-        ("sum_send", dma((len(ROUND_ROWS),))), ("sum_recv", dma((len(ROUND_ROWS),))),
-        ("halo_send", dma((9,))), ("halo_recv", dma((9,))),
-        ("cot_send", dma((6, nr))), ("cot_recv", dma((6, nr))),
-        ("out_send", dma((6, nr))), ("out_recv", dma((6, nr))),
-        ("full_sem", dma((len(GROUPS),))),
-        ("grad_send", dma((len(GROUPS), 6))), ("grad_recv", dma((len(GROUPS), 6))),
-    ]
-    scratch += [(f"sums{i}", vmem((ndev, n, LANES), F32)) for i, n in enumerate(ROUND_ROWS)]
-    for g, size in enumerate(sizes):
-        levels = (size, size // 2, size // nc, size // ndev)
-        for level, n in enumerate((2, nxy, nr)):
-            scratch.append((f"part{g}_{level}", vmem((levels[level], LANES), BF16)))
-            scratch.append((f"came{g}_{level}", vmem((n - 1, levels[level + 1], LANES), BF16)))
-        scratch.append((f"full{g}", vmem((size, LANES), BF16)))
+
+    def f32(*shape):
+        return pltpu.VMEM(shape, F32)
+
+    def bf16(*shape):
+        return pltpu.VMEM(shape, BF16)
+
+    def dma(*shape):
+        return pltpu.SemaphoreType.DMA(shape)
+
+    def mid():
+        return f32(*half, LANES)
+
+    def wide():
+        return f32(*half, c_out)
+
+    def low(width):
+        return bf16(*half, width)
+
+    weights = dict(
+        reduce_one=reduce_one, shortcut=shortcut, mid_gain=mid_gain, mid_bias=mid_bias,
+        spatial_one=spatial_one.reshape(3, 3 * LANES, LANES), expand_one=expand_one,
+        wide_gain=wide_gain, wide_bias=wide_bias, reduce_two=reduce_two,
+        spatial_two=spatial_two.reshape(3, 3 * LANES, LANES), expand_two=expand_two,
+    )
+    scalars = dict(widths=widths.T, depth_gate=depth_gate)
+    ins = dict(images=images, cot=cot, weights=weights)
+    outs = dict(
+        out=jax.ShapeDtypeStruct(cot.shape, BF16),
+        images_grad=jax.ShapeDtypeStruct(images.shape, BF16),
+        summed=[jax.ShapeDtypeStruct((size, LANES), BF16) for size in sizes],
+        summed_one=jax.ShapeDtypeStruct((2,) + chunk, F32),
+        mid_grads=jax.ShapeDtypeStruct((8, LANES), F32),
+        wide_grads=jax.ShapeDtypeStruct((6, c_out), F32),
+    )
+    edges = [bf16(2 if i == 0 else 1, nk, PAD, LANES) for i in range(9)]
+    levels = [(n, n // 2, n // nc, n // ndev) for n in sizes]
+    halves = {i: ROUND_ROWS[i] // 2 for i in WIDE}
+    scratch = dict(
+        held={name: pltpu.VMEM(a.shape, a.dtype) for name, a in weights.items()},
+        x_in=bf16(*images.shape), spread=f32(c_in // LANES, 2 * hh, 2 * PAD, LANES), x=bf16(*quad, c_in),
+        z1=f32(*quad, LANES), s1=f32(*quad, LANES), q1=f32(*quad, LANES), dz1=bf16(*quad, LANES),
+        part_z=f32(c_in, LANES), part_m=f32(c_in, LANES),
+        one_both=f32(2, *chunk), one_came=f32(*chunk), one_half=f32(*chunk), one_slots=f32(*chunk),
+        one_whole=f32(2, *chunk), mid_held=f32(8, LANES), wide_held=f32(6, c_out),
+        pair_rows=f32(2, 4, LANES), pair_came=f32(4, LANES), pair_chips=f32(ndev // 2, 4, LANES),
+        pair_total=f32(2, 4, LANES),
+        even=low(3 * LANES), odd=bf16(nk, hh + 1, PAD, 3 * LANES), dz2=bf16(nk, hh + 1, PAD, 2 * LANES),
+        a4=bf16(nk, hh + 2, PAD, 3 * LANES), dz5=bf16(nk, hh + 2, PAD, 3 * LANES),
+        cot_rows=bf16(nk, hh, wv, c_out), out_rows=bf16(nk, hh, wv, c_out), skip_back=f32(*half, c_in),
+        back_two=bf16(3, 3 * LANES, LANES), back_here=bf16(2 * LANES, 4 * LANES),
+        back_below=bf16(2 * LANES, 2 * LANES),
+        mask_one=f32(nk, 1, LANES), mask_two=f32(nk, 1, LANES), gates=f32(nk, 1, c_out),
+        z2=mid(), s2=mid(), q2=mid(), z4=mid(), s4=mid(), q4=mid(), z5=mid(), s5=mid(), q5=mid(),
+        z3=wide(), zs=wide(), s3=wide(), q3=wide(), z6=wide(), live=wide(),
+        a2=low(LANES), a5=low(LANES), dz4=low(LANES),
+        hidden=low(c_out), dz6=low(c_out), dz3=low(c_out), dzs=low(c_out),
+        edge=edges, halo=edges,
+        sums=[f32(ndev, halves.get(i, n), LANES) for i, n in enumerate(ROUND_ROWS)],
+        both={i: f32(2, n, LANES) for i, n in halves.items()},
+        from_pair={i: f32(n, LANES) for i, n in halves.items()},
+        part=[[bf16(n[i], LANES) for i in range(3)] for n in levels],
+        came=[[bf16(m - 1, n[i + 1], LANES) for i, m in enumerate((2, nxy, nr))] for n in levels],
+        full=[bf16(n, LANES) for n in sizes],
+        image_sem=dma(nk), local_sem=dma(3), full_sem=dma(groups + 3), weight_sem=dma(len(weights)),
+        sum_send=dma(len(ROUND_ROWS)), sum_recv=dma(len(ROUND_ROWS)), halo_send=dma(9), halo_recv=dma(9),
+        row_send=dma(2), row_recv=dma(2), pair_send=dma(16), pair_recv=dma(16), chip_send=dma(3),
+        chip_recv=dma(3), grad_send=dma(groups, 6), grad_recv=dma(groups, 6),
+    )
     cfg = SimpleNamespace(
         nr=nr, nc=nc, nk=nk, hh=hh, wv=wv, c_in=c_in, c_out=c_out, group_size=sizes,
-        pieces=[(i * hh // 6, (i + 1) * hh // 6) for i in range(6)],
-        names=[n for n, *_ in ins] + [n for n, *_ in outs] + [n for n, _ in scratch],
+        pieces=split(hh, 7), order=list(weights),
     )
+    flat, trees = [], []
+    for part in (scalars, ins, outs, scratch):
+        leaves, tree = jax.tree.flatten(part)
+        flat.append(leaves)
+        trees.append(tree)
 
     def body(*refs):
-        named = dict(zip(cfg.names, refs))
-        named["sums"] = [named[f"sums{i}"] for i in range(len(ROUND_ROWS))]
-        named["part"] = [[named[f"part{g}_{j}"] for j in range(3)] for g in range(len(GROUPS))]
-        named["came"] = [[named[f"came{g}_{j}"] for j in range(3)] for g in range(len(GROUPS))]
-        named["full"] = [named[f"full{g}"] for g in range(len(GROUPS))]
-        inner = SimpleNamespace(**vars(cfg))
-        inner.names = list(named)
-        mega(inner, *named.values())
-
+        named, at = {}, 0
+        for leaves, tree in zip(flat, trees):
+            named.update(jax.tree.unflatten(tree, refs[at : at + len(leaves)]))
+            at += len(leaves)
+        mega(cfg, SimpleNamespace(**named, **named["held"]))
+
+    smem, hbm = pl.BlockSpec(memory_space=pltpu.SMEM), pl.BlockSpec(memory_space=pl.ANY)
     result = pl.pallas_call(
         body,
-        out_shape=[jax.ShapeDtypeStruct(s, t) for _, s, t, _ in outs],
-        in_specs=[pl.BlockSpec(memory_space=m) for _, _, m in ins],
-        out_specs=[pl.BlockSpec(memory_space=m) for _, _, _, m in outs],
-        scratch_shapes=[s for _, s in scratch],
+        out_shape=flat[2],
+        in_specs=[smem] * len(flat[0]) + [hbm] * len(flat[1]),
+        out_specs=[hbm] * len(flat[2]),
+        scratch_shapes=flat[3],
         compiler_params=pltpu.CompilerParams(
             collective_id=0, has_side_effects=True, vmem_limit_bytes=60 << 20
         ),
-    )(*[a for _, a, _ in ins])
-    return finished(result, mid_gain.shape, wide_gain.shape)
+    )(*flat[0], *flat[1])
+    made = SimpleNamespace(**jax.tree.unflatten(trees[2], result))
+    parts = [made.out, made.images_grad, *made.summed, made.summed_one, made.mid_grads, made.wide_grads]
+    return finished(parts, mid_gain.shape, wide_gain.shape)
 
 
 WEIGHTS = (
@@ -885,17 +1082,18 @@
 
 
 def finish(*refs):
-    ins, outs, held = refs[:7], refs[7:20], refs[20:27]
-    wide_to, (in_sem, out_sem) = refs[27:38], refs[38:]
+    n = len(GROUPS) + 5
+    ins, outs, held = refs[:n], refs[n : n + 13], refs[n + 13 : 2 * n + 13]
+    wide_to, (in_sem, out_sem) = refs[2 * n + 13 : 2 * n + 24], refs[2 * n + 24 :]
     chunks = [(0, i) for i in range(4)] + [(1, i) for i in range(4)]
 
     def part(ref, which, i):
-        n = ref.shape[1 - which] // 4
-        return ref.at[:, pl.ds(i * n, n)] if which == 0 else ref.at[pl.ds(i * n, n)]
-
-    small = [pltpu.make_async_copy(ins[i], held[i], in_sem.at[i]) for i in (5, 6, 2, 3, 4)]
+        size = ref.shape[1 - which] // 4
+        return ref.at[:, pl.ds(i * size, size)] if which == 0 else ref.at[pl.ds(i * size, size)]
+
+    small = [pltpu.make_async_copy(ins[i], held[i], in_sem.at[i]) for i in (n - 2, n - 1, *range(2, n - 2))]
     large = [
-        pltpu.make_async_copy(part(ins[w], w, i), part(held[w], w, i), in_sem.at[7 + 4 * w + i])
+        pltpu.make_async_copy(part(ins[w], w, i), part(held[w], w, i), in_sem.at[n + 4 * w + i])
         for w, i in chunks
     ]
     for copy in small + large:
@@ -909,7 +1107,7 @@
 
     for i in range(2):
         small[i].wait()
-    mid, wide = held[5], held[6]
+    mid, wide = held[n - 2], held[n - 1]
     grads = (mid[0:4, :], mid[4:8, :], wide[0:3, :], wide[3:6, :])
     for ref, value, to in zip(wide_to[7:], grads, outs[9:]):
         ref[...] = value
@@ -927,12 +1125,15 @@
                     lo = at + i * LANES
                     ref[i // 3, i % 3] = summed[lo : lo + LANES, :].astype(F32)
             else:
-                n = ref.shape[0]
+                height = ref.shape[0]
                 for q in range(ref.shape[1] // LANES):
-                    lo = at + q * n
-                    ref[:, q * LANES : (q + 1) * LANES] = summed[lo : lo + n, :].astype(F32)
+                    lo = at + q * height
+                    ref[:, q * LANES : (q + 1) * LANES] = summed[lo : lo + height, :].astype(F32)
             leave(ref, outs[2 + which])
             at += rows
+    small[n - 3].wait()
+    wide_to[0][...] = held[n - 3][...].reshape(wide_to[0].shape)
+    leave(wide_to[0], outs[2])
     for copy, (w, i) in zip(large, chunks):
         copy.wait()
         leave(part(held[w], w, i), part(outs[w], w, i))
@@ -950,11 +1151,11 @@
         pl.pallas_call(
             finish,
             out_shape=outs,
-            in_specs=[hbm] * 7,
+            in_specs=[hbm] * len(parts),
             out_specs=[hbm] * 13,
             scratch_shapes=[pltpu.VMEM(p.shape, p.dtype) for p in parts]
             + [pltpu.VMEM(o.shape, o.dtype) for o in outs[2:]]
-            + [dma((15,)), dma((19,))],
+            + [dma((len(parts) + 8,)), dma((19,))],
             compiler_params=pltpu.CompilerParams(vmem_limit_bytes=60 << 20),
         )(*parts)
     )

time: 130 us -> 112 us (0.86)
  Pallas kernels: 129 us -> 111 us
    pallas_call x2, Pallas kernels: 129 us -> 111 us  [the longest x1 107 us: on_device(): pl.pallas_call(body, out_shape=flat[2], in_specs=[smem] * len(flat[0]) +...]
where the time goes in v4:
time: 112 us
  Pallas kernels  111 us (99%)
    pallas_call x1, Pallas kernels, on_device(): pl.pallas_call(body, out_shape=flat[2], in_specs=[smem] * len(flat[0]) +...  107 us
    pallas_call x1, Pallas kernels, finished(): pl.pallas_call(finish, out_shape=outs, in_specs=[hbm] * len(parts), out_s...  3.94 us

profile of v4, /device:TPU:0, one launch (start us, length us, event | category | flops | bytes accessed | tf_op | source)
XLA Modules:
  0.0 111.9 jit_solution(17726955684530277890)
XLA Ops:
  0.7 107.3 %shard_map.246 = (bf16[4,14,56,256]{3,2,1,0:T(8,128)(2,1)}, f32[8,128]{1,0:T(8,128)}, bf16[1,28,28,512]{3,2,1,0:T(8,128)(2,1)}, bf16[512,128]{1,0:T(8,128)(2,1)}...) custom-call(s32[4]{0:T(128)} %refs_0_.1, ...), custom_call_target="tpu_custom_call" | custom-call | tf_op jit(solution)/shard_map/pallas_call | solution.py:1058
  107.9 3.9 %shard_map.247 = (bf16[1,28,28,512]{3,2,1,0:T(8,128)(2,1)}, bf16[4,14,56,256]{3,2,1,0:T(8,128)(2,1)}, f32[256,128]{1,0:T(8,128)}, f32[3,3,128,128]{3,2,1,0:T(8,1...) custom-call(bf16[1,28,28,512]{3,2,1,0:T(8,128)(2,1)} %get-tuple-elem, ...), custom_call_target="tpu_custom_call" | custom-call | tf_op jit(solution)/shard_map/pallas_call | solution.py:1151

commit v5 on v4

--- a/solution.py
+++ b/solution.py
@@ -12,23 +12,27 @@
 F32 = jnp.float32
 BF16 = jnp.bfloat16
 epsilon = 1e-05
+COT_AT = ((0,), (1,), (2, 3), (4,), (5, 6))
+OUT_AT = ((0, 1), (2,), (3, 4), (5,), (6,), ())
 PAD = 32
 LANES = 128
 
-ROUND_ROWS = (4, 2, 8, 2, 2, 8, 8, 2, 2, 12, 2, 2)
+ROUND_ROWS = (4, 2, 8, 2, 2, 10, 8, 2, 2, 14, 2)
 WIDE = (2, 5, 6, 9)
 
+
 GROUPS = (
-    (("expand_two", 512),),
-    (("spatial_two", 1152),),
+    (("expand_two", 512), ("spatial_two", 1152)),
     (("reduce_two", 512),),
     (("expand_one", 512), ("shortcut", 1024)),
     (("spatial_one", 1152),),
+    (("slope", 128), ("slope_z", 128)),
 )
-
-
-def group_rows(group, devices):
-    unit = 16 * devices
+GROUP_TYPES = (BF16, BF16, BF16, BF16, F32)
+
+
+def group_rows(g, devices):
+    group, unit = GROUPS[g], (16 if GROUP_TYPES[g] == BF16 else 8) * devices
     return -(-sum(rows for _, rows in group) // unit) * unit
 
 
@@ -46,6 +50,11 @@
 
 def dot_tn(a, b):
     return lax.dot_general(a, b, (((0,), (0,)), ((), ())), preferred_element_type=F32)
+
+
+def two_terms(x):
+    high = x.astype(BF16)
+    return high, (x - high.astype(F32)).astype(BF16)
 
 
 def half_silu(h, half_mask=0.5):
@@ -114,6 +123,29 @@
     col_mask = (lax.broadcasted_iota(jnp.int32, (PAD, 1), 0) < wv).astype(F32)
     half_mask = 0.5 * col_mask
 
+    chips = nr * nxy
+    chip = row * nxy + xy
+
+    def chip_copy(src, dst, to, send_sem, recv_sem):
+        return pltpu.make_async_remote_copy(
+            src_ref=src,
+            dst_ref=dst,
+            send_sem=send_sem,
+            recv_sem=recv_sem,
+            device_id=(lax.div(to, nxy), lax.rem(to, nxy) * 2 + core),
+            device_id_type=MESH,
+        )
+
+    def to_chips(copy_to):
+        def send(k, c):
+            copy_to(lax.rem(chip + k, chips)).start()
+            return c
+
+        lax.fori_loop(1, chips, send, 0)
+
+    def all_of(ref, n, sem):
+        pltpu.make_async_copy(ref.at[pl.ds(0, n)], ref.at[pl.ds(0, n)], sem).wait()
+
     def to_all(copy_to):
         def send(k, c):
             copy_to(lax.rem(me + k, ndev)).start()
@@ -148,6 +180,7 @@
     def send_sums(idx, vectors):
         rows = lines(vectors)
         assert len(rows) == ROUND_ROWS[idx]
+        slots = r.sums[idx]
         if idx in WIDE:
             half = len(rows) // 2
             both, came = r.both[idx], r.from_pair[idx]
@@ -156,24 +189,33 @@
             copy = pair_copy(idx, both.at[1 - core], came)
             copy.start()
             copy.wait()
-            r.sums[idx][me] = both[core] + came[...]
+            slots[chip] = both[core] + came[...]
         else:
             for at, v in enumerate(rows):
-                r.sums[idx][me, at : at + 1, :] = v
-        to_all(lambda p: sum_copy(idx, p))
+                slots[me, at : at + 1, :] = v
+        if idx in WIDE:
+            mine = slots.at[chip]
+            to_chips(lambda to: chip_copy(mine, mine, to, r.sum_send.at[idx], r.sum_recv.at[idx]))
+        else:
+            to_all(lambda p: sum_copy(idx, p))
 
     def take_sums(idx, widths):
-        buf = r.sums[idx]
-        others = buf.at[pl.ds(0, ndev - 1)]
-        pltpu.make_async_copy(others, others, r.sum_recv.at[idx]).wait()
+        slots = r.sums[idx]
+        others = slots.shape[0] - 1
+        all_of(slots, others, r.sum_recv.at[idx])
         if idx in WIDE:
+            totals = r.totals[idx]
+            totals[core] = jnp.sum(slots[...], axis=0)
+            mine = totals.at[core]
+            copy = pair_copy(14 + WIDE.index(idx), mine, mine)
+            copy.start()
+            copy.wait()
             half = ROUND_ROWS[idx] // 2
-            total = jnp.sum(buf[...].reshape(ndev // 2, 2, half, LANES), axis=0)
-            rows = [total[at // half, at % half : at % half + 1, :] for at in range(2 * half)]
+            rows = [totals[at // half, at % half : at % half + 1, :] for at in range(2 * half)]
         else:
-            total = jnp.sum(buf[...], axis=0)
+            total = jnp.sum(slots[...], axis=0)
             rows = [total[at : at + 1, :] for at in range(ROUND_ROWS[idx])]
-        pltpu.make_async_copy(others, others, r.sum_send.at[idx]).wait()
+        all_of(slots, others, r.sum_send.at[idx])
         result, at = [], 0
         for w in widths:
             parts = rows[at : at + w // LANES]
@@ -218,29 +260,6 @@
         halo_put(idx, 0, ref[:, hh - 1])
         halo_put(idx + 1, 0, ref[:, 0])
 
-    chips = nr * nxy
-    chip = row * nxy + xy
-
-    def chip_copy(src, dst, to, send_sem, recv_sem):
-        return pltpu.make_async_remote_copy(
-            src_ref=src,
-            dst_ref=dst,
-            send_sem=send_sem,
-            recv_sem=recv_sem,
-            device_id=(lax.div(to, nxy), lax.rem(to, nxy) * 2 + core),
-            device_id_type=MESH,
-        )
-
-    def to_chips(copy_to):
-        def send(k, c):
-            copy_to(lax.rem(chip + k, chips)).start()
-            return c
-
-        lax.fori_loop(1, chips, send, 0)
-
-    def all_of(ref, n, sem):
-        pltpu.make_async_copy(ref.at[pl.ds(0, n)], ref.at[pl.ds(0, n)], sem).wait()
-
     def skip_send(vectors):
         for at, v in enumerate(lines(vectors)):
             r.pair_rows[at // 4, at % 4 : at % 4 + 1, :] = v
@@ -287,7 +306,7 @@
         at = 0
         for i, (kind, _) in enumerate(axes[:level]):
             at = at + seat[kind] * level_rows(g, i + 1)
-        return pl.multiple_of(at, 16) if level else 0
+        return pl.multiple_of(at, 8) if level else 0
 
     def scatter_send(g, level):
         kind, n = axes[level]
@@ -295,7 +314,7 @@
         for k in range(1, n):
             p = lax.rem(seat[kind] + k, n)
             pltpu.make_async_remote_copy(
-                src_ref=r.part[g][level].at[pl.ds(pl.multiple_of(p * chunk, 16), chunk)],
+                src_ref=r.part[g][level].at[pl.ds(pl.multiple_of(p * chunk, 8), chunk)],
                 dst_ref=r.came[g][level].at[k - 1],
                 send_sem=r.grad_send.at[g, level],
                 recv_sem=r.grad_recv.at[g, level],
@@ -308,13 +327,13 @@
         chunk = level_rows(g, level + 1)
         came = r.came[g][level]
         pltpu.make_async_copy(came, came, r.grad_recv.at[g, level]).wait()
-        mine = pl.ds(pl.multiple_of(seat[kind] * chunk, 16), chunk)
+        mine = pl.ds(pl.multiple_of(seat[kind] * chunk, 8), chunk)
         total = r.part[g][level][mine, :].astype(F32) + jnp.sum(came[...].astype(F32), axis=0)
         pltpu.make_async_copy(came, came, r.grad_send.at[g, level]).wait()
         if level + 1 < len(axes):
-            r.part[g][level + 1][...] = total.astype(BF16)
+            r.part[g][level + 1][...] = total.astype(GROUP_TYPES[g])
         else:
-            r.full[g][pl.ds(offset(g, 3), chunk), :] = total.astype(BF16)
+            r.full[g][pl.ds(offset(g, 3), chunk), :] = total.astype(GROUP_TYPES[g])
 
     def gather_send(g, level):
         kind, n = axes[level]
@@ -358,36 +377,39 @@
         for q in range(blocks):
             n = value.shape[0]
             lo = at + q * n
-            r.part[g][0][lo : lo + n, :] = value[:, q * LANES : (q + 1) * LANES].astype(BF16)
+            r.part[g][0][lo : lo + n, :] = value[:, q * LANES : (q + 1) * LANES].astype(GROUP_TYPES[g])
 
     def one_send(value):
         r.one_both[...] = value.reshape(2, chips, -1, LANES)
-        pair_copy(14, r.one_both.at[1 - core], r.one_came).start()
+        pair_copy(18, r.one_both.at[1 - core], r.one_came).start()
 
     def one_spread():
-        pair_copy(14, r.one_both.at[1 - core], r.one_came).wait()
-        r.one_half[...] = r.one_both[core] + r.one_came[...]
-        to_chips(
-            lambda to: chip_copy(
-                r.one_half.at[to], r.one_slots.at[chip], to, r.chip_send.at[1], r.chip_recv.at[1]
-            )
-        )
+        pair_copy(18, r.one_both.at[1 - core], r.one_came).wait()
+        half, slots = r.one_half, r.one_slots
+        half[...] = r.one_both[core] + r.one_came[...]
+        sems = (r.chip_send.at[1], r.chip_recv.at[1])
+        to_chips(lambda to: chip_copy(half.at[to], slots.at[chip], to, *sems))
 
     def one_gather():
-        all_of(r.one_slots, chips - 1, r.chip_recv.at[1])
-        r.one_slots[chip] = r.one_half[chip]
-        r.one_whole[core, chip] = jnp.sum(r.one_slots[...], axis=0)
+        slots = r.one_slots
+        all_of(slots, chips - 1, r.chip_recv.at[1])
+        slots[chip] = r.one_half[chip]
+        r.one_whole[core, chip] = jnp.sum(slots[...], axis=0)
         mine = r.one_whole.at[core, chip]
-        to_chips(lambda to: chip_copy(mine, mine, to, r.chip_send.at[2], r.chip_recv.at[2]))
+        sems = (r.chip_send.at[2], r.chip_recv.at[2])
+        to_chips(lambda to: chip_copy(mine, mine, to, *sems))
 
     def one_return():
-        all_of(r.one_slots, chips - 1, r.chip_send.at[1])
-        all_of(r.one_slots, chips - 1, r.chip_recv.at[2])
-        all_of(r.one_slots, chips - 1, r.chip_send.at[2])
-        pair_copy(15, r.one_whole.at[core], r.one_whole.at[core]).start()
+        slots = r.one_slots
+        all_of(slots, chips - 1, r.chip_send.at[1])
+        all_of(slots, chips - 1, r.chip_recv.at[2])
+        all_of(slots, chips - 1, r.chip_send.at[2])
+        mine = r.one_whole.at[core]
+        pair_copy(19, mine, mine).start()
 
     def one_take():
-        pair_copy(15, r.one_whole.at[core], r.one_whole.at[core]).wait()
+        mine = r.one_whole.at[core]
+        pair_copy(19, mine, mine).wait()
 
     def coefficients(total, square, count, gain, bias):
         n = jnp.maximum(count, 1.0)
@@ -396,14 +418,42 @@
         scale = gain * inv
         return SimpleNamespace(n=n, mu=mu, inv=inv, scale=scale, shift=bias - mu * scale)
 
-    def backward(norm, dbias, dz_sum):
-        dgain = norm.inv * (dz_sum - norm.mu * dbias)
+    def factors(norm, dbias, dgain):
         c2 = -norm.scale * norm.inv * dgain / norm.n
         c3 = -norm.scale * dbias / norm.n - c2 * norm.mu
-        return dgain, (norm.scale, c2, c3)
+        return norm.scale, c2, c3
+
+    def gain_sum(norm, total, z_total):
+        return norm.inv * (z_total - norm.mu * total)
+
+    def slope_sums(mask, slope, z, a, norm):
+        def scaled(k, c):
+            t = mask[k] * slope[k]
+            r.dz4[k] = t.astype(BF16)
+            r.slope_z[k] = (t * ((z[k] - norm.mu) * norm.inv)).astype(BF16)
+            return c
+
+        loop(scaled)
+        flat_a = flat2(a[...])
+        stage(4, "slope", dot_tn(flat_a, flat2(r.dz4[...])))
+        stage(4, "slope_z", dot_tn(flat_a, flat2(r.slope_z[...])))
+
+    def through(weight, c2, c3):
+        high, low = two_terms(weight.astype(F32) * c2)
+        b = dot_nt(high, weight) + dot_nt(low, weight)
+        v = sum(dot_nt(jnp.broadcast_to(c, (16, c.shape[1])), weight) for c in two_terms(c3))
+        return b, v[0:1]
+
+    def chained(norm, u_sum, uz_sum, t_sum, tz_sum, b, v):
+        k1, k2 = r.full[4][0:LANES, :], r.full[4][LANES : 2 * LANES, :]
+        dbias = u_sum + row_sum(k1 * b) + t_sum * v
+        dgain = gain_sum(norm, u_sum, uz_sum) + row_sum(k2 * b) + gain_sum(norm, t_sum, tz_sum) * v
+        return dbias, dgain
 
     def loop(body, init=0):
-        return lax.fori_loop(0, nk, body, init)
+        for k in range(nk):
+            init = body(k, init)
+        return init
 
     def zero8(width, count):
         return tuple(jnp.zeros((8, width), F32) for _ in range(count))
@@ -497,7 +547,7 @@
     send_sums(0, [row_sum(s1), row_sum(s2), count_one, count_two])
     halo_start(0)
     skip_send([row_sum(zs1), row_sum(zs2)])
-    start_pieces(cot_copies, 0)
+    start_pieces(cot_copies, *COT_AT[0])
     arrived("mid_gain", "mid_bias", "spatial_one")
     t1, t2, active_one, active_two = take_sums(0, [LANES] * 4)
     half_px, full_px = float(hh * wv), float(4 * hh * wv)
@@ -549,7 +599,6 @@
     s1, s2 = loop(second, zero8(LANES, 2))
     send_sums(1, [row_sum(s1), row_sum(s2)])
     skip_spread()
-    start_pieces(cot_copies, 1)
 
     def early(k, c):
         m = r.mask_one[k]
@@ -566,6 +615,7 @@
     planes = [(pr, pc) for pr in range(2) for pc in range(2)]
     r.part_z[...] = sum(dot_tn(flat2(r.x[q]), flat2(r.dz1[q])) for q in planes)
     r.part_m[...] = sum(dot_tn(flat2(r.x[q]), flat2(r.dz4[...])) for q in planes)
+    start_pieces(cot_copies, *COT_AT[1])
     t1, t2 = take_sums(1, [LANES] * 2)
     n2 = coefficients(t1, t2, active_one * half_px, r.mid_gain[1:2, :], r.mid_bias[1:2, :])
     e1 = r.expand_one[...]
@@ -578,11 +628,15 @@
         r.a2[k] = a
         z = dot(flat2(a), e1)
         r.z3[k] = z.reshape(hh, PAD, cfg.c_out)
-        return acc[0] + folded(z), acc[1] + folded(z * z)
-
-    s1, s2 = loop(third, zero8(cfg.c_out, 2))
+        t = r.mask_one[k] * s
+        return (
+            acc[0] + folded(z), acc[1] + folded(z * z), acc[2] + folded(t), acc[3] + folded(t * r.z2[k])
+        )
+
+    s1, s2, t2_sum, t2z_sum = loop(third, zero8(cfg.c_out, 2) + zero8(LANES, 2))
     send_sums(2, [row_sum(s1), row_sum(s2)])
-    start_pieces(cot_copies, 2, 3)
+    slope_sums(r.mask_one, r.s2, r.z2, r.a2, n2)
+    advance(4, 0)
     arrived("spatial_two", "expand_two")
     def tap(ref, i, j):
         return ref[i, j * LANES : (j + 1) * LANES, :].T
@@ -600,6 +654,7 @@
             for j, block in enumerate(line):
                 ref[i * LANES : (i + 1) * LANES, j * LANES : (j + 1) * LANES] = block
     skip_return()
+    start_pieces(cot_copies, *COT_AT[2])
     t1, t2 = take_sums(2, [cfg.c_out] * 2)
     ts1, ts2 = skip_take()
     all_px = float(nk * nc) * float(nr) * half_px
@@ -624,7 +679,21 @@
     both_edges(1, r.z4)
     halo_start(1)
     halo_start(2)
-    start_pieces(cot_copies, 4)
+
+    def hats(k, c):
+        for i in range(hh):
+            r.dz3[k, i] = ((r.z3[k, i] - n3.mu) * n3.inv).astype(BF16)
+            r.dzs[k, i] = ((r.zs[k, i] - ns.mu) * ns.inv).astype(BF16)
+        return c
+
+    advance(4, 1)
+    loop(hats)
+    ones = jnp.ones((nk * m_half, LANES), BF16)
+    r.expand_z[...] = dot_tn(flat2(r.a2[...]), flat2(r.dz3[...]))
+    r.expand_m[...] = dot_tn(flat2(r.a2[...]), ones)
+    r.skip_z[...] = dot_tn(flat2(r.x[0, 0]), flat2(r.dzs[...]))
+    r.skip_m[...] = dot_tn(flat2(r.x[0, 0]), ones)
+    start_pieces(cot_copies, *COT_AT[3])
     t1, t2 = take_sums(3, [LANES] * 2)
     n4 = coefficients(t1, t2, active_two * half_px, r.mid_gain[2:3, :], r.mid_bias[2:3, :])
     halo_wait(1)
@@ -654,7 +723,8 @@
 
     s1, s2 = loop(fifth, zero8(LANES, 2))
     send_sums(4, [row_sum(s1), row_sum(s2)])
-    start_pieces(cot_copies, 5, 6)
+    advance(4, 2)
+    start_pieces(cot_copies, *COT_AT[4])
     t1, t2 = take_sums(4, [LANES] * 2)
     n5 = coefficients(t1, t2, active_two * half_px, r.mid_gain[3:4, :], r.mid_bias[3:4, :])
     e2 = r.expand_two[...]
@@ -671,13 +741,14 @@
         return acc[0] + g * folded(z), acc[1] + g * folded(z * z)
 
     s1, s2 = loop(sixth, zero8(cfg.c_out, 2))
-    send_sums(5, [row_sum(s1), row_sum(s2)])
+    send_sums(5, [row_sum(v) for v in (s1, s2, t2_sum, t2z_sum)])
     both_edges(3, r.z5)
     halo_start(3)
     halo_start(4)
+    advance(4, 3)
     wait_pieces(0)
     cot_local.wait()
-    t1, t2 = take_sums(5, [cfg.c_out] * 2)
+    t1, t2, t2_sum, t2z_sum = take_sums(5, [cfg.c_out] * 2 + [LANES] * 2)
     gate_count = active_gate * half_px
     n6 = coefficients(t1, t2, gate_count, r.wide_gain[2:3, :], r.wide_bias[2:3, :])
     pad_rows = jnp.zeros((PAD - wv, cfg.c_out), F32)
@@ -700,13 +771,15 @@
             d2 += folded(live * z)
         return d1, d2
 
-    d1, d2 = loop(seventh, zero8(cfg.c_out, 2))
-    send_sums(6, [row_sum(d1), row_sum(d2)])
-
-    start_pieces(out_copies, 0, 1)
+    sums = loop(seventh, zero8(cfg.c_out, 2))
+    send_sums(6, [row_sum(v) for v in sums])
+
+    advance(4, 4)
+    start_pieces(out_copies, *OUT_AT[0])
     out_local.start()
     db6, q6 = take_sums(6, [cfg.c_out] * 2)
-    dg6, (c1, c2, c3) = backward(n6, db6, q6)
+    dg6 = gain_sum(n6, db6, q6)
+    c1, c2, c3 = factors(n6, db6, dg6)
 
     def eighth(k, acc, c1=c1, c2=c2, c3=c3):
         g = r.gates[k]
@@ -723,13 +796,14 @@
     both_edges(5, r.q5)
     halo_start(5)
     halo_start(6)
-    start_pieces(out_copies, 2)
     stage(0, "expand_two", dot_tn(flat2(r.a5[...]), flat2(r.dz6[...])))
-    advance(0, 0)
     halo_wait(3)
     halo_wait(4)
+    advance(4, 5)
+    start_pieces(out_copies, *OUT_AT[1])
     db5, q5 = take_sums(7, [LANES] * 2)
-    dg5, (c1, c2, c3) = backward(n5, db5, q5)
+    dg5 = gain_sum(n5, db5, q5)
+    c1, c2, c3 = factors(n5, db5, dg5)
     halo_wait(5)
     halo_wait(6)
 
@@ -748,80 +822,94 @@
 
     d1, d2 = loop(ninth, zero8(LANES, 2))
     send_sums(8, [row_sum(d1), row_sum(d2)])
-    start_pieces(out_copies, 3)
+    halo_put(8, 0, r.z2[:, 0])
+    halo_start(8)
+
     d5 = flat2(r.dz5[:, 1 : hh + 1, :, LANES : 2 * LANES])
     stage(
-        1,
+        0,
         "spatial_two",
         jnp.concatenate([dot_tn(flat2(r.a4[:, i : i + hh]), d5) for i in range(3)], axis=0),
     )
-    halo_put(8, 0, r.z2[:, 0])
-    halo_start(8)
+    advance(4, 6)
+    advance(0, 0)
+    start_pieces(out_copies, *OUT_AT[2])
+    db4, q4 = take_sums(8, [LANES] * 2)
     advance(0, 1)
-    advance(1, 0)
-    db4, q4 = take_sums(8, [LANES] * 2)
-    dg4, (c1, c2, c3) = backward(n4, db4, q4)
+    dg4 = gain_sum(n4, db4, q4)
+    c1, c2, c3 = factors(n4, db4, dg4)
 
     def tenth(k, acc, c1=c1, c2=c2, c3=c3):
         m, g = r.mask_two[k], r.gates[k]
         f1, f2, f3 = m * c1, m * c2, (m * c3) * col_mask
         r.dz4[k] = (r.q4[k] * f1 + r.z4[k] * f2 + f3).astype(BF16)
         back = dot_nt(flat2(r.dz4[k]), w2).reshape(hh, PAD, cfg.c_out)
-        e1_, e2_, e3_ = acc
+        e1_, e2_, e3_, u1, u2 = acc
         for i in range(hh):
             d = back[i] + (1.0 - g) * cot_row(k, i) + r.live[k, i]
             q = d.astype(BF16).astype(F32) * r.s3[k, i]
             r.q3[k, i] = q
+            r.dz3[k, i] = (q * n3.scale).astype(BF16)
             e1_ += folded(q)
             e2_ += folded(q * r.z3[k, i])
             e3_ += folded(q * r.zs[k, i])
-        return e1_, e2_, e3_
-
-    d1, d2, d3 = loop(tenth, zero8(cfg.c_out, 3))
-    send_sums(9, [row_sum(d1), row_sum(d2), row_sum(d3)])
-    start_pieces(out_copies, 4)
-    stage(2, "reduce_two", dot_tn(flat2(r.hidden[...]), flat2(r.dz4[...])))
+        u = dot_nt(flat2(r.dz3[k]), e1).reshape(hh, PAD, LANES)
+        r.q2[k] = u
+        ut = (r.mask_one[k] * u) * r.s2[k]
+        return e1_, e2_, e3_, u1 + folded(ut), u2 + folded(ut * r.z2[k])
+
+    sums = loop(tenth, zero8(cfg.c_out, 3) + zero8(LANES, 2))
+    send_sums(9, [row_sum(v) for v in sums])
+    halo_put(7, 0, r.q2[:, 0])
+    halo_start(7)
+    stage(1, "reduce_two", dot_tn(flat2(r.hidden[...]), flat2(r.dz4[...])))
+    advance(1, 0)
+    expand_q = dot_tn(flat2(r.a2[...]), flat2(r.dz3[...]))
+    skip_q = dot_tn(flat2(r.x[0, 0]), flat2(r.dz3[...]))
+    halo_wait(8)
+
+    def edge_slope(k, c):
+        ah, bh = affine(n2, r.mask_one[k])
+        a, t = half_silu(halo_row(8, 0, k) * ah + bh, half_mask)
+        r.edge_a[k] = a.astype(BF16)
+        r.edge_t[k] = t
+        return c
+
+    loop(edge_slope)
     advance(1, 1)
     advance(0, 2)
+    start_pieces(out_copies, *OUT_AT[3])
+    db3, q3, qs, u_sum, uz_sum = take_sums(9, [cfg.c_out] * 3 + [LANES] * 2)
+    dg3, dgs = gain_sum(n3, db3, q3), gain_sum(ns, db3, qs)
+    f3_, fs_ = factors(n3, db3, dg3), factors(ns, db3, dgs)
+    b, v2 = through(e1, *f3_[1:])
+    db2, dg2 = chained(n2, u_sum, uz_sum, t2_sum, t2z_sum, b, v2)
+    c1, c2, c3 = factors(n2, db2, dg2)
+    b2 = two_terms(b)
+
+    def four(x):
+        return jnp.concatenate([x] * (cfg.c_out // LANES), axis=1)
+
+    def by_parts(q_part, z_part, m_part, norm, fs):
+        total = q_part + (fs[1] / norm.inv) * z_part[...]
+        return total + (fs[2] + fs[1] * norm.mu) * four(m_part[...])
+
+    stage(2, "expand_one", by_parts(expand_q, r.expand_z, r.expand_m, n3, f3_))
+    stage(2, "shortcut", by_parts(skip_q * (ns.scale / n3.scale), r.skip_z, r.skip_m, ns, fs_))
     advance(2, 0)
-    db3, q3, qs = take_sums(9, [cfg.c_out] * 3)
-    dg3, (c1, c2, c3) = backward(n3, db3, q3)
-    dgs, (p1, p2, p3) = backward(ns, db3, qs)
-
-    def eleventh(k, acc, c1=c1, c2=c2, c3=c3):
-        f3, h3 = c3 * col_mask, p3 * col_mask
-        for i in range(hh):
-            q = r.q3[k, i]
-            r.dz3[k, i] = (q * c1 + r.z3[k, i] * c2 + f3).astype(BF16)
-            r.dzs[k, i] = (q * p1 + r.zs[k, i] * p2 + h3).astype(BF16)
-        q = dot_nt(flat2(r.dz3[k]), e1).reshape(hh, PAD, LANES) * r.s2[k]
-        r.q2[k] = q
-        m = r.mask_one[k]
-        return acc[0] + m * folded(q), acc[1] + m * folded(q * r.z2[k])
-
-    d1, d2 = loop(eleventh, zero8(LANES, 2))
-    send_sums(10, [row_sum(d1), row_sum(d2)])
-    halo_put(7, 0, r.q2[:, 0])
-    halo_start(7)
-    stage(3, "expand_one", dot_tn(flat2(r.a2[...]), flat2(r.dz3[...])))
-    stage(3, "shortcut", dot_tn(flat2(r.x[0, 0]), flat2(r.dzs[...])))
-    advance(3, 0)
-    advance(1, 2)
-    advance(2, 1)
-    start_pieces(out_copies, 5)
-    halo_wait(8)
-    db2, q2 = take_sums(10, [LANES] * 2)
-    dg2, (c1, c2, c3) = backward(n2, db2, q2)
     halo_wait(7)
-    advance(3, 1)
+    edge_ab = sum(dot(flat2(r.edge_a[...]), t) for t in b2).reshape(nk, PAD, LANES)
 
     def twelfth(k, c, c1=c1, c2=c2, c3=c3):
         m = r.mask_one[k]
         f1, f2, f3 = m * c1, m * c2, (m * c3) * col_mask
-        d = r.q2[k] * f1 + r.z2[k] * f2 + f3
+        ab = sum(dot(flat2(r.a2[k]), t) for t in b2).reshape(hh, PAD, LANES)
+        q = (r.q2[k] + ab + v2) * r.s2[k]
+        d = q * f1 + r.z2[k] * f2 + f3
         r.dz2[k, 0:hh, :, 0:LANES] = d.astype(BF16)
         r.dz2[k, 0:hh, :, LANES : 2 * LANES] = shifted_left(d).astype(BF16)
-        d = jnp.where(row < nr - 1, halo_row(7, 0, k) * f1 + halo_row(8, 0, k) * f2 + f3, 0.0)
+        q = (halo_row(7, 0, k) + edge_ab[k] + v2) * r.edge_t[k]
+        d = jnp.where(row < nr - 1, q * f1 + halo_row(8, 0, k) * f2 + f3, 0.0)
         r.dz2[k, hh, :, 0:LANES] = d.astype(BF16)
         r.dz2[k, hh, :, LANES : 2 * LANES] = shifted_left(d).astype(BF16)
         return c
@@ -829,8 +917,11 @@
     loop(twelfth)
     d2_ = flat2(r.dz2[:, 0:hh, :, 0:LANES])
     inputs = [r.odd[:, 0:hh], r.even[...], r.odd[:, 1 : hh + 1]]
-    stage(4, "spatial_one", jnp.concatenate([dot_tn(flat2(a), d2_) for a in inputs], axis=0))
-    advance(4, 0)
+    stage(3, "spatial_one", jnp.concatenate([dot_tn(flat2(a), d2_) for a in inputs], axis=0))
+
+
+    advance(3, 0)
+    advance(2, 1)
 
     def thirteenth(k, acc):
         m = r.mask_one[k]
@@ -852,32 +943,34 @@
         return s1, s2
 
     d1, d2 = loop(thirteenth, zero8(LANES, 2))
-    send_sums(11, [row_sum(d1), row_sum(d2)])
-    advance(4, 1)
+    send_sums(10, [row_sum(d1), row_sum(d2)])
+    advance(3, 1)
     advance(0, 3)
-    start_pieces(out_copies, 6)
+    advance(1, 2)
     part_q = sum(dot_tn(flat2(r.x[q]), flat2(r.dz1[q])) for q in planes)
-    advance(1, 3)
-    advance(2, 2)
 
     def skip_back(k, c):
+        h3 = fs_[2] * col_mask
+        for i in range(hh):
+            r.dzs[k, i] = (r.q3[k, i] * fs_[0] + r.zs[k, i] * fs_[1] + h3).astype(BF16)
         r.skip_back[k] = dot_nt(flat2(r.dzs[k]), sc).reshape(hh, PAD, cfg.c_in)
         return c
 
     loop(skip_back)
-    advance(3, 2)
-    db1, q1 = take_sums(11, [LANES] * 2)
-    dg1, (c1, c2, c3) = backward(n1, db1, q1)
+    start_pieces(out_copies, *OUT_AT[4])
+    advance(2, 2)
+    db1, q1 = take_sums(10, [LANES] * 2)
+    dg1 = gain_sum(n1, db1, q1)
+    c1, c2, c3 = factors(n1, db1, dg1)
 
     total = n1.scale * part_q
     total += (c2 / n1.inv) * r.part_z[...] + (c3 + c2 * n1.mu) * r.part_m[...]
     one_send(total)
-    advance(4, 2)
     one_spread()
-    advance(3, 3)
-    advance(1, 4)
-    advance(2, 3)
+    advance(3, 2)
     advance(0, 4)
+    advance(1, 3)
+    start_pieces(out_copies, *OUT_AT[5])
 
     def last(k, acc, c1=c1, c2=c2, c3=c3):
         m = r.mask_one[k]
@@ -928,29 +1021,27 @@
     def result(g):
         give(r.full[g], r.summed[g])
 
-    advance(4, 3)
+    advance(2, 3)
+    advance(3, 3)
     one_gather()
+    advance(0, 5)
+    advance(1, 4)
+    advance(2, 4)
     advance(3, 4)
+    one_return()
+    advance(0, 6)
+    result(0)
     advance(1, 5)
-    advance(2, 4)
-    advance(0, 5)
-    advance(4, 4)
-    one_return()
+    advance(2, 5)
     advance(3, 5)
+    one_take()
+    give(r.one_whole, r.summed_one)
     advance(1, 6)
     result(1)
-    advance(2, 5)
-    advance(0, 6)
-    result(0)
-    advance(4, 5)
+    advance(2, 6)
+    result(2)
     advance(3, 6)
     result(3)
-    advance(2, 6)
-    result(2)
-    one_take()
-    give(r.one_whole, r.summed_one)
-    advance(4, 6)
-    result(4)
     wait_pieces(1)
     out_local.wait()
     back_copy.wait()
@@ -965,7 +1056,7 @@
     hh, wv, c_out = full_rows // 2, full_cols // 2, expand_one.shape[1]
     own = cot.shape[0]
     ndev, nxy, groups = nr * nc, nc // 2, len(GROUPS)
-    sizes = [group_rows(g, ndev) for g in GROUPS]
+    sizes = [group_rows(g, ndev) for g in range(groups)]
     chunk = (ndev // 2, c_in // ndev, LANES)
     half, quad = (nk, hh, PAD), (2, 2, nk, hh, PAD)
 
@@ -998,7 +1089,7 @@
     outs = dict(
         out=jax.ShapeDtypeStruct(cot.shape, BF16),
         images_grad=jax.ShapeDtypeStruct(images.shape, BF16),
-        summed=[jax.ShapeDtypeStruct((size, LANES), BF16) for size in sizes],
+        summed=[jax.ShapeDtypeStruct((size, LANES), BF16) for size in sizes[:4]],
         summed_one=jax.ShapeDtypeStruct((2,) + chunk, F32),
         mid_grads=jax.ShapeDtypeStruct((8, LANES), F32),
         wide_grads=jax.ShapeDtypeStruct((6, c_out), F32),
@@ -1012,7 +1103,10 @@
         z1=f32(*quad, LANES), s1=f32(*quad, LANES), q1=f32(*quad, LANES), dz1=bf16(*quad, LANES),
         part_z=f32(c_in, LANES), part_m=f32(c_in, LANES),
         one_both=f32(2, *chunk), one_came=f32(*chunk), one_half=f32(*chunk), one_slots=f32(*chunk),
-        one_whole=f32(2, *chunk), mid_held=f32(8, LANES), wide_held=f32(6, c_out),
+        one_whole=f32(2, *chunk), slope_z=low(LANES),
+        edge_a=bf16(nk, PAD, LANES), edge_t=f32(nk, PAD, LANES),
+        expand_z=f32(LANES, c_out), expand_m=f32(LANES, LANES), skip_z=f32(c_in, c_out),
+        skip_m=f32(c_in, LANES), mid_held=f32(8, LANES), wide_held=f32(6, c_out),
         pair_rows=f32(2, 4, LANES), pair_came=f32(4, LANES), pair_chips=f32(ndev // 2, 4, LANES),
         pair_total=f32(2, 4, LANES),
         even=low(3 * LANES), odd=bf16(nk, hh + 1, PAD, 3 * LANES), dz2=bf16(nk, hh + 1, PAD, 2 * LANES),
@@ -1026,15 +1120,22 @@
         a2=low(LANES), a5=low(LANES), dz4=low(LANES),
         hidden=low(c_out), dz6=low(c_out), dz3=low(c_out), dzs=low(c_out),
         edge=edges, halo=edges,
-        sums=[f32(ndev, halves.get(i, n), LANES) for i, n in enumerate(ROUND_ROWS)],
+        sums=[
+            f32(ndev // 2 if i in WIDE else ndev, halves.get(i, n), LANES)
+            for i, n in enumerate(ROUND_ROWS)
+        ],
         both={i: f32(2, n, LANES) for i, n in halves.items()},
+        totals={i: f32(2, n, LANES) for i, n in halves.items()},
         from_pair={i: f32(n, LANES) for i, n in halves.items()},
-        part=[[bf16(n[i], LANES) for i in range(3)] for n in levels],
-        came=[[bf16(m - 1, n[i + 1], LANES) for i, m in enumerate((2, nxy, nr))] for n in levels],
-        full=[bf16(n, LANES) for n in sizes],
+        part=[[pltpu.VMEM((n[i], LANES), t) for i in range(3)] for n, t in zip(levels, GROUP_TYPES)],
+        came=[
+            [pltpu.VMEM((m - 1, n[i + 1], LANES), t) for i, m in enumerate((2, nxy, nr))]
+            for n, t in zip(levels, GROUP_TYPES)
+        ],
+        full=[pltpu.VMEM((n, LANES), t) for n, t in zip(sizes, GROUP_TYPES)],
         image_sem=dma(nk), local_sem=dma(3), full_sem=dma(groups + 3), weight_sem=dma(len(weights)),
         sum_send=dma(len(ROUND_ROWS)), sum_recv=dma(len(ROUND_ROWS)), halo_send=dma(9), halo_recv=dma(9),
-        row_send=dma(2), row_recv=dma(2), pair_send=dma(16), pair_recv=dma(16), chip_send=dma(3),
+        row_send=dma(2), row_recv=dma(2), pair_send=dma(20), pair_recv=dma(20), chip_send=dma(3),
         chip_recv=dma(3), grad_send=dma(groups, 6), grad_recv=dma(groups, 6),
     )
     cfg = SimpleNamespace(
@@ -1082,7 +1183,7 @@
 
 
 def finish(*refs):
-    n = len(GROUPS) + 5
+    n = len(GROUPS) + 4
     ins, outs, held = refs[:n], refs[n : n + 13], refs[n + 13 : 2 * n + 13]
     wide_to, (in_sem, out_sem) = refs[2 * n + 13 : 2 * n + 24], refs[2 * n + 24 :]
     chunks = [(0, i) for i in range(4)] + [(1, i) for i in range(4)]
@@ -1113,7 +1214,7 @@
         ref[...] = value
         leave(ref, to)
     names = [name for name, _ in WEIGHTS]
-    for g, group in enumerate(GROUPS):
+    for g, group in enumerate(GROUPS[:4]):
         small[2 + g].wait()
         summed = held[2 + g]
         at = 0

time: 112 us -> 101 us (0.902)
  Pallas kernels: 111 us -> 99.6 us
    pallas_call x1, Pallas kernels: 107 us -> 95.9 us  [on_device(): pl.pallas_call(body, out_shape=flat[2], in_specs=[smem] * len(flat[0]) +...]
where the time goes in v5:
time: 101 us; the launch traced here: 100 us
  Pallas kernels  99.6 us (99%)
    pallas_call x1, Pallas kernels, on_device(): pl.pallas_call(body, out_shape=flat[2], in_specs=[smem] * len(flat[0]) +...  95.9 us
    pallas_call x1, Pallas kernels, finished(): pl.pallas_call(finish, out_shape=outs, in_specs=[hbm] * len(parts), out_s...  3.71 us

profile of v5, /device:TPU:0, one launch (start us, length us, event | category | flops | bytes accessed | tf_op | source)
XLA Modules:
  0.0 100.4 jit_solution(3787711691448111695)
XLA Ops:
  0.7 95.9 %shard_map.246 = (bf16[4,14,56,256]{3,2,1,0:T(8,128)(2,1)}, f32[8,128]{1,0:T(8,128)}, bf16[1,28,28,512]{3,2,1,0:T(8,128)(2,1)}, bf16[2048,128]{1,0:T(8,128)(2,1)...) custom-call(s32[4]{0:T(128)} %refs_0_.1, ...), custom_call_target="tpu_custom_call" | custom-call | tf_op jit(solution)/shard_map/pallas_call | solution.py:1159
  96.5 3.7 %shard_map.247 = (bf16[1,28,28,512]{3,2,1,0:T(8,128)(2,1)}, bf16[4,14,56,256]{3,2,1,0:T(8,128)(2,1)}, f32[256,128]{1,0:T(8,128)}, f32[3,3,128,128]{3,2,1,0:T(8,1...) custom-call(bf16[1,28,28,512]{3,2,1,0:T(8,128)(2,1)} %get-tuple-elem, ...), custom_call_target="tpu_custom_call" | custom-call | tf_op jit(solution)/shard_map/pallas_call | solution.py:1252

commit v6 on v5

--- a/solution.py
+++ b/solution.py
@@ -22,10 +22,10 @@
 
 
 GROUPS = (
-    (("expand_two", 512), ("spatial_two", 1152)),
+    (("expand_two", 384), ("spatial_two", 1152)),
     (("reduce_two", 512),),
     (("expand_one", 512), ("shortcut", 1024)),
-    (("spatial_one", 1152),),
+    (("spatial_one", 1152), ("expand_rest", 128)),
     (("slope", 128), ("slope_z", 128)),
 )
 GROUP_TYPES = (BF16, BF16, BF16, BF16, F32)
@@ -55,6 +55,10 @@
 def two_terms(x):
     high = x.astype(BF16)
     return high, (x - high.astype(F32)).astype(BF16)
+
+
+def half_act(h):
+    return h + h * jnp.tanh(h)
 
 
 def half_silu(h, half_mask=0.5):
@@ -158,7 +162,7 @@
         return pltpu.make_async_remote_copy(
             src_ref=mine,
             dst_ref=mine,
-            send_sem=r.sum_send.at[idx],
+            send_sem=r.sum_send,
             recv_sem=r.sum_recv.at[idx],
             device_id=place(p),
             device_id_type=MESH,
@@ -186,7 +190,7 @@
             both, came = r.both[idx], r.from_pair[idx]
             for at, v in enumerate(rows):
                 both[at // half, at % half : at % half + 1, :] = v
-            copy = pair_copy(idx, both.at[1 - core], came)
+            copy = pair_copy(WIDE.index(idx), both.at[1 - core], came)
             copy.start()
             copy.wait()
             slots[chip] = both[core] + came[...]
@@ -195,7 +199,7 @@
                 slots[me, at : at + 1, :] = v
         if idx in WIDE:
             mine = slots.at[chip]
-            to_chips(lambda to: chip_copy(mine, mine, to, r.sum_send.at[idx], r.sum_recv.at[idx]))
+            to_chips(lambda to: chip_copy(mine, mine, to, r.sum_send, r.sum_recv.at[idx]))
         else:
             to_all(lambda p: sum_copy(idx, p))
 
@@ -207,7 +211,7 @@
             totals = r.totals[idx]
             totals[core] = jnp.sum(slots[...], axis=0)
             mine = totals.at[core]
-            copy = pair_copy(14 + WIDE.index(idx), mine, mine)
+            copy = pair_copy(4 + WIDE.index(idx), mine, mine)
             copy.start()
             copy.wait()
             half = ROUND_ROWS[idx] // 2
@@ -215,7 +219,7 @@
         else:
             total = jnp.sum(slots[...], axis=0)
             rows = [total[at : at + 1, :] for at in range(ROUND_ROWS[idx])]
-        all_of(slots, others, r.sum_send.at[idx])
+        all_of(slots, others, r.sum_send)
         result, at = [], 0
         for w in widths:
             parts = rows[at : at + w // LANES]
@@ -263,10 +267,10 @@
     def skip_send(vectors):
         for at, v in enumerate(lines(vectors)):
             r.pair_rows[at // 4, at % 4 : at % 4 + 1, :] = v
-        pair_copy(12, r.pair_rows.at[1 - core], r.pair_came).start()
+        pair_copy(8, r.pair_rows.at[1 - core], r.pair_came).start()
 
     def skip_spread():
-        pair_copy(12, r.pair_rows.at[1 - core], r.pair_came).wait()
+        pair_copy(8, r.pair_rows.at[1 - core], r.pair_came).wait()
         r.pair_chips[chip] = r.pair_rows[core] + r.pair_came[...]
         mine = r.pair_chips.at[chip]
         to_chips(lambda to: chip_copy(mine, mine, to, r.chip_send.at[0], r.chip_recv.at[0]))
@@ -276,11 +280,11 @@
         all_of(r.pair_chips, chips - 1, r.chip_send.at[0])
         r.pair_total[core] = jnp.sum(r.pair_chips[...], axis=0)
         mine = r.pair_total.at[core]
-        pair_copy(13, mine, mine).start()
+        pair_copy(9, mine, mine).start()
 
     def skip_take():
         mine = r.pair_total.at[core]
-        pair_copy(13, mine, mine).wait()
+        pair_copy(9, mine, mine).wait()
         return [
             jnp.concatenate([r.pair_total[i, q : q + 1, :] for q in range(4)], axis=1)
             for i in range(2)
@@ -316,7 +320,7 @@
             pltpu.make_async_remote_copy(
                 src_ref=r.part[g][level].at[pl.ds(pl.multiple_of(p * chunk, 8), chunk)],
                 dst_ref=r.came[g][level].at[k - 1],
-                send_sem=r.grad_send.at[g, level],
+                send_sem=r.grad_send.at[g],
                 recv_sem=r.grad_recv.at[g, level],
                 device_id=device_of(kind, p),
                 device_id_type=MESH,
@@ -329,7 +333,7 @@
         pltpu.make_async_copy(came, came, r.grad_recv.at[g, level]).wait()
         mine = pl.ds(pl.multiple_of(seat[kind] * chunk, 8), chunk)
         total = r.part[g][level][mine, :].astype(F32) + jnp.sum(came[...].astype(F32), axis=0)
-        pltpu.make_async_copy(came, came, r.grad_send.at[g, level]).wait()
+        pltpu.make_async_copy(came, came, r.grad_send.at[g]).wait()
         if level + 1 < len(axes):
             r.part[g][level + 1][...] = total.astype(GROUP_TYPES[g])
         else:
@@ -344,7 +348,7 @@
             pltpu.make_async_remote_copy(
                 src_ref=region,
                 dst_ref=region,
-                send_sem=r.grad_send.at[g, 3 + level],
+                send_sem=r.grad_send.at[g],
                 recv_sem=r.grad_recv.at[g, 3 + level],
                 device_id=device_of(kind, p),
                 device_id_type=MESH,
@@ -355,7 +359,7 @@
         size = level_rows(g, level + 1) * (n - 1)
         bytes_of = r.full[g].at[pl.ds(0, size)]
         pltpu.make_async_copy(bytes_of, bytes_of, r.grad_recv.at[g, 3 + level]).wait()
-        pltpu.make_async_copy(bytes_of, bytes_of, r.grad_send.at[g, 3 + level]).wait()
+        pltpu.make_async_copy(bytes_of, bytes_of, r.grad_send.at[g]).wait()
 
     steps = (
         (scatter_send, 0), (scatter_take, 0), (scatter_send, 1), (scatter_take, 1),
@@ -381,10 +385,10 @@
 
     def one_send(value):
         r.one_both[...] = value.reshape(2, chips, -1, LANES)
-        pair_copy(18, r.one_both.at[1 - core], r.one_came).start()
+        pair_copy(10, r.one_both.at[1 - core], r.one_came).start()
 
     def one_spread():
-        pair_copy(18, r.one_both.at[1 - core], r.one_came).wait()
+        pair_copy(10, r.one_both.at[1 - core], r.one_came).wait()
         half, slots = r.one_half, r.one_slots
         half[...] = r.one_both[core] + r.one_came[...]
         sems = (r.chip_send.at[1], r.chip_recv.at[1])
@@ -405,11 +409,11 @@
         all_of(slots, chips - 1, r.chip_recv.at[2])
         all_of(slots, chips - 1, r.chip_send.at[2])
         mine = r.one_whole.at[core]
-        pair_copy(19, mine, mine).start()
+        pair_copy(11, mine, mine).start()
 
     def one_take():
         mine = r.one_whole.at[core]
-        pair_copy(19, mine, mine).wait()
+        pair_copy(11, mine, mine).wait()
 
     def coefficients(total, square, count, gain, bias):
         n = jnp.maximum(count, 1.0)
@@ -572,8 +576,7 @@
         ah, bh = affine(n1, m)
         for pr in range(2):
             for pc in range(2):
-                a, s = half_silu(r.z1[pr, pc, k] * ah + bh, half_mask)
-                r.s1[pr, pc, k] = s
+                a = half_act(r.z1[pr, pc, k] * ah + bh)
                 dst = r.even if pr == 0 else r.odd
                 rows = pl.ds(0, hh) if pr == 0 else pl.ds(1, hh)
                 if pc == 0:
@@ -582,7 +585,7 @@
                     dst[k, rows, :, 2 * LANES : 3 * LANES] = a.astype(BF16)
                     dst[k, rows, :, 0:LANES] = shifted_right(a).astype(BF16)
         for pc in range(2):
-            a, _ = half_silu(halo_row(0, pc, k) * ah + bh)
+            a = half_act(halo_row(0, pc, k) * ah + bh)
             a = jnp.where(row > 0, a, 0.0)
             if pc == 0:
                 r.odd[k, 0, :, LANES : 2 * LANES] = a.astype(BF16)
@@ -602,10 +605,12 @@
 
     def early(k, c):
         m = r.mask_one[k]
+        ah, bh = affine(n1, m)
         for pr in range(2):
             for pc in range(2):
                 zhat = (r.z1[pr, pc, k] - n1.mu) * (m * n1.inv)
                 r.dz1[pr, pc, k] = zhat.astype(BF16)
+                _, r.s1[pr, pc, k] = half_silu(r.z1[pr, pc, k] * ah + bh, half_mask)
         r.dz4[k] = jnp.broadcast_to(m, (hh, PAD, LANES)).astype(BF16)
         return c
 
@@ -662,13 +667,13 @@
     ns = coefficients(ts1, ts2, all_px, r.wide_gain[1:2, :], r.wide_bias[1:2, :])
     w2 = r.reduce_two[...]
 
+    a3, as_ = 0.5 * n3.scale, 0.5 * ns.scale
+    b3 = (0.5 * (n3.shift + ns.shift)) * col_mask
+
     def fourth(k, acc):
-        a3, as_ = 0.5 * n3.scale, 0.5 * ns.scale
-        b3 = (0.5 * (n3.shift + ns.shift)) * col_mask
         for i in range(hh):
-            a, s = half_silu(r.z3[k, i] * a3 + r.zs[k, i] * as_ + b3, half_mask)
-            r.hidden[k, i] = a.astype(BF16)
-            r.s3[k, i] = s
+            h = r.z3[k, i] * a3 + r.zs[k, i] * as_ + b3
+            r.hidden[k, i] = half_act(h).astype(BF16)
         z = dot(flat2(r.hidden[k]), w2)
         r.z4[k] = z.reshape(hh, PAD, LANES)
         m = r.mask_two[k]
@@ -684,6 +689,7 @@
         for i in range(hh):
             r.dz3[k, i] = ((r.z3[k, i] - n3.mu) * n3.inv).astype(BF16)
             r.dzs[k, i] = ((r.zs[k, i] - ns.mu) * ns.inv).astype(BF16)
+            _, r.s3[k, i] = half_silu(r.z3[k, i] * a3 + r.zs[k, i] * as_ + b3, half_mask)
         return c
 
     advance(4, 1)
@@ -709,12 +715,10 @@
     def fifth(k, acc):
         m = r.mask_two[k]
         ah, bh = affine(n4, m)
-        a, s = half_silu(r.z4[k] * ah + bh, half_mask)
-        r.s4[k] = s
-        put3(r.a4, k, pl.ds(1, hh), a)
-        a, _ = half_silu(halo_row(1, 0, k) * ah + bh)
+        put3(r.a4, k, pl.ds(1, hh), half_act(r.z4[k] * ah + bh))
+        a = half_act(halo_row(1, 0, k) * ah + bh)
         put3(r.a4, k, 0, jnp.where(row > 0, a, 0.0))
-        a, _ = half_silu(halo_row(2, 0, k) * ah + bh)
+        a = half_act(halo_row(2, 0, k) * ah + bh)
         put3(r.a4, k, hh + 1, jnp.where(row < nr - 1, a, 0.0))
         z = sum(dot(flat2(r.a4[k, i : i + hh]), k_two[i]) for i in range(3))
         z = z.reshape(hh, PAD, LANES) * col_mask
@@ -725,15 +729,20 @@
     send_sums(4, [row_sum(s1), row_sum(s2)])
     advance(4, 2)
     start_pieces(cot_copies, *COT_AT[4])
+
+    def slope_four(k, c):
+        ah, bh = affine(n4, r.mask_two[k])
+        _, r.s4[k] = half_silu(r.z4[k] * ah + bh, half_mask)
+        return c
+
+    loop(slope_four)
     t1, t2 = take_sums(4, [LANES] * 2)
     n5 = coefficients(t1, t2, active_two * half_px, r.mid_gain[3:4, :], r.mid_bias[3:4, :])
     e2 = r.expand_two[...]
 
     def sixth(k, acc):
         ah, bh = affine(n5, r.mask_two[k])
-        a, s = half_silu(r.z5[k] * ah + bh, half_mask)
-        r.s5[k] = s
-        a = a.astype(BF16)
+        a = half_act(r.z5[k] * ah + bh).astype(BF16)
         r.a5[k] = a
         z = dot(flat2(a), e2)
         r.z6[k] = z.reshape(hh, PAD, cfg.c_out)
@@ -742,6 +751,12 @@
 
     s1, s2 = loop(sixth, zero8(cfg.c_out, 2))
     send_sums(5, [row_sum(v) for v in (s1, s2, t2_sum, t2z_sum)])
+    def slope_five(k, c):
+        ah, bh = affine(n5, r.mask_two[k])
+        _, r.s5[k] = half_silu(r.z5[k] * ah + bh, half_mask)
+        return c
+
+    loop(slope_five)
     both_edges(3, r.z5)
     halo_start(3)
     halo_start(4)
@@ -796,7 +811,9 @@
     both_edges(5, r.q5)
     halo_start(5)
     halo_start(6)
-    stage(0, "expand_two", dot_tn(flat2(r.a5[...]), flat2(r.dz6[...])))
+    expand_grad = dot_tn(flat2(r.a5[...]), flat2(r.dz6[...]))
+    stage(0, "expand_two", expand_grad[:, : 3 * LANES])
+    stage(3, "expand_rest", expand_grad[:, 3 * LANES :])
     halo_wait(3)
     halo_wait(4)
     advance(4, 5)
@@ -1134,9 +1151,9 @@
         ],
         full=[pltpu.VMEM((n, LANES), t) for n, t in zip(sizes, GROUP_TYPES)],
         image_sem=dma(nk), local_sem=dma(3), full_sem=dma(groups + 3), weight_sem=dma(len(weights)),
-        sum_send=dma(len(ROUND_ROWS)), sum_recv=dma(len(ROUND_ROWS)), halo_send=dma(9), halo_recv=dma(9),
-        row_send=dma(2), row_recv=dma(2), pair_send=dma(20), pair_recv=dma(20), chip_send=dma(3),
-        chip_recv=dma(3), grad_send=dma(groups, 6), grad_recv=dma(groups, 6),
+        sum_send=pltpu.SemaphoreType.DMA, sum_recv=dma(len(ROUND_ROWS)), halo_send=dma(9), halo_recv=dma(9),
+        row_send=dma(2), row_recv=dma(2), pair_send=dma(12), pair_recv=dma(12), chip_send=dma(3),
+        chip_recv=dma(3), grad_send=dma(groups), grad_recv=dma(groups, 6),
     )
     cfg = SimpleNamespace(
         nr=nr, nc=nc, nk=nk, hh=hh, wv=wv, c_in=c_in, c_out=c_out, group_size=sizes,
@@ -1219,7 +1236,8 @@
         summed = held[2 + g]
         at = 0
         for name, rows in group:
-            which = names.index(name)
+            rest = name not in names
+            which = names.index("expand_two" if rest else name)
             ref = wide_to[which]
             if len(ref.shape) == 4:
                 for i in range(9):
@@ -1227,10 +1245,12 @@
                     ref[i // 3, i % 3] = summed[lo : lo + LANES, :].astype(F32)
             else:
                 height = ref.shape[0]
-                for q in range(ref.shape[1] // LANES):
-                    lo = at + q * height
-                    ref[:, q * LANES : (q + 1) * LANES] = summed[lo : lo + height, :].astype(F32)
-            leave(ref, outs[2 + which])
+                first = ref.shape[1] // LANES - 1 if rest else 0
+                for q in range(rows // height):
+                    lo, to = at + q * height, (first + q) * LANES
+                    ref[:, to : to + LANES] = summed[lo : lo + height, :].astype(F32)
+            if rest or name != "expand_two":
+                leave(ref, outs[2 + which])
             at += rows
     small[n - 3].wait()
     wide_to[0][...] = held[n - 3][...].reshape(wide_to[0].shape)

time: 101 us -> 98.5 us (0.975)
  Pallas kernels: 99.6 us -> 97.4 us
    pallas_call x1, Pallas kernels: 95.9 us -> 93.8 us  [on_device(): pl.pallas_call(body, out_shape=flat[2], in_specs=[smem] * len(flat[0]) +...]
where the time goes in v6:
time: 98.5 us; the launch traced here: 98.3 us
  Pallas kernels  97.4 us (99%)
    pallas_call x1, Pallas kernels, on_device(): pl.pallas_call(body, out_shape=flat[2], in_specs=[smem] * len(flat[0]) +...  93.8 us
    pallas_call x1, Pallas kernels, finished(): pl.pallas_call(finish, out_shape=outs, in_specs=[hbm] * len(parts), out_s...  3.68 us

profile of v6, /device:TPU:0, one launch (start us, length us, event | category | flops | bytes accessed | tf_op | source)
XLA Modules:
  0.0 98.3 jit_solution(1459078066053555450)
XLA Ops:
  0.7 93.8 %shard_map.246 = (bf16[4,14,56,256]{3,2,1,0:T(8,128)(2,1)}, f32[8,128]{1,0:T(8,128)}, bf16[1,28,28,512]{3,2,1,0:T(8,128)(2,1)}, bf16[1536,128]{1,0:T(8,128)(2,1)...) custom-call(s32[4]{0:T(128)} %refs_0_.1, ...), custom_call_target="tpu_custom_call" | custom-call | tf_op jit(solution)/shard_map/pallas_call | solution.py:1176
  94.4 3.7 %shard_map.247 = (bf16[1,28,28,512]{3,2,1,0:T(8,128)(2,1)}, bf16[4,14,56,256]{3,2,1,0:T(8,128)(2,1)}, f32[256,128]{1,0:T(8,128)}, f32[3,3,128,128]{3,2,1,0:T(8,1...) custom-call(bf16[1,28,28,512]{3,2,1,0:T(8,128)(2,1)} %get-tuple-elem, ...), custom_call_target="tpu_custom_call" | custom-call | tf_op jit(solution)/shard_map/pallas_call | solution.py:1272

commit v7 on v6

--- a/solution.py
+++ b/solution.py
@@ -12,8 +12,8 @@
 F32 = jnp.float32
 BF16 = jnp.bfloat16
 epsilon = 1e-05
-COT_AT = ((0,), (1,), (2, 3), (4,), (5, 6))
-OUT_AT = ((0, 1), (2,), (3, 4), (5,), (6,), ())
+COT_AT = ((0,), (1,), (2, 3), (4,), (5, 6), ())
+OUT_AT = ((0, 1), (2,), (3, 4), (5, 6), (), ())
 PAD = 32
 LANES = 128
 
@@ -551,8 +551,29 @@
     send_sums(0, [row_sum(s1), row_sum(s2), count_one, count_two])
     halo_start(0)
     skip_send([row_sum(zs1), row_sum(zs2)])
+    arrived("mid_gain", "mid_bias", "spatial_one")
+    arrived("spatial_two", "expand_two")
+    def tap(ref, i, j):
+        return ref[i, j * LANES : (j + 1) * LANES, :].T
+
+    for i in range(3):
+        for j in range(3):
+            r.back_two[i, j * LANES : (j + 1) * LANES, :] = tap(r.spatial_two, 2 - i, 2 - j)
+    zeros = jnp.zeros((LANES, LANES), BF16)
+    k1 = r.spatial_one
+    here = [[tap(k1, 2, 2), tap(k1, 1, 2), tap(k1, 2, 1), tap(k1, 1, 1)],
+            [tap(k1, 2, 0), tap(k1, 1, 0), zeros, zeros]]
+    below = [[tap(k1, 0, 2), tap(k1, 0, 1)], [tap(k1, 0, 0), zeros]]
+    for ref, blocks in ((r.back_here, here), (r.back_below, below)):
+        for i, line in enumerate(blocks):
+            for j, block in enumerate(line):
+                ref[i * LANES : (i + 1) * LANES, j * LANES : (j + 1) * LANES] = block
+
+    for k in range(nk):
+        r.dz4[k] = jnp.broadcast_to(r.mask_one[k], (hh, PAD, LANES)).astype(BF16)
+    planes = [(pr, pc) for pr in range(2) for pc in range(2)]
+    r.part_m[...] = sum(dot_tn(flat2(r.x[q]), flat2(r.dz4[...])) for q in planes)
     start_pieces(cot_copies, *COT_AT[0])
-    arrived("mid_gain", "mid_bias", "spatial_one")
     t1, t2, active_one, active_two = take_sums(0, [LANES] * 4)
     half_px, full_px = float(hh * wv), float(4 * hh * wv)
     active_gate = active_two[:, 0:1]
@@ -611,15 +632,12 @@
                 zhat = (r.z1[pr, pc, k] - n1.mu) * (m * n1.inv)
                 r.dz1[pr, pc, k] = zhat.astype(BF16)
                 _, r.s1[pr, pc, k] = half_silu(r.z1[pr, pc, k] * ah + bh, half_mask)
-        r.dz4[k] = jnp.broadcast_to(m, (hh, PAD, LANES)).astype(BF16)
         return c
 
     loop(early)
     for name in ("expand_one", "wide_gain", "wide_bias", "reduce_two"):
         arrived(name)
-    planes = [(pr, pc) for pr in range(2) for pc in range(2)]
     r.part_z[...] = sum(dot_tn(flat2(r.x[q]), flat2(r.dz1[q])) for q in planes)
-    r.part_m[...] = sum(dot_tn(flat2(r.x[q]), flat2(r.dz4[...])) for q in planes)
     start_pieces(cot_copies, *COT_AT[1])
     t1, t2 = take_sums(1, [LANES] * 2)
     n2 = coefficients(t1, t2, active_one * half_px, r.mid_gain[1:2, :], r.mid_bias[1:2, :])
@@ -642,22 +660,6 @@
     send_sums(2, [row_sum(s1), row_sum(s2)])
     slope_sums(r.mask_one, r.s2, r.z2, r.a2, n2)
     advance(4, 0)
-    arrived("spatial_two", "expand_two")
-    def tap(ref, i, j):
-        return ref[i, j * LANES : (j + 1) * LANES, :].T
-
-    for i in range(3):
-        for j in range(3):
-            r.back_two[i, j * LANES : (j + 1) * LANES, :] = tap(r.spatial_two, 2 - i, 2 - j)
-    zeros = jnp.zeros((LANES, LANES), BF16)
-    k1 = r.spatial_one
-    here = [[tap(k1, 2, 2), tap(k1, 1, 2), tap(k1, 2, 1), tap(k1, 1, 1)],
-            [tap(k1, 2, 0), tap(k1, 1, 0), zeros, zeros]]
-    below = [[tap(k1, 0, 2), tap(k1, 0, 1)], [tap(k1, 0, 0), zeros]]
-    for ref, blocks in ((r.back_here, here), (r.back_below, below)):
-        for i, line in enumerate(blocks):
-            for j, block in enumerate(line):
-                ref[i * LANES : (i + 1) * LANES, j * LANES : (j + 1) * LANES] = block
     skip_return()
     start_pieces(cot_copies, *COT_AT[2])
     t1, t2 = take_sums(2, [cfg.c_out] * 2)
@@ -751,6 +753,8 @@
 
     s1, s2 = loop(sixth, zero8(cfg.c_out, 2))
     send_sums(5, [row_sum(v) for v in (s1, s2, t2_sum, t2z_sum)])
+    start_pieces(cot_copies, *COT_AT[5])
+
     def slope_five(k, c):
         ah, bh = affine(n5, r.mask_two[k])
         _, r.s5[k] = half_silu(r.z5[k] * ah + bh, half_mask)
@@ -771,25 +775,34 @@
     def cot_row(k, i):
         return jnp.concatenate([r.cot_rows[k, i].astype(F32), pad_rows], axis=0)
 
+    def half_pre_two(k, i):
+        g = 0.5 * r.gates[k]
+        return 0.5 * r.hidden[k, i].astype(F32) + (r.z6[k, i] * (g * n6.scale) + (g * n6.shift) * col_mask)
+
     def seventh(k, acc):
         g = r.gates[k]
-        a6, b6 = (0.5 * g) * n6.scale, ((0.5 * g) * n6.shift) * col_mask
         d1, d2 = acc
         for i in range(hh):
-            hid = r.hidden[k, i].astype(F32)
-            z = r.z6[k, i]
-            a, s = half_silu(0.5 * hid + (z * a6 + b6))
-            r.out_rows[k, i] = jnp.where(g > 0.0, a, hid)[:wv].astype(BF16)
+            _, s = half_silu(half_pre_two(k, i))
             live = g * cot_row(k, i) * s
             r.live[k, i] = live
             d1 += folded(live)
-            d2 += folded(live * z)
+            d2 += folded(live * r.z6[k, i])
         return d1, d2
 
     sums = loop(seventh, zero8(cfg.c_out, 2))
     send_sums(6, [row_sum(v) for v in sums])
 
     advance(4, 4)
+
+    def results(k, c):
+        for i in range(hh):
+            hid = r.hidden[k, i].astype(F32)
+            a = half_act(half_pre_two(k, i))
+            r.out_rows[k, i] = jnp.where(r.gates[k] > 0.0, a, hid)[:wv].astype(BF16)
+        return c
+
+    loop(results)
     start_pieces(out_copies, *OUT_AT[0])
     out_local.start()
     db6, q6 = take_sums(6, [cfg.c_out] * 2)
@@ -811,6 +824,12 @@
     both_edges(5, r.q5)
     halo_start(5)
     halo_start(6)
+    def passed_by(k, c):
+        for i in range(hh):
+            r.live[k, i] = (1.0 - r.gates[k]) * cot_row(k, i) + r.live[k, i]
+        return c
+
+    loop(passed_by)
     expand_grad = dot_tn(flat2(r.a5[...]), flat2(r.dz6[...]))
     stage(0, "expand_two", expand_grad[:, : 3 * LANES])
     stage(3, "expand_rest", expand_grad[:, 3 * LANES :])
@@ -857,13 +876,13 @@
     c1, c2, c3 = factors(n4, db4, dg4)
 
     def tenth(k, acc, c1=c1, c2=c2, c3=c3):
-        m, g = r.mask_two[k], r.gates[k]
+        m = r.mask_two[k]
         f1, f2, f3 = m * c1, m * c2, (m * c3) * col_mask
         r.dz4[k] = (r.q4[k] * f1 + r.z4[k] * f2 + f3).astype(BF16)
         back = dot_nt(flat2(r.dz4[k]), w2).reshape(hh, PAD, cfg.c_out)
         e1_, e2_, e3_, u1, u2 = acc
         for i in range(hh):
-            d = back[i] + (1.0 - g) * cot_row(k, i) + r.live[k, i]
+            d = back[i] + r.live[k, i]
             q = d.astype(BF16).astype(F32) * r.s3[k, i]
             r.q3[k, i] = q
             r.dz3[k, i] = (q * n3.scale).astype(BF16)
@@ -954,7 +973,6 @@
         for pr, pc, q in parts:
             q = q.reshape(hh, PAD, LANES) * r.s1[pr, pc, k]
             r.q1[pr, pc, k] = q
-            r.dz1[pr, pc, k] = (m * q).astype(BF16)
             s1 += m * folded(q)
             s2 += m * folded(q * r.z1[pr, pc, k])
         return s1, s2
@@ -964,6 +982,12 @@
     advance(3, 1)
     advance(0, 3)
     advance(1, 2)
+    def masked(k, c):
+        for q in planes:
+            r.dz1[(*q, k)] = (r.mask_one[k] * r.q1[(*q, k)]).astype(BF16)
+        return c
+
+    loop(masked)
     part_q = sum(dot_tn(flat2(r.x[q]), flat2(r.dz1[q])) for q in planes)
 
     def skip_back(k, c):
@@ -1037,6 +1061,11 @@
 
     def result(g):
         give(r.full[g], r.summed[g])
+
+    def half_result(g, which):
+        size = level_rows(g, 1)
+        half = pl.ds(pl.multiple_of(which * size, 16), size)
+        give(r.full[g].at[half], r.summed[g].at[half])
 
     advance(2, 3)
     advance(3, 3)
@@ -1057,8 +1086,9 @@
     result(1)
     advance(2, 6)
     result(2)
+    half_result(3, core)
     advance(3, 6)
-    result(3)
+    half_result(3, 1 - core)
     wait_pieces(1)
     out_local.wait()
     back_copy.wait()
@@ -1116,7 +1146,7 @@
     halves = {i: ROUND_ROWS[i] // 2 for i in WIDE}
     scratch = dict(
         held={name: pltpu.VMEM(a.shape, a.dtype) for name, a in weights.items()},
-        x_in=bf16(*images.shape), spread=f32(c_in // LANES, 2 * hh, 2 * PAD, LANES), x=bf16(*quad, c_in),
+        x_in=bf16(*images.shape), spread=f32(c_in // LANES, 2 * hh, 2 * PAD + 8, LANES), x=bf16(*quad, c_in),
         z1=f32(*quad, LANES), s1=f32(*quad, LANES), q1=f32(*quad, LANES), dz1=bf16(*quad, LANES),
         part_z=f32(c_in, LANES), part_m=f32(c_in, LANES),
         one_both=f32(2, *chunk), one_came=f32(*chunk), one_half=f32(*chunk), one_slots=f32(*chunk),
@@ -1150,7 +1180,7 @@
             for n, t in zip(levels, GROUP_TYPES)
         ],
         full=[pltpu.VMEM((n, LANES), t) for n, t in zip(sizes, GROUP_TYPES)],
-        image_sem=dma(nk), local_sem=dma(3), full_sem=dma(groups + 3), weight_sem=dma(len(weights)),
+        image_sem=dma(nk), local_sem=dma(3), full_sem=dma(groups + 4), weight_sem=dma(len(weights)),
         sum_send=pltpu.SemaphoreType.DMA, sum_recv=dma(len(ROUND_ROWS)), halo_send=dma(9), halo_recv=dma(9),
         row_send=dma(2), row_recv=dma(2), pair_send=dma(12), pair_recv=dma(12), chip_send=dma(3),
         chip_recv=dma(3), grad_send=dma(groups), grad_recv=dma(groups, 6),

time: 98.5 us -> 97.9 us (level)
  no operation moved by 1% of the time
where the time goes in v7:
time: 97.9 us; the launch traced here: 97.6 us
  Pallas kernels  96.8 us (99%)
    pallas_call x1, Pallas kernels, on_device(): pl.pallas_call(body, out_shape=flat[2], in_specs=[smem] * len(flat[0]) +...  93.1 us
    pallas_call x1, Pallas kernels, finished(): pl.pallas_call(finish, out_shape=outs, in_specs=[hbm] * len(parts), out_s...  3.68 us

profile of v7, /device:TPU:0, one launch (start us, length us, event | category | flops | bytes accessed | tf_op | source)
XLA Modules:
  0.0 97.6 jit_solution(9845462807817375518)
XLA Ops:
  0.7 93.1 %shard_map.246 = (bf16[4,14,56,256]{3,2,1,0:T(8,128)(2,1)}, f32[8,128]{1,0:T(8,128)}, bf16[1,28,28,512]{3,2,1,0:T(8,128)(2,1)}, bf16[1536,128]{1,0:T(8,128)(2,1)...) custom-call(s32[4]{0:T(128)} %refs_0_.1, ...), custom_call_target="tpu_custom_call" | custom-call | tf_op jit(solution)/shard_map/pallas_call | solution.py:1206
  93.8 3.7 %shard_map.247 = (bf16[1,28,28,512]{3,2,1,0:T(8,128)(2,1)}, bf16[4,14,56,256]{3,2,1,0:T(8,128)(2,1)}, f32[256,128]{1,0:T(8,128)}, f32[3,3,128,128]{3,2,1,0:T(8,1...) custom-call(bf16[1,28,28,512]{3,2,1,0:T(8,128)(2,1)} %get-tuple-elem, ...), custom_call_target="tpu_custom_call" | custom-call | tf_op jit(solution)/shard_map/pallas_call | solution.py:1302

commit v8 on v7

--- a/solution.py
+++ b/solution.py
@@ -930,9 +930,6 @@
         total = q_part + (fs[1] / norm.inv) * z_part[...]
         return total + (fs[2] + fs[1] * norm.mu) * four(m_part[...])
 
-    stage(2, "expand_one", by_parts(expand_q, r.expand_z, r.expand_m, n3, f3_))
-    stage(2, "shortcut", by_parts(skip_q * (ns.scale / n3.scale), r.skip_z, r.skip_m, ns, fs_))
-    advance(2, 0)
     halo_wait(7)
     edge_ab = sum(dot(flat2(r.edge_a[...]), t) for t in b2).reshape(nk, PAD, LANES)
 
@@ -951,6 +948,9 @@
         return c
 
     loop(twelfth)
+    stage(2, "expand_one", by_parts(expand_q, r.expand_z, r.expand_m, n3, f3_))
+    stage(2, "shortcut", by_parts(skip_q * (ns.scale / n3.scale), r.skip_z, r.skip_m, ns, fs_))
+    advance(2, 0)
     d2_ = flat2(r.dz2[:, 0:hh, :, 0:LANES])
     inputs = [r.odd[:, 0:hh], r.even[...], r.odd[:, 1 : hh + 1]]
     stage(3, "spatial_one", jnp.concatenate([dot_tn(flat2(a), d2_) for a in inputs], axis=0))

time: 97.9 us -> 97.8 us (level)
  no operation moved by 1% of the time
where the time goes in v8:
time: 97.8 us; the launch traced here: 97.6 us
  Pallas kernels  96.8 us (99%)
    pallas_call x1, Pallas kernels, on_device(): pl.pallas_call(body, out_shape=flat[2], in_specs=[smem] * len(flat[0]) +...  93.1 us
    pallas_call x1, Pallas kernels, finished(): pl.pallas_call(finish, out_shape=outs, in_specs=[hbm] * len(parts), out_s...  3.68 us

profile of v8, /device:TPU:0, one launch (start us, length us, event | category | flops | bytes accessed | tf_op | source)
XLA Modules:
  0.0 97.6 jit_solution(12593392897682683646)
XLA Ops:
  0.7 93.1 %shard_map.246 = (bf16[4,14,56,256]{3,2,1,0:T(8,128)(2,1)}, f32[8,128]{1,0:T(8,128)}, bf16[1,28,28,512]{3,2,1,0:T(8,128)(2,1)}, bf16[1536,128]{1,0:T(8,128)(2,1)...) custom-call(s32[4]{0:T(128)} %refs_0_.1, ...), custom_call_target="tpu_custom_call" | custom-call | tf_op jit(solution)/shard_map/pallas_call | solution.py:1206
  93.8 3.7 %shard_map.247 = (bf16[1,28,28,512]{3,2,1,0:T(8,128)(2,1)}, bf16[4,14,56,256]{3,2,1,0:T(8,128)(2,1)}, f32[256,128]{1,0:T(8,128)}, f32[3,3,128,128]{3,2,1,0:T(8,1...) custom-call(bf16[1,28,28,512]{3,2,1,0:T(8,128)(2,1)} %get-tuple-elem, ...), custom_call_target="tpu_custom_call" | custom-call | tf_op jit(solution)/shard_map/pallas_call | solution.py:1302
